TPU v7x, 32 devices: a whole 2x2x4 slice. The times are simulated.
32 devices in a mesh: dp: 32 (over z, y, x, core).
Axes of the slice: x: 2, y: 2, z: 4, core: 2. Of those that a mesh axis runs over, the one named last changes fastest.
Arguments:
- tokens: int32 [16384], P('dp'), may hold values from 0 to 30719
- positions: int32 [2, 16384], P(None, 'dp'), may hold values from 0 to 1000
- documents: int32 [32], P('dp'), may hold values from 0 to 7
- masking: int32 [16384], P('dp'), may hold values from 0 to 1, as said below
- negative_page: int32 [8, 16384], P(None, 'dp'), may hold values from 0 to 31
- negative_row: int32 [8, 16384], P(None, 'dp'), may hold values from 0 to 63, as said below
- pages: bfloat16 [32, 64, 768], P('dp'), may hold values from -6 to 6
- vocabulary: float32 [30720, 768], P('dp'), may hold values from -4.2 to 4.2
- geometry: float32 [768, 768], P(None, 'dp'), may hold values from -0.21875 to 0.21875
- mixing: float32 [768, 2304], P('dp'), may hold values from -0.21875 to 0.21875
- relative: float32 [768, 1536], P(None, 'dp'), may hold values from -0.3125 to 0.3125
- merging: float32 [768, 768], P('dp'), may hold values from -0.875 to 0.875
- widening: float32 [768, 3072], P('dp'), may hold values from -0.21875 to 0.21875
- narrowing: float32 [3072, 768], P('dp'), may hold values from -0.109375 to 0.109375
- scaling: float32 [6, 768], P(None, 'dp'), may hold values from -0.9 to 2.5
- moment_vocabulary: float32 [30720, 768], P('dp'), may hold values from -7.4505806e-08 to 7.4505806e-08
- moment_geometry: float32 [768, 768], P(None, 'dp'), may hold values from -3.0517578e-05 to 3.0517578e-05
- moment_mixing: float32 [768, 2304], P('dp'), may hold values from -3.0517578e-05 to 3.0517578e-05
- moment_relative: float32 [768, 1536], P(None, 'dp'), may hold values from -3.0517578e-05 to 3.0517578e-05
- moment_merging: float32 [768, 768], P('dp'), may hold values from -3.0517578e-05 to 3.0517578e-05
- moment_widening: float32 [768, 3072], P('dp'), may hold values from -3.0517578e-05 to 3.0517578e-05
- moment_narrowing: float32 [3072, 768], P('dp'), may hold values from -3.0517578e-05 to 3.0517578e-05
- moment_scaling: float32 [6, 768], P(None, 'dp'), may hold values from -0.00030517578 to 0.00030517578
- average_vocabulary: float32 [30720, 768], P('dp'), may hold values from -4.2 to 4.2
- average_geometry: float32 [768, 768], P(None, 'dp'), may hold values from -0.21875 to 0.21875
- average_mixing: float32 [768, 2304], P('dp'), may hold values from -0.21875 to 0.21875
- average_relative: float32 [768, 1536], P(None, 'dp'), may hold values from -0.3125 to 0.3125
- average_merging: float32 [768, 768], P('dp'), may hold values from -0.875 to 0.875
- average_widening: float32 [768, 3072], P('dp'), may hold values from -0.21875 to 0.21875
- average_narrowing: float32 [3072, 768], P('dp'), may hold values from -0.109375 to 0.109375
- average_scaling: float32 [6, 768], P(None, 'dp'), may hold values from -0.9 to 2.5
Outputs:
- loss: float32 [], replicated
- grad_norm: float32 [], replicated
- master_vocabulary: float32 [30720, 768], P('dp')
- master_geometry: float32 [768, 768], P(None, 'dp')
- master_mixing: float32 [768, 2304], P('dp')
- master_relative: float32 [768, 1536], P(None, 'dp')
- master_merging: float32 [768, 768], P('dp')
- master_widening: float32 [768, 3072], P('dp')
- master_narrowing: float32 [3072, 768], P('dp')
- master_scaling: float32 [6, 768], P(None, 'dp')
- velocity_vocabulary: float32 [30720, 768], P('dp')
- velocity_geometry: float32 [768, 768], P(None, 'dp')
- velocity_mixing: float32 [768, 2304], P('dp')
- velocity_relative: float32 [768, 1536], P(None, 'dp')
- velocity_merging: float32 [768, 768], P('dp')
- velocity_widening: float32 [768, 3072], P('dp')
- velocity_narrowing: float32 [3072, 768], P('dp')
- velocity_scaling: float32 [6, 768], P(None, 'dp')
- smooth_vocabulary: float32 [30720, 768], P('dp')
- smooth_geometry: float32 [768, 768], P(None, 'dp')
- smooth_mixing: float32 [768, 2304], P('dp')
- smooth_relative: float32 [768, 1536], P(None, 'dp')
- smooth_merging: float32 [768, 768], P('dp')
- smooth_widening: float32 [768, 3072], P('dp')
- smooth_narrowing: float32 [3072, 768], P('dp')
- smooth_scaling: float32 [6, 768], P(None, 'dp')
Inputs may be any that keep to these rules, and one draw needn't show every extreme that they name: `masking`: 1 marks a masked token. negative_row[n, t] % 8 equals n.
All inputs are finite; a program needn't handle non-finite values.
Results may differ from a plain program's by a relative error of at most 0.011.
Values may be sent and summed in bfloat16 or wider, within the bound.
A program may use at most 248 MiB of HBM per device.

v0:
```python
from functools import partial

import jax
import jax.numpy as jnp
from jax import lax
from jax.sharding import PartitionSpec as P

HD = 64
DOCS = 8
STEP = 10


mask_token = 103
ln_epsilon = 1e-06
momentum_decay = 0.9
learn_rate = 5000.0
table_rate = 1000000.0
clip_limit = 0.01
average_cap = 0.999


def sinusoids(positions, count):
    ranks = jnp.arange(count).astype(jnp.float32)
    omegas = jnp.power(10000.0, -ranks / count)
    angle_x = positions[0].astype(jnp.float32)[:, None] * omegas[None, :]
    angle_y = positions[1].astype(jnp.float32)[:, None] * omegas[None, :]
    return (jnp.sin(angle_x), jnp.cos(angle_x), jnp.sin(angle_y), jnp.cos(angle_y))


def rotate(table, waves):
    sin_x, cos_x, sin_y, cos_y = waves
    count = sin_x.shape[-1]
    sine_x = table[..., :count]
    cosine_x = table[..., count : 2 * count]
    sine_y = table[..., 2 * count : 3 * count]
    cosine_y = table[..., 3 * count :]
    return jnp.concatenate(
        [
            sine_x * sin_x + cosine_x * cos_x,
            sine_y * sin_y + cosine_y * cos_y,
            cosine_x * sin_x - sine_x * cos_x,
            cosine_y * sin_y - sine_y * cos_y,
        ],
        -1,
    )


def rotate_back(upstream, waves):
    sin_x, cos_x, sin_y, cos_y = waves
    count = sin_x.shape[-1]
    first = upstream[..., :count]
    second = upstream[..., count : 2 * count]
    third = upstream[..., 2 * count : 3 * count]
    fourth = upstream[..., 3 * count :]
    return jnp.concatenate(
        [
            first * sin_x - third * cos_x,
            first * cos_x + third * sin_x,
            second * sin_y - fourth * cos_y,
            second * cos_y + fourth * sin_y,
        ],
        -1,
    )


def layer_norm(rows, gain, bias):
    centred = rows - jnp.mean(rows, -1, keepdims=True)
    rescale = lax.rsqrt(jnp.mean(centred * centred, -1, keepdims=True) + ln_epsilon)
    whitened = centred * rescale
    return (whitened * gain + bias, whitened, rescale)


def norm_back(upstream, whitened, rescale, gain):
    scaled = upstream * gain
    inner = (
        scaled
        - jnp.mean(scaled, -1, keepdims=True)
        - whitened * jnp.mean(scaled * whitened, -1, keepdims=True)
    )
    return (rescale * inner, jnp.sum(upstream * whitened, 0), jnp.sum(upstream, 0))


def contract_rows(left, right):
    return lax.dot_general(
        left, right, (((0,), (0,)), ((), ())), preferred_element_type=jnp.float32
    )


def contract_cols(left, right):
    return lax.dot_general(
        left, right, (((1,), (1,)), ((), ())), preferred_element_type=jnp.float32
    )


def forward(weights, tokens, positions, masking):
    table, box_map, mix_map, rel_map, out_map, up_map, down_map, norm_rows = weights
    gains = norm_rows.astype(jnp.float32)
    count_tok = tokens.shape[0]
    model = mix_map.shape[0]
    heads = model // HD
    sin_count = box_map.shape[0]
    waves = sinusoids(positions, sin_count // 4)
    boxes = jnp.concatenate(waves, -1).astype(jnp.bfloat16)
    entry = jnp.where(masking == 1, mask_token, tokens)
    embedded = table[entry].astype(jnp.float32) + jnp.dot(
        boxes, box_map, preferred_element_type=jnp.float32
    )
    first = layer_norm(embedded, gains[0], gains[1])
    normed = first[0].astype(jnp.bfloat16)
    joined = jnp.dot(normed, mix_map, preferred_element_type=jnp.float32).astype(jnp.bfloat16)
    queries = joined[:, :model].reshape(count_tok, heads, HD)
    keys_low = joined[:, model : 2 * model].reshape(count_tok, heads, HD)
    values_low = joined[:, 2 * model :].reshape(count_tok, heads, HD)
    text_terms = jnp.einsum(
        "thd,fhd->htf",
        queries,
        rel_map[:, :model].reshape(sin_count, heads, HD),
        preferred_element_type=jnp.float32,
    )
    box_terms = jnp.einsum(
        "thd,fhd->htf",
        keys_low,
        rel_map[:, model:].reshape(sin_count, heads, HD),
        preferred_element_type=jnp.float32,
    )
    bases = jnp.concatenate([waves[1], waves[3], waves[0], waves[2]], -1).astype(jnp.bfloat16)
    spread = jnp.broadcast_to(bases[None], (heads, count_tok, sin_count))
    query_ext = jnp.concatenate(
        [queries.transpose(1, 0, 2), rotate(text_terms, waves).astype(jnp.bfloat16), spread], -1
    )
    key_ext = jnp.concatenate(
        [keys_low.transpose(1, 0, 2), spread, rotate(box_terms, waves).astype(jnp.bfloat16)], -1
    )
    scores = jnp.einsum(
        "htf,hsf->hts", query_ext, key_ext, preferred_element_type=jnp.float32
    ) * HD ** (-0.5)
    highest = jnp.max(scores, -1, keepdims=True)
    totals = highest + jnp.log(jnp.sum(jnp.exp(scores - highest), -1, keepdims=True))
    probs_low = jnp.exp(scores - totals).astype(jnp.bfloat16)
    attended = jnp.einsum("hts,shd->thd", probs_low, values_low, preferred_element_type=jnp.float32)
    attended = attended.reshape(count_tok, model).astype(jnp.bfloat16)
    second = layer_norm(
        first[0] + jnp.dot(attended, out_map, preferred_element_type=jnp.float32),
        gains[2],
        gains[3],
    )
    middle = second[0].astype(jnp.bfloat16)
    hidden_pre = jnp.dot(middle, up_map, preferred_element_type=jnp.float32)
    hidden = jax.nn.gelu(hidden_pre, approximate=False).astype(jnp.bfloat16)
    third = layer_norm(
        second[0] + jnp.dot(hidden, down_map, preferred_element_type=jnp.float32),
        gains[4],
        gains[5],
    )
    return {
        "waves": waves,
        "boxes": boxes,
        "entry": entry,
        "first": first,
        "normed": normed,
        "queries": queries,
        "keys": keys_low,
        "values": values_low,
        "query_ext": query_ext,
        "key_ext": key_ext,
        "totals": totals,
        "attended": attended,
        "second": second,
        "middle": middle,
        "hidden_pre": hidden_pre,
        "hidden": hidden,
        "third": third,
    }


def backward(weights, cache, d_states):
    table, box_map, mix_map, rel_map, out_map, up_map, down_map, norm_rows = weights
    gains = norm_rows.astype(jnp.float32)
    count_tok = d_states.shape[0]
    model = mix_map.shape[0]
    heads = model // HD
    sin_count = box_map.shape[0]
    d_mid, gain_last, bias_last = norm_back(
        d_states, cache["third"][1], cache["third"][2], gains[4]
    )
    d_down = d_mid.astype(jnp.bfloat16)
    grad_down = contract_rows(cache["hidden"], d_down)
    d_hidden = contract_cols(d_down, down_map)
    gelu_exact = partial(jax.nn.gelu, approximate=False)
    d_pre = jax.vjp(gelu_exact, cache["hidden_pre"])[1](d_hidden)[0].astype(jnp.bfloat16)
    grad_up = contract_rows(cache["middle"], d_pre)
    d_second = d_mid + contract_cols(d_pre, up_map)
    d_lower, gain_mid, bias_mid = norm_back(
        d_second, cache["second"][1], cache["second"][2], gains[2]
    )
    d_attn = d_lower.astype(jnp.bfloat16)
    grad_out = contract_rows(cache["attended"], d_attn)
    d_attended = contract_cols(d_attn, out_map).astype(jnp.bfloat16).reshape(count_tok, heads, HD)
    query_ext = cache["query_ext"]
    key_ext = cache["key_ext"]
    scores = jnp.einsum(
        "htf,hsf->hts", query_ext, key_ext, preferred_element_type=jnp.float32
    ) * HD ** (-0.5)
    probs = jnp.exp(scores - cache["totals"])
    d_probs = jnp.einsum(
        "thd,shd->hts", d_attended, cache["values"], preferred_element_type=jnp.float32
    )
    grad_values = jnp.einsum(
        "hts,thd->shd", probs.astype(jnp.bfloat16), d_attended, preferred_element_type=jnp.float32
    )
    d_scores = (probs * (d_probs - jnp.sum(d_probs * probs, -1, keepdims=True))).astype(
        jnp.bfloat16
    )
    d_query = jnp.einsum(
        "hts,hsf->htf", d_scores, key_ext, preferred_element_type=jnp.float32
    ) * HD ** (-0.5)
    d_key = jnp.einsum(
        "hts,htf->hsf", d_scores, query_ext, preferred_element_type=jnp.float32
    ) * HD ** (-0.5)
    d_text = rotate_back(d_query[..., HD : HD + sin_count], cache["waves"]).astype(jnp.bfloat16)
    d_box = rotate_back(d_key[..., HD + sin_count :], cache["waves"]).astype(jnp.bfloat16)
    rel_text = rel_map[:, :model].reshape(sin_count, heads, HD)
    rel_box = rel_map[:, model:].reshape(sin_count, heads, HD)
    grad_rel = jnp.concatenate(
        [
            jnp.einsum(
                "htf,thd->fhd", d_text, cache["queries"], preferred_element_type=jnp.float32
            ).reshape(sin_count, model),
            jnp.einsum(
                "htf,thd->fhd", d_box, cache["keys"], preferred_element_type=jnp.float32
            ).reshape(sin_count, model),
        ],
        1,
    )
    grad_queries = d_query[..., :HD].transpose(1, 0, 2) + jnp.einsum(
        "htf,fhd->thd", d_text, rel_text, preferred_element_type=jnp.float32
    )
    grad_keys = d_key[..., :HD].transpose(1, 0, 2) + jnp.einsum(
        "htf,fhd->thd", d_box, rel_box, preferred_element_type=jnp.float32
    )
    d_joined = jnp.concatenate(
        [
            grad_queries.reshape(count_tok, model),
            grad_keys.reshape(count_tok, model),
            grad_values.reshape(count_tok, model),
        ],
        1,
    ).astype(jnp.bfloat16)
    grad_mix = contract_rows(cache["normed"], d_joined)
    d_first = d_lower + contract_cols(d_joined, mix_map)
    d_embedded, gain_low, bias_low = norm_back(
        d_first, cache["first"][1], cache["first"][2], gains[0]
    )
    grad_box = contract_rows(cache["boxes"], d_embedded.astype(jnp.bfloat16))
    grad_norms = jnp.stack([gain_low, bias_low, gain_mid, bias_mid, gain_last, bias_last], 0)
    return (d_embedded, (grad_box, grad_mix, grad_rel, grad_out, grad_up, grad_down, grad_norms))


def per_device(
    tokens,
    positions,
    documents,
    masking,
    negative_page,
    negative_row,
    pages,
    vocabulary,
    geometry,
    mixing,
    relative,
    merging,
    widening,
    narrowing,
    scaling,
    moment_vocabulary,
    moment_geometry,
    moment_mixing,
    moment_relative,
    moment_merging,
    moment_widening,
    moment_narrowing,
    moment_scaling,
    average_vocabulary,
    average_geometry,
    average_mixing,
    average_relative,
    average_merging,
    average_widening,
    average_narrowing,
    average_scaling,
):
    mask_float = masking.astype(jnp.float32)
    chosen = (documents[0] == jnp.arange(DOCS)).astype(jnp.float32)
    counts = lax.psum(chosen * jnp.sum(mask_float), "dp")
    gathered = (
        lax.all_gather(vocabulary.astype(jnp.bfloat16), "dp", axis=0, tiled=True),
        lax.all_gather(geometry.astype(jnp.bfloat16), "dp", axis=1, tiled=True),
        lax.all_gather(mixing.astype(jnp.bfloat16), "dp", axis=0, tiled=True),
        lax.all_gather(relative.astype(jnp.bfloat16), "dp", axis=1, tiled=True),
        lax.all_gather(merging.astype(jnp.bfloat16), "dp", axis=0, tiled=True),
        lax.all_gather(widening.astype(jnp.bfloat16), "dp", axis=0, tiled=True),
        lax.all_gather(narrowing.astype(jnp.bfloat16), "dp", axis=0, tiled=True),
        lax.all_gather(scaling.astype(jnp.bfloat16), "dp", axis=1, tiled=True),
    )
    cache = forward(gathered, tokens, positions, masking)
    states_low = cache["third"][0].astype(jnp.bfloat16)
    model = mixing.shape[1] // 3
    inv_root = model ** (-0.5)
    target_rows = gathered[0][tokens].astype(jnp.float32)
    positive = jnp.sum(states_low.astype(jnp.float32) * target_rows, -1) * inv_root
    page_rows = pages.shape[1]
    flat_index = negative_page * page_rows + negative_row
    score_piece = lax.all_gather(pages, "dp", axis=0, tiled=True)
    rows = score_piece.reshape(-1, score_piece.shape[2])
    raw = contract_cols(states_low, rows)
    local = flat_index
    inside = (local >= 0) & (local < rows.shape[0])
    picked = jnp.take_along_axis(raw, jnp.clip(local, 0, rows.shape[0] - 1).T, axis=1).T
    raw_negative = jnp.where(inside, picked, 0.0)
    logits = jnp.concatenate([positive[None], raw_negative * inv_root], 0)
    highest = jnp.max(logits, 0, keepdims=True)
    totals = highest + jnp.log(jnp.sum(jnp.exp(logits - highest), 0, keepdims=True))
    per_token = totals[0] - positive
    local_sums = chosen * jnp.sum(mask_float * per_token)
    share = jnp.sum(chosen / (DOCS * jnp.maximum(counts, 1.0)))
    leading = (jnp.arange(logits.shape[0]) == 0).astype(jnp.float32)[:, None]
    d_logits = share * mask_float[None, :] * (jnp.exp(logits - totals) - leading)
    doc_sums = lax.psum(local_sums, "dp")
    coeffs = (d_logits[1:] * inv_root).astype(jnp.bfloat16)
    positive_grad = (d_logits[0] * inv_root)[:, None]
    spread_piece = lax.all_gather(pages, "dp", axis=0, tiled=True)
    rows = spread_piece.reshape(-1, spread_piece.shape[2])
    local = flat_index
    slots = jnp.arange(rows.shape[0])[None, :]
    weight_map = jnp.zeros((local.shape[1], rows.shape[0]), jnp.bfloat16)
    for member in range(local.shape[0]):
        weight_map = jnp.where(local[member][:, None] == slots, coeffs[member][:, None], weight_map)
    d_states = positive_grad * target_rows + jnp.dot(
        weight_map, rows, preferred_element_type=jnp.float32
    )
    weights_back = (
        lax.all_gather(vocabulary.astype(jnp.bfloat16), "dp", axis=0, tiled=True),
        lax.all_gather(geometry.astype(jnp.bfloat16), "dp", axis=1, tiled=True),
        lax.all_gather(mixing.astype(jnp.bfloat16), "dp", axis=0, tiled=True),
        lax.all_gather(relative.astype(jnp.bfloat16), "dp", axis=1, tiled=True),
        lax.all_gather(merging.astype(jnp.bfloat16), "dp", axis=0, tiled=True),
        lax.all_gather(widening.astype(jnp.bfloat16), "dp", axis=0, tiled=True),
        lax.all_gather(narrowing.astype(jnp.bfloat16), "dp", axis=0, tiled=True),
        lax.all_gather(scaling.astype(jnp.bfloat16), "dp", axis=1, tiled=True),
    )
    d_embedded, layer_grads = backward(weights_back, cache, d_states)
    table_grad = jnp.zeros(weights_back[0].shape, jnp.float32).at[cache["entry"]].add(d_embedded)
    table_grad = table_grad.at[tokens].add(positive_grad * states_low.astype(jnp.float32))
    reduced = (
        lax.psum_scatter(table_grad, "dp", scatter_dimension=0, tiled=True),
        lax.psum_scatter(layer_grads[0], "dp", scatter_dimension=1, tiled=True),
        lax.psum_scatter(layer_grads[1], "dp", scatter_dimension=0, tiled=True),
        lax.psum_scatter(layer_grads[2], "dp", scatter_dimension=1, tiled=True),
        lax.psum_scatter(layer_grads[3], "dp", scatter_dimension=0, tiled=True),
        lax.psum_scatter(layer_grads[4], "dp", scatter_dimension=0, tiled=True),
        lax.psum_scatter(layer_grads[5], "dp", scatter_dimension=0, tiled=True),
        lax.psum_scatter(layer_grads[6], "dp", scatter_dimension=1, tiled=True),
    )
    square = sum((jnp.sum(piece * piece) for piece in reduced))
    norm_total = lax.psum(square, "dp")
    loss = jnp.sum(doc_sums / (DOCS * jnp.maximum(counts, 1.0)))
    grad_norm = jnp.sqrt(norm_total)
    factor = clip_limit / jnp.maximum(grad_norm, clip_limit)
    decay = min(average_cap, (1.0 + STEP) / (10.0 + STEP))
    masters = (vocabulary, geometry, mixing, relative, merging, widening, narrowing, scaling)
    moments = (
        moment_vocabulary,
        moment_geometry,
        moment_mixing,
        moment_relative,
        moment_merging,
        moment_widening,
        moment_narrowing,
        moment_scaling,
    )
    averages = (
        average_vocabulary,
        average_geometry,
        average_mixing,
        average_relative,
        average_merging,
        average_widening,
        average_narrowing,
        average_scaling,
    )
    rates = (table_rate,) + (learn_rate,) * 7
    fresh, speeds, smooths = ([], [], [])
    for master, moment, average, piece, rate in zip(masters, moments, averages, reduced, rates):
        clipped = piece * factor
        velocity = momentum_decay * moment + clipped
        updated = master - rate * (clipped + momentum_decay * velocity)
        fresh.append(updated)
        speeds.append(velocity)
        smooths.append(decay * average + (1.0 - decay) * updated)
    return (
        loss,
        grad_norm,
        fresh[0],
        fresh[1],
        fresh[2],
        fresh[3],
        fresh[4],
        fresh[5],
        fresh[6],
        fresh[7],
        speeds[0],
        speeds[1],
        speeds[2],
        speeds[3],
        speeds[4],
        speeds[5],
        speeds[6],
        speeds[7],
        smooths[0],
        smooths[1],
        smooths[2],
        smooths[3],
        smooths[4],
        smooths[5],
        smooths[6],
        smooths[7],
    )


def solution(mesh):
    return jax.shard_map(
        per_device,
        mesh=mesh,
        in_specs=(
            P("dp"),
            P(None, "dp"),
            P("dp"),
            P("dp"),
            P(None, "dp"),
            P(None, "dp"),
            P("dp", None, None),
            P("dp", None),
            P(None, "dp"),
            P("dp", None),
            P(None, "dp"),
            P("dp", None),
            P("dp", None),
            P("dp", None),
            P(None, "dp"),
            P("dp", None),
            P(None, "dp"),
            P("dp", None),
            P(None, "dp"),
            P("dp", None),
            P("dp", None),
            P("dp", None),
            P(None, "dp"),
            P("dp", None),
            P(None, "dp"),
            P("dp", None),
            P(None, "dp"),
            P("dp", None),
            P("dp", None),
            P("dp", None),
            P(None, "dp"),
        ),
        out_specs=(
            P(),
            P(),
            P("dp", None),
            P(None, "dp"),
            P("dp", None),
            P(None, "dp"),
            P("dp", None),
            P("dp", None),
            P("dp", None),
            P(None, "dp"),
            P("dp", None),
            P(None, "dp"),
            P("dp", None),
            P(None, "dp"),
            P("dp", None),
            P("dp", None),
            P("dp", None),
            P(None, "dp"),
            P("dp", None),
            P(None, "dp"),
            P("dp", None),
            P(None, "dp"),
            P("dp", None),
            P("dp", None),
            P("dp", None),
            P(None, "dp"),
        ),
        check_vma=False,
    )
```

profile of v0, /device:TPU:0, one launch (start us, length us, event | category | flops | bytes accessed | tf_op | source)
XLA Modules:
  0.0 2487.1 jit_solution(15718329466660386451)
XLA Ops:
  19.5 43.7 %all-gather = bf16[32,24,6]{1,2,0:T(8,128)(2,1)S(1)} all-gather(bf16[1,24,6]{1,2,0:T(8,128)(2,1)S(1)} %convert_bitcast_fusion), channel_id=1, replica_groups=mesh['dp'=32] {'dp'}, dimensions={0}, use_global_device_ids=true | all-gather | bytes 9504 | tf_op jit(solution)/shard_map/all_gather | solution.py:303
  74.7 259.6 %all-gather.10.cloned.1.call-done = bf16[30720,768]{1,0:T(8,128)(2,1)} async-done(((bf16[960,768]{1,0:T(8,128)(2,1)}), bf16[30720,768]{1,0:T(8,128)(2,1)}) %all-gather.10.cloned.1.call-update) | async-done | bytes 47185936 | tf_op jit(solution)/shard_map/all_gather | solution.py:296
  341.3 48.6 %all-gather.12.cloned.1.call-done = bf16[768,768]{0,1:T(8,128)(2,1)} async-done(((bf16[768,24]{0,1:T(8,128)(2,1)}), bf16[768,768]{0,1:T(8,128)(2,1)}) %all-gather.12.cloned.1.call-update) | async-done | bytes 1179664 | tf_op jit(solution)/shard_map/all_gather | solution.py:297
  393.9 58.4 %all-gather.14.cloned.1.call-done = bf16[768,2304]{1,0:T(8,128)(2,1)} async-done(((bf16[24,2304]{1,0:T(8,128)(2,1)}), bf16[768,2304]{1,0:T(8,128)(2,1)}) %all-gather.14.cloned.1.call-update) | async-done | bytes 3538960 | tf_op jit(solution)/shard_map/all_gather | solution.py:298
  463.4 9.1 fusion.108
  472.5 15.9 subtract_convert_fusion.6
  506.5 9.1 fusion.109
  515.7 16.2 subtract_convert_fusion.4
  559.2 8.7 broadcast_dynamic-update-slice_fusion
  577.1 22.9 multiply_reduce_fusion.1
  620.2 20.1 multiply_convert_fusion.1
  648.3 52.8 %all-gather.24.cloned.1.call-done = bf16[32,64,768]{2,1,0:T(8,128)(2,1)} async-done(((bf16[1,64,768]{2,1,0:T(8,128)(2,1)}), bf16[32,64,768]{2,1,0:T(8,128)(2,1)}) %all-gather.24.cloned.1.call-update) | async-done | bytes 3145744 | tf_op jit(solution)/shard_map/all_gather | solution.py:313
  707.1 56.9 %gather_fusion.2 = f32[4096]{0:T(1024)S(1)} fusion(f32[512,2048]{1,0:T(8,128)} %fusion.110, s32[4096]{0:T(1024)S(1)} %copy-done.1), kind=kCustom, calls=%fused_computation.2 | custom fusion | bytes 65536 | tf_op jit(solution)/shard_map/jit(take_along_axis)/gather | solution.py:318
  766.3 38.6 %all-reduce.1 = (f32[8]{0:T(128)S(1)}, f32[8]{0:T(128)S(1)}) all-reduce(f32[8]{0:T(128)S(1)} %get-tuple-element.162, f32[8]{0:T(128)S(1)} %get-tuple-element.163), channel_id=1, replica_groups=mesh['dp'=32] {'dp'}, use_global_device_ids=true, to_apply=%region_14.15 | all-reduce | flops 16 | bytes 128 | tf_op jit(solution)/shard_map/psum | solution.py:294
  818.0 8.1 add_convert_fusion.4
  836.4 8.5 multiply_reduce_fusion
  850.2 26.1 %broadcast_multiply_fusion = f32[12,512,1600]{2,1,0:T(8,128)} fusion(bf16[12,512,512]{1,2,0:T(8,128)(2,1)} %multiply_convert_fusion, bf16[12,512,1600]{1,2,0:T(8,128)(2,1)} %get-tuple-element.121), kind=kOutput, calls=%fused_computation.5 | convolution fusion | flops 10076160000 | bytes 65273856 | tf_op jit(solution)/shard_map/hts,htf->hsf/dot_general | solution.py:217
  876.3 26.5 %broadcast_multiply_fusion.1 = f32[12,512,1600]{2,1,0:T(8,128)} fusion(bf16[12,512,512]{1,2,0:T(8,128)(2,1)} %multiply_convert_fusion, bf16[12,512,1600]{1,2,0:T(8,128)(2,1)} %constant_dynamic-update-slice_fusion.5), kind=kOutput, calls=%fused_computation.6 | convolution fusion | flops 10076160000 | bytes 65273856 | tf_op jit(solution)/shard_map/hts,hsf->htf/dot_general | solution.py:214
  902.9 17.9 subtract_convert_fusion.1
  920.8 18.2 subtract_convert_fusion.3
  939.1 8.7 fusion.30
  947.8 8.4 fusion.29
  974.1 8.9 fusion.62
  1018.9 30.1 %broadcast_in_dim.155 = f32[30720,768]{1,0:T(8,128)} broadcast(f32[]{:T(128)} %constant.60.clone.1), dimensions={} | broadcast | bytes 94371840 | tf_op jit(solution)/shard_map/broadcast_in_dim | solution.py:352
  1049.1 66.7 %scatter_fusion = f32[30720,768]{1,0:T(8,128)} fusion(f32[30720,768]{1,0:T(8,128)} %broadcast_in_dim.155, s32[512]{0:T(512)S(1)} %copy-done.90, f32[512,768]{1,0:T(8,128)S(1)} %subtract_multiply_fusion), kind=kCustom, calls=%fused_computation.3 | custom fusion | flops 393216 | bytes 4720640 | tf_op jit(solution)/shard_map/scatter-add | solution.py:352
  1116.0 65.7 %scatter_fusion.1 = f32[30720,768]{1,0:T(8,128)} fusion(f32[30720,768]{1,0:T(8,128)} %scatter_fusion, s32[512]{0:T(512)S(1)} %copy-done.88, f32[512,768]{1,0:T(8,128)S(1)} %convert_multiply_fusion.2), kind=kCustom, calls=%fused_computation.4 | custom fusion | flops 393216 | bytes 4720640 | tf_op jit(solution)/shard_map/scatter-add | solution.py:353
  1182.5 49.5 %all-reduce = f32[6,768]{1,0:T(8,128)S(1)} all-reduce(f32[6,768]{1,0:T(8,128)S(1)} %stack.27), channel_id=9, replica_groups=mesh['dp'=32] {'dp'}, use_global_device_ids=true, to_apply=%region_46.47.clone | all-reduce | flops 4608 | bytes 36864
  1237.2 106.6 %reduce-scatter.13.cloned.1.call-done = f32[24,2304]{1,0:T(8,128)} async-done(((f32[768,2304]{1,0:T(8,128)}), f32[24,2304]{1,0:T(8,128)}) %reduce-scatter.13.cloned.1.call-update) | async-done | bytes 221200 | tf_op jit(solution)/shard_map/reduce_scatter | solution.py:357
  1345.4 139.3 %reduce-scatter.19.cloned.1.call-done = f32[24,3072]{1,0:T(8,128)} async-done(((f32[768,3072]{1,0:T(8,128)}), f32[24,3072]{1,0:T(8,128)}) %reduce-scatter.19.cloned.1.call-update) | async-done | bytes 294928 | tf_op jit(solution)/shard_map/reduce_scatter | solution.py:360
  1486.3 139.6 %reduce-scatter.21.cloned.1.call-done = f32[96,768]{1,0:T(8,128)} async-done(((f32[3072,768]{1,0:T(8,128)}), f32[96,768]{1,0:T(8,128)}) %reduce-scatter.21.cloned.1.call-update) | async-done | bytes 294928 | tf_op jit(solution)/shard_map/reduce_scatter | solution.py:361
  1627.5 784.7 %reduce-scatter.9.cloned.1.call-done = f32[960,768]{1,0:T(8,128)} async-done(((f32[30720,768]{1,0:T(8,128)}), f32[960,768]{1,0:T(8,128)}) %reduce-scatter.9.cloned.1.call-update) | async-done | bytes 2949136 | tf_op jit(solution)/shard_map/reduce_scatter | solution.py:355
  2420.7 39.4 %psum.23 = f32[]{:T(128)} all-reduce(f32[]{:T(128)S(6)} %add.310), channel_id=1, replica_groups=mesh['dp'=32] {'dp'}, use_global_device_ids=true, to_apply=%region_48.49 | all-reduce | flops 1 | bytes 8 | tf_op jit(solution)/shard_map/psum | solution.py:365
  (435 shorter events, 250.3 us)
Async XLA Ops:
  7.2 64.3 %all-gather.16.cloned.1.call-start = ((), (), s32[]{:S(2)}) async-start(), calls=%async_computation.10 | async-start | bytes 2433024 | tf_op jit(solution)/shard_map/all_gather | solution.py:299
  9.0 325.2 %all-gather.10.cloned.1.call-start = ((), (), s32[]{:S(2)}) async-start(), calls=%async_computation.7 | async-start | bytes 48660480 | tf_op jit(solution)/shard_map/all_gather | solution.py:296
  12.3 377.6 %all-gather.12.cloned.1.call-start = ((), (), s32[]{:S(2)}) async-start(), calls=%async_computation.8 | async-start | bytes 1216512 | tf_op jit(solution)/shard_map/all_gather | solution.py:297
  13.1 439.2 %all-gather.14.cloned.1.call-start = ((), (), s32[]{:S(2)}) async-start(), calls=%async_computation.9 | async-start | bytes 3649536 | tf_op jit(solution)/shard_map/all_gather | solution.py:298
  13.8 597.0 %all-gather.18.cloned.1.call-start = ((), (), s32[]{:S(2)}) async-start(), calls=%async_computation.11 | async-start | bytes 1216512 | tf_op jit(solution)/shard_map/all_gather | solution.py:300
  14.5 605.6 %all-gather.20.cloned.1.call-start = ((), (), s32[]{:S(2)}) async-start(), calls=%async_computation.12 | async-start | bytes 4866048 | tf_op jit(solution)/shard_map/all_gather | solution.py:301
  15.3 625.1 %all-gather.22.cloned.1.call-start = ((), (), s32[]{:S(2)}) async-start(), calls=%async_computation.13 | async-start | bytes 4866048 | tf_op jit(solution)/shard_map/all_gather | solution.py:302
  16.1 685.0 %all-gather.24.cloned.1.call-start = ((), (), s32[]{:S(2)}) async-start(), calls=%async_computation.14 | async-start | bytes 3244032 | tf_op jit(solution)/shard_map/all_gather | solution.py:313
  16.8 1215.9 %reduce-scatter.17.cloned.1.call-start = ((), (), s32[]{:S(2)}) async-start(), calls=%async_computation.19 | async-start | bytes 2433024 | tf_op jit(solution)/shard_map/reduce_scatter | solution.py:359
  64.1 546.8 %copy-start.96 = (f32[768]{0:T(1024)}, f32[768]{0:T(1024)S(1)}, u32[]{:S(2)}) copy-start(f32[768]{0:T(1024)S(1)} %get-tuple-element.43) | copy-start | bytes 9220
  64.1 546.8 %copy-start.119 = (f32[768]{0:T(1024)}, f32[768]{0:T(1024)S(1)}, u32[]{:S(2)}) copy-start(f32[768]{0:T(1024)S(1)} %get-tuple-element.42) | copy-start | bytes 9220
  64.1 576.3 %copy-start.117 = (f32[768]{0:T(1024)}, f32[768]{0:T(1024)S(1)}, u32[]{:S(2)}) copy-start(f32[768]{0:T(1024)S(1)} %get-tuple-element.40) | copy-start | bytes 9220
  68.7 321.3 %copy-start.53 = (bf16[512,192]{1,0:T(8,128)(2,1)}, bf16[512,192]{1,0:T(8,128)(2,1)S(1)}, u32[]{:S(2)}) copy-start(bf16[512,192]{1,0:T(8,128)(2,1)S(1)} %get-tuple-element.133) | copy-start | bytes 589828
  68.7 321.2 %copy-start.55 = (bf16[512,192]{1,0:T(8,128)(2,1)}, bf16[512,192]{1,0:T(8,128)(2,1)S(1)}, u32[]{:S(2)}) copy-start(bf16[512,192]{1,0:T(8,128)(2,1)S(1)} %get-tuple-element.134) | copy-start | bytes 589828
  68.7 446.9 %copy-start.2 = (f32[512,192]{1,0:T(8,128)}, f32[512,192]{1,0:T(8,128)S(1)}, u32[]{:S(2)}) copy-start(f32[512,192]{1,0:T(8,128)S(1)} %get-tuple-element.132) | copy-start | bytes 1179652
  68.8 446.9 %copy-start.4 = (f32[512,192]{1,0:T(8,128)}, f32[512,192]{1,0:T(8,128)S(1)}, u32[]{:S(2)}) copy-start(f32[512,192]{1,0:T(8,128)S(1)} %get-tuple-element.135) | copy-start | bytes 1179652
  68.8 446.9 %copy-start.6 = (f32[512,192]{1,0:T(8,128)}, f32[512,192]{1,0:T(8,128)S(1)}, u32[]{:S(2)}) copy-start(f32[512,192]{1,0:T(8,128)S(1)} %get-tuple-element.144) | copy-start | bytes 1179652
  68.8 446.9 %copy-start.8 = (f32[512,192]{1,0:T(8,128)}, f32[512,192]{1,0:T(8,128)S(1)}, u32[]{:S(2)}) copy-start(f32[512,192]{1,0:T(8,128)S(1)} %get-tuple-element.147) | copy-start | bytes 1179652
  74.7 315.3 %copy-start.58 = (bf16[512,192]{1,0:T(8,128)(2,1)S(1)}, bf16[512,192]{1,0:T(8,128)(2,1)}, u32[]{:S(2)}) copy-start(bf16[512,192]{1,0:T(8,128)(2,1)} %copy-done.57) | copy-start | bytes 589828
  74.7 315.3 %copy-start.61 = (bf16[512,192]{1,0:T(8,128)(2,1)S(1)}, bf16[512,192]{1,0:T(8,128)(2,1)}, u32[]{:S(2)}) copy-start(bf16[512,192]{1,0:T(8,128)(2,1)} %copy-done.60) | copy-start | bytes 589828
  392.4 218.5 %copy-start.83 = (f32[512]{0:T(512)}, f32[512]{0:T(512)S(1)}, u32[]{:S(2)}) copy-start(f32[512]{0:T(512)S(1)} %broadcast_multiply_fusion.11) | copy-start | bytes 6148
  902.8 331.3 %reduce-scatter.11.cloned.1.call-start = ((), (), s32[]{:S(2)}) async-start(), calls=%async_computation.16 | async-start | bytes 2433024 | tf_op jit(solution)/shard_map/reduce_scatter | solution.py:356
  974.0 261.7 %reduce-scatter.15.cloned.1.call-start = ((), (), s32[]{:S(2)}) async-start(), calls=%async_computation.18 | async-start | bytes 4866048 | tf_op jit(solution)/shard_map/reduce_scatter | solution.py:358
  992.5 351.3 %reduce-scatter.13.cloned.1.call-start = ((), (), s32[]{:S(2)}) async-start(), calls=%async_computation.17 | async-start | bytes 7299072 | tf_op jit(solution)/shard_map/reduce_scatter | solution.py:357
  1000.7 484.0 %reduce-scatter.19.cloned.1.call-start = ((), (), s32[]{:S(2)}) async-start(), calls=%async_computation.20 | async-start | bytes 9732096 | tf_op jit(solution)/shard_map/reduce_scatter | solution.py:360
  1009.4 616.5 %reduce-scatter.21.cloned.1.call-start = ((), (), s32[]{:S(2)}) async-start(), calls=%async_computation.21 | async-start | bytes 9732096 | tf_op jit(solution)/shard_map/reduce_scatter | solution.py:361
  1018.9 1393.3 %reduce-scatter.9.cloned.1.call-start = ((), (), s32[]{:S(2)}) async-start(), calls=%async_computation.15 | async-start | bytes 97320960 | tf_op jit(solution)/shard_map/reduce_scatter | solution.py:355
  1181.7 1279.1 %copy-start.95 = (f32[6,24]{1,0:T(8,128)S(1)}, f32[6,24]{1,0:T(8,128)}, u32[]{:S(2)}) copy-start(f32[6,24]{1,0:T(8,128)} %param.45) | copy-start | bytes 1732
  1181.7 1279.1 %copy-start.115 = (f32[6,24]{1,0:T(8,128)S(1)}, f32[6,24]{1,0:T(8,128)}, u32[]{:S(2)}) copy-start(f32[6,24]{1,0:T(8,128)} %param.61) | copy-start | bytes 1732
  1181.7 1279.1 %copy-start.116 = (f32[6,24]{1,0:T(8,128)S(1)}, f32[6,24]{1,0:T(8,128)}, u32[]{:S(2)}) copy-start(f32[6,24]{1,0:T(8,128)} %param.53) | copy-start | bytes 1732
  1232.0 395.5 %copy-start.81 = (f32[6,768]{1,0:T(8,128)}, f32[6,768]{1,0:T(8,128)S(1)}, u32[]{:S(2)}) copy-start(f32[6,768]{1,0:T(8,128)S(1)} %all-reduce) | copy-start | bytes 55300
  1627.5 842.6 %copy-start.64 = (f32[24,3072]{1,0:T(8,128)S(1)}, f32[24,3072]{1,0:T(8,128)}, u32[]{:S(2)}) copy-start(f32[24,3072]{1,0:T(8,128)} %param.43) | copy-start | bytes 884740
  (115 other events, 2215.2 us)
Sparse Core Ops, SparseCore 0:
  11.5 59.9 all-gather.15
  75.0 259.2 all-gather.9
  337.7 52.1 all-gather.11
  393.3 58.9 all-gather.13
  455.6 52.8 all-gather.17
  511.8 62.5 all-gather.19
  577.9 62.4 all-gather.21
  643.3 57.7 all-gather.23
  903.0 99.8 reduce-scatter.16
  1009.4 98.0 reduce-scatter.10
  1113.0 105.9 reduce-scatter.14
  1225.5 118.2 reduce-scatter.12
  1349.7 134.9 reduce-scatter.18
  1491.4 134.4 reduce-scatter.20
  1632.1 779.9 reduce-scatter.8
where the time goes:
time: 2500 us; the launch traced here: 2490 us
  waiting for transfers between devices  1590 us (64%)
  other arithmetic  273 us (11%)
  matrix products  235 us (9%)
  local copies, waits for them, and re-layouts  193 us (8%)
  blocking collectives  171 us (7%)
    reduce_scatter x1, waiting for transfers between devices, per_device(): lax.psum_scatter(table_grad, 'dp', scatter_dimension=0, tiled=True)  785 us
    all_gather x1, waiting for transfers between devices, per_device(): lax.all_gather(vocabulary.astype(jnp.bfloat16), 'dp', axis=0, tiled=True)  260 us
    reduce_scatter x1, waiting for transfers between devices, per_device(): lax.psum_scatter(layer_grads[5], 'dp', scatter_dimension=0, tiled=True)  140 us
    reduce_scatter x1, waiting for transfers between devices, per_device(): lax.psum_scatter(layer_grads[4], 'dp', scatter_dimension=0, tiled=True)  139 us
    reduce_scatter x1, waiting for transfers between devices, per_device(): lax.psum_scatter(layer_grads[1], 'dp', scatter_dimension=0, tiled=True)  107 us
    another operation x4, other arithmetic  68.2 us
    scatter-add x1, other arithmetic, per_device(): jnp.zeros(weights_back[0].shape, jnp.float32).at[cache['entry']]  66.7 us
    scatter-add x1, other arithmetic, per_device(): table_grad.at[tokens].add(positive_grad * states_low.astype(jnp.float32))  65.7 us
  transfers between devices with their start and end apart: 15, of which 10 were waited for; matrix products, arithmetic and copies ran while one was open for 20% of the time, Pallas kernels for 0%

commit v1 on v0

v1 whole, which is shorter than its diff:
```python
from functools import partial

import jax
import jax.numpy as jnp
from jax import lax
from jax.experimental import pallas as pl
from jax.experimental.pallas import tpu as pltpu
from jax.sharding import PartitionSpec as P

HD = 64
DOCS = 8
STEP = 10
MESH = pl.DeviceIdType.MESH

mask_token = 103
ln_epsilon = 1e-06
momentum_decay = 0.9
learn_rate = 5000.0
table_rate = 1000000.0
clip_limit = 0.01
average_cap = 0.999


def sinusoids(positions, count):
    ranks = jnp.arange(count).astype(jnp.float32)
    omegas = jnp.power(10000.0, -ranks / count)
    angle_x = positions[0].astype(jnp.float32)[:, None] * omegas[None, :]
    angle_y = positions[1].astype(jnp.float32)[:, None] * omegas[None, :]
    return (jnp.sin(angle_x), jnp.cos(angle_x), jnp.sin(angle_y), jnp.cos(angle_y))


def rotate(table, waves):
    sin_x, cos_x, sin_y, cos_y = waves
    count = sin_x.shape[-1]
    sine_x = table[..., :count]
    cosine_x = table[..., count : 2 * count]
    sine_y = table[..., 2 * count : 3 * count]
    cosine_y = table[..., 3 * count :]
    return jnp.concatenate(
        [
            sine_x * sin_x + cosine_x * cos_x,
            sine_y * sin_y + cosine_y * cos_y,
            cosine_x * sin_x - sine_x * cos_x,
            cosine_y * sin_y - sine_y * cos_y,
        ],
        -1,
    )


def rotate_back(upstream, waves):
    sin_x, cos_x, sin_y, cos_y = waves
    count = sin_x.shape[-1]
    first = upstream[..., :count]
    second = upstream[..., count : 2 * count]
    third = upstream[..., 2 * count : 3 * count]
    fourth = upstream[..., 3 * count :]
    return jnp.concatenate(
        [
            first * sin_x - third * cos_x,
            first * cos_x + third * sin_x,
            second * sin_y - fourth * cos_y,
            second * cos_y + fourth * sin_y,
        ],
        -1,
    )


def layer_norm(rows, gain, bias):
    centred = rows - jnp.mean(rows, -1, keepdims=True)
    rescale = lax.rsqrt(jnp.mean(centred * centred, -1, keepdims=True) + ln_epsilon)
    whitened = centred * rescale
    return (whitened * gain + bias, whitened, rescale)


def norm_back(upstream, whitened, rescale, gain):
    scaled = upstream * gain
    inner = (
        scaled
        - jnp.mean(scaled, -1, keepdims=True)
        - whitened * jnp.mean(scaled * whitened, -1, keepdims=True)
    )
    return (rescale * inner, jnp.sum(upstream * whitened, 0), jnp.sum(upstream, 0))


def dot_nn(left, right):
    return lax.dot_general(
        left, right, (((1,), (0,)), ((), ())), preferred_element_type=jnp.float32
    )


def dot_tn(left, right):
    return lax.dot_general(
        left, right, (((0,), (0,)), ((), ())), preferred_element_type=jnp.float32
    )


def dot_nt(left, right):
    return lax.dot_general(
        left, right, (((1,), (1,)), ((), ())), preferred_element_type=jnp.float32
    )


def exchange_kernel(n, src, dst, send_sem, recv_sem, own_sem):
    me = lax.axis_index("dp")
    barrier = pltpu.get_barrier_semaphore()

    def greet(step, carry):
        pl.semaphore_signal(
            barrier, inc=1, device_id=(lax.rem(me + step, n),), device_id_type=MESH
        )
        return carry

    lax.fori_loop(1, n, greet, 0)
    own = pltpu.make_async_copy(src.at[me], dst.at[me], own_sem)
    own.start()
    pl.semaphore_wait(barrier, n - 1)

    def copy(step):
        peer = lax.rem(me + step, n)
        return pltpu.make_async_remote_copy(
            src_ref=src.at[peer],
            dst_ref=dst.at[me],
            send_sem=send_sem.at[step],
            recv_sem=recv_sem.at[step],
            device_id=(peer,),
            device_id_type=MESH,
        )

    def start(step, carry):
        copy(step).start()
        return carry

    def finish(step, carry):
        copy(step).wait()
        return carry

    lax.fori_loop(1, n, start, 0)
    lax.fori_loop(1, n, finish, 0)
    own.wait()


def exchange(blocks, ident, name):
    n = blocks.shape[0]
    return pl.pallas_call(
        partial(exchange_kernel, n),
        name=name,
        out_shape=jax.ShapeDtypeStruct(blocks.shape, blocks.dtype),
        in_specs=[pl.BlockSpec(memory_space=pl.ANY)],
        out_specs=pl.BlockSpec(memory_space=pl.ANY),
        scratch_shapes=[
            pltpu.SemaphoreType.DMA((n,)),
            pltpu.SemaphoreType.DMA((n,)),
            pltpu.SemaphoreType.DMA,
        ],
        compiler_params=pltpu.CompilerParams(collective_id=ident, has_side_effects=True),
        cost_estimate=pl.CostEstimate(
            flops=0, bytes_accessed=2 * blocks.size * blocks.dtype.itemsize, transcendentals=0
        ),
    )(blocks)


def plan_kernel(
    n, rows_own, capacity, tok_col, tok_row, mask_row, doc, info, lists, place
):
    size = tok_col.shape[0]
    ids_col = tok_col[...]
    ids_row = tok_row[...]
    owner_col = lax.div(ids_col, rows_own)
    owner_row = lax.div(ids_row, rows_own)
    at_col = lax.broadcasted_iota(jnp.int32, (size, size), 0)
    at_row = lax.broadcasted_iota(jnp.int32, (size, size), 1)
    same = ids_col == ids_row
    first_col = jnp.min(jnp.where(same, at_row, size), 1, keepdims=True)
    first_row = jnp.min(jnp.where(same, at_col, size), 0, keepdims=True)
    leads_row = first_row == lax.broadcasted_iota(jnp.int32, (1, size), 1)
    leads_col = first_col == lax.broadcasted_iota(jnp.int32, (size, 1), 0)
    ahead = (owner_col == owner_row) & leads_row & (at_row < first_col)
    slot = jnp.sum(jnp.where(ahead, 1.0, 0.0), 1, keepdims=True).astype(jnp.int32)
    fits = slot < capacity - 1
    place[...] = jnp.where(fits, owner_col * capacity + slot, -1)
    over = jnp.max(jnp.where(fits, 0.0, 1.0), keepdims=True)
    local = ids_col - owner_col * rows_own + 1
    high = lax.div(local, 128)
    to_owner = lax.broadcasted_iota(jnp.int32, (size, n), 1) == owner_col
    to_owner = to_owner & leads_col & fits
    in_slot = lax.broadcasted_iota(jnp.int32, (size, 128), 1) == slot
    in_slot = jnp.where(in_slot, 1.0, 0.0).astype(jnp.bfloat16)
    high_part = jnp.where(to_owner, high.astype(jnp.float32), 0.0).astype(jnp.bfloat16)
    low_part = jnp.where(to_owner, (local - high * 128).astype(jnp.float32), 0.0)
    table = dot_tn(high_part, in_slot) * 128.0 + dot_tn(low_part.astype(jnp.bfloat16), in_slot)
    lane = lax.broadcasted_iota(jnp.int32, (n, 128), 1)
    line = lax.broadcasted_iota(jnp.int32, (n, 128), 0)
    fixed = (line == mask_token // rows_own) & (lane == capacity - 1)
    table = jnp.where(fixed, float(mask_token % rows_own + 1), table)
    count = jnp.sum(mask_row[...].astype(jnp.float32), keepdims=True)
    table = jnp.where(lane == 125, count, table)
    table = jnp.where(lane == 126, doc[0].astype(jnp.float32), table)
    table = jnp.where(lane == 127, over, table)
    lists[...] = jnp.broadcast_to(table[:, None, :], lists.shape)


def make_plan(tokens, masking, documents, n, rows_own, capacity):
    size = tokens.shape[0]
    vmem = pl.BlockSpec(memory_space=pltpu.VMEM)
    return pl.pallas_call(
        partial(plan_kernel, n, rows_own, capacity),
        name="plan",
        out_shape=(
            jax.ShapeDtypeStruct((n, 8, 128), jnp.float32),
            jax.ShapeDtypeStruct((size, 1), jnp.int32),
        ),
        in_specs=[vmem, vmem, vmem, pl.BlockSpec(memory_space=pltpu.SMEM), vmem],
        out_specs=(vmem, vmem),
        compiler_params=pltpu.CompilerParams(vmem_limit_bytes=32 * 2**20),
    )(
        tokens[:, None],
        tokens[None, :],
        masking[None, :],
        documents,
        jnp.zeros((8, 128), jnp.float32),
    )


def forward(weights, rows, positions):
    box_map, mix_map, rel_map, out_map, up_map, down_map, norm_rows = weights
    gains = norm_rows.astype(jnp.float32)
    count_tok = rows.shape[0]
    model = rows.shape[1]
    heads = model // HD
    sin_count = box_map.shape[1]
    waves = sinusoids(positions, sin_count // 4)
    boxes = jnp.concatenate(waves, -1).astype(jnp.bfloat16)
    embedded = rows + dot_nt(boxes, box_map)
    first = layer_norm(embedded, gains[0], gains[1])
    normed = first[0].astype(jnp.bfloat16)
    thirds = [dot_nn(normed, part).astype(jnp.bfloat16) for part in mix_map]
    queries, keys_low, values_low = [
        third.reshape(count_tok, heads, HD).transpose(1, 0, 2) for third in thirds
    ]
    rel_text = rel_map[:model].reshape(heads, HD, sin_count)
    rel_box = rel_map[model:].reshape(heads, HD, sin_count)
    text_terms = jnp.einsum("htd,hdf->htf", queries, rel_text, preferred_element_type=jnp.float32)
    box_terms = jnp.einsum("htd,hdf->htf", keys_low, rel_box, preferred_element_type=jnp.float32)
    bases = jnp.concatenate([waves[1], waves[3], waves[0], waves[2]], -1).astype(jnp.bfloat16)
    text_rot = rotate(text_terms, waves).astype(jnp.bfloat16)
    box_rot = rotate(box_terms, waves).astype(jnp.bfloat16)
    scores = (
        jnp.einsum("htd,hsd->hts", queries, keys_low, preferred_element_type=jnp.float32)
        + jnp.einsum("htf,sf->hts", text_rot, bases, preferred_element_type=jnp.float32)
        + jnp.einsum("tf,hsf->hts", bases, box_rot, preferred_element_type=jnp.float32)
    ) * HD ** (-0.5)
    highest = jnp.max(scores, -1, keepdims=True)
    totals = highest + jnp.log(jnp.sum(jnp.exp(scores - highest), -1, keepdims=True))
    probs = jnp.exp(scores - totals)
    attended = jnp.einsum(
        "hts,hsd->thd", probs.astype(jnp.bfloat16), values_low, preferred_element_type=jnp.float32
    )
    attended = attended.reshape(count_tok, model).astype(jnp.bfloat16)
    second = layer_norm(first[0] + dot_nn(attended, out_map), gains[2], gains[3])
    middle = second[0].astype(jnp.bfloat16)
    hidden_pre = [dot_nn(middle, part) for part in up_map]
    hidden = [jax.nn.gelu(part, approximate=False).astype(jnp.bfloat16) for part in hidden_pre]
    lowered = sum(dot_nn(part, weight) for part, weight in zip(hidden, down_map))
    third = layer_norm(second[0] + lowered, gains[4], gains[5])
    return {
        "waves": waves,
        "boxes": boxes,
        "bases": bases,
        "first": first,
        "normed": normed,
        "queries": queries,
        "keys": keys_low,
        "values": values_low,
        "probs": probs,
        "attended": attended,
        "second": second,
        "middle": middle,
        "hidden_pre": hidden_pre,
        "hidden": hidden,
        "third": third,
    }


def backward(weights, cache, d_states):
    box_map, mix_map, rel_map, out_map, up_map, down_map, norm_rows = weights
    gains = norm_rows.astype(jnp.float32)
    count_tok = d_states.shape[0]
    model = d_states.shape[1]
    heads = model // HD
    sin_count = box_map.shape[1]
    d_mid, gain_last, bias_last = norm_back(
        d_states, cache["third"][1], cache["third"][2], gains[4]
    )
    d_down = d_mid.astype(jnp.bfloat16)
    gelu_exact = partial(jax.nn.gelu, approximate=False)
    grad_down, grad_up, d_second = [], [], d_mid
    for pre, hidden, up, down in zip(cache["hidden_pre"], cache["hidden"], up_map, down_map):
        grad_down.append(dot_tn(hidden, d_down))
        d_pre = jax.vjp(gelu_exact, pre)[1](dot_nt(d_down, down))[0].astype(jnp.bfloat16)
        grad_up.append(dot_tn(cache["middle"], d_pre))
        d_second = d_second + dot_nt(d_pre, up)
    d_lower, gain_mid, bias_mid = norm_back(
        d_second, cache["second"][1], cache["second"][2], gains[2]
    )
    d_attn = d_lower.astype(jnp.bfloat16)
    grad_out = dot_tn(cache["attended"], d_attn)
    d_attended = dot_nt(d_attn, out_map).astype(jnp.bfloat16).reshape(count_tok, heads, HD)
    d_attended = d_attended.transpose(1, 0, 2)
    probs, bases = cache["probs"], cache["bases"]
    d_probs = jnp.einsum(
        "htd,hsd->hts", d_attended, cache["values"], preferred_element_type=jnp.float32
    )
    grad_values = jnp.einsum(
        "hts,htd->hsd", probs.astype(jnp.bfloat16), d_attended, preferred_element_type=jnp.float32
    )
    d_scores = (probs * (d_probs - jnp.sum(d_probs * probs, -1, keepdims=True))).astype(
        jnp.bfloat16
    )
    scale = HD ** (-0.5)
    d_text = jnp.einsum("hts,sf->htf", d_scores, bases, preferred_element_type=jnp.float32) * scale
    d_box = jnp.einsum("hts,tf->hsf", d_scores, bases, preferred_element_type=jnp.float32) * scale
    d_text = rotate_back(d_text, cache["waves"]).astype(jnp.bfloat16)
    d_box = rotate_back(d_box, cache["waves"]).astype(jnp.bfloat16)
    rel_text = rel_map[:model].reshape(heads, HD, sin_count)
    rel_box = rel_map[model:].reshape(heads, HD, sin_count)
    grad_rel = jnp.concatenate(
        [
            jnp.einsum(
                "htd,htf->hdf", cache["queries"], d_text, preferred_element_type=jnp.float32
            ).reshape(model, sin_count),
            jnp.einsum(
                "htd,htf->hdf", cache["keys"], d_box, preferred_element_type=jnp.float32
            ).reshape(model, sin_count),
        ],
        0,
    )
    grad_queries = jnp.einsum(
        "hts,hsd->htd", d_scores, cache["keys"], preferred_element_type=jnp.float32
    ) * scale + jnp.einsum("htf,hdf->htd", d_text, rel_text, preferred_element_type=jnp.float32)
    grad_keys = jnp.einsum(
        "hts,htd->hsd", d_scores, cache["queries"], preferred_element_type=jnp.float32
    ) * scale + jnp.einsum("htf,hdf->htd", d_box, rel_box, preferred_element_type=jnp.float32)
    d_joined = [
        part.astype(jnp.bfloat16).transpose(1, 0, 2).reshape(count_tok, model)
        for part in (grad_queries, grad_keys, grad_values)
    ]
    grad_mix = [dot_tn(cache["normed"], part) for part in d_joined]
    d_first = d_lower + sum(dot_nt(part, weight) for part, weight in zip(d_joined, mix_map))
    d_embedded, gain_low, bias_low = norm_back(
        d_first, cache["first"][1], cache["first"][2], gains[0]
    )
    grad_box = dot_tn(d_embedded.astype(jnp.bfloat16), cache["boxes"])
    grad_norms = jnp.stack([gain_low, bias_low, gain_mid, bias_mid, gain_last, bias_last], 0)
    return (d_embedded, (grad_box, grad_mix, grad_rel, grad_out, grad_up, grad_down, grad_norms))


def per_device(
    n,
    tokens,
    positions,
    documents,
    masking,
    negative_page,
    negative_row,
    pages,
    vocabulary,
    geometry,
    mixing,
    relative,
    merging,
    widening,
    narrowing,
    scaling,
    moment_vocabulary,
    moment_geometry,
    moment_mixing,
    moment_relative,
    moment_merging,
    moment_widening,
    moment_narrowing,
    moment_scaling,
    average_vocabulary,
    average_geometry,
    average_mixing,
    average_relative,
    average_merging,
    average_widening,
    average_narrowing,
    average_scaling,
):
    me = lax.axis_index("dp")
    size = tokens.shape[0]
    rows_own, model = vocabulary.shape
    page_rows = pages.shape[1]
    capacity = max(16, -(-2 * size // n) // 16 * 16)
    slots = n * capacity
    mask_float = masking.astype(jnp.float32)
    low = jnp.bfloat16

    parts = (
        geometry.T.astype(low),
        relative.T.astype(low),
        *[mixing[:, k * model : (k + 1) * model].astype(low) for k in range(3)],
    )
    later = (
        merging.astype(low),
        *[
            widening[:, k * model : (k + 1) * model].astype(low)
            for k in range(widening.shape[1] // model)
        ],
        narrowing.astype(low),
        pages.reshape(-1, model),
    )

    def gather(pieces):
        rows = [piece.shape[0] for piece in pieces]
        joined = lax.all_gather(jnp.concatenate(pieces, 0), "dp", axis=0, tiled=False)
        out, at = [], 0
        for count in rows:
            out.append(joined[:, at : at + count].reshape(-1, model))
            at += count
        return out

    early = gather(parts)
    late = gather(later)
    norm_rows = lax.all_gather(scaling.astype(low), "dp", axis=1, tiled=True)
    box_map, rel_map, mix_map = early[0], early[1], early[2:5]
    out_map, up_map, down_full, bank = late[0], late[1:-2], late[-2], late[-1]

    lists, place = make_plan(tokens, masking, documents, n, rows_own, capacity)
    asked = exchange(lists, 1, "ask")[:, 0, :]
    doc_of, count_of = asked[:, 126], asked[:, 125]
    overflow = jnp.max(asked[:, 127]) > 0.0
    my_count = jnp.sum(jnp.where(doc_of == documents[0].astype(jnp.float32), count_of, 0.0))
    share = 1.0 / (DOCS * jnp.maximum(my_count, 1.0))
    wanted = asked[:, :capacity].reshape(slots, 1)
    picks = (wanted == (jnp.arange(rows_own) + 1).astype(jnp.float32)[None, :]).astype(low)
    answer = dot_nn(picks, vocabulary.astype(low)).astype(low)
    table_rows = exchange(answer.reshape(n, capacity, model), 2, "rows").reshape(slots, model)
    fixed = (mask_token // rows_own) * capacity + capacity - 1
    seats = (place == jnp.arange(slots)[None, :]).astype(low)
    target_rows = dot_nn(seats, table_rows)
    mask_rows = table_rows[fixed : fixed + 1].astype(jnp.float32)

    def dense_rows():
        table = lax.all_gather(vocabulary.astype(low), "dp", axis=0, tiled=True)
        return (
            table[tokens].astype(jnp.float32),
            table[mask_token : mask_token + 1].astype(jnp.float32),
        )

    target_rows, mask_rows = lax.cond(overflow, dense_rows, lambda: (target_rows, mask_rows))
    entry_rows = jnp.where(masking[:, None] == 1, mask_rows, target_rows)

    ff = len(up_map)
    down_map = [down_full[k * model : (k + 1) * model] for k in range(ff)]
    weights = (box_map, mix_map, rel_map, out_map, up_map, down_map, norm_rows)
    cache = forward(weights, entry_rows, positions)

    states_low = cache["third"][0].astype(low)
    inv_root = model ** (-0.5)
    positive = jnp.sum(states_low.astype(jnp.float32) * target_rows, -1, keepdims=True) * inv_root
    flat_index = (negative_page * page_rows + negative_row).T
    count_neg = flat_index.shape[1]
    width = bank.shape[0]
    repeated = jnp.tile(flat_index, (1, width // count_neg))
    chosen = repeated == jnp.arange(width)[None, :]
    logits = jnp.where(chosen, dot_nt(states_low, bank) * inv_root, -jnp.inf)
    highest = jnp.maximum(jnp.max(logits, -1, keepdims=True), positive)
    powers = jnp.exp(logits - highest)
    lead = jnp.exp(positive - highest)
    total = jnp.sum(powers, -1, keepdims=True) + lead
    per_token = highest + jnp.log(total) - positive
    mask_col = mask_float[:, None]
    loss_part = share * jnp.sum(mask_col * per_token)
    weight_map = (powers * (share * mask_col / total) * inv_root).astype(low)
    positive_grad = share * mask_col * (lead / total - 1.0) * inv_root
    d_states = positive_grad * target_rows + dot_nn(weight_map, bank)

    d_embedded, layer_grads = backward(weights, cache, d_states)

    positive_rows = positive_grad * states_low.astype(jnp.float32)

    def sparse_table():
        token_grads = jnp.where(mask_col == 1.0, positive_rows, d_embedded).astype(low)
        mask_grad = jnp.sum(mask_col * d_embedded, 0, keepdims=True)
        sent = dot_tn(seats, token_grads)
        sent = jnp.where(jnp.arange(slots)[:, None] == fixed, mask_grad, sent).astype(low)
        came = exchange(sent.reshape(n, capacity, model), 3, "grads").reshape(slots, model)
        return dot_tn(picks, came)

    def dense_table():
        entry = jnp.where(masking == 1, mask_token, tokens)
        table_grad = jnp.zeros((rows_own * n, model), jnp.float32).at[entry].add(d_embedded)
        table_grad = table_grad.at[tokens].add(positive_rows)
        return lax.psum_scatter(table_grad, "dp", scatter_dimension=0, tiled=True)

    table_piece = lax.cond(overflow, dense_table, sparse_table)

    grad_box, grad_mix, grad_rel, grad_out, grad_up, grad_down, grad_norms = layer_grads
    grad_down = jnp.concatenate(grad_down, 0)

    def scatter(pieces):
        blocks = [piece.astype(low).reshape(n, -1, model) for piece in pieces]
        rows = [block.shape[1] for block in blocks]
        joined = jnp.concatenate(blocks, 1).reshape(-1, model)
        mine = lax.psum_scatter(joined, "dp", scatter_dimension=0, tiled=True).astype(jnp.float32)
        out, at = [], 0
        for count in rows:
            out.append(mine[at : at + count])
            at += count
        return out

    first = scatter([grad_down, *grad_up])
    last = scatter([grad_out, grad_box, grad_rel, *grad_mix])
    norm_piece = lax.psum_scatter(grad_norms, "dp", scatter_dimension=1, tiled=True)
    reduced = (
        table_piece,
        last[1].T,
        jnp.concatenate(last[3:], 1),
        last[2].T,
        last[0],
        jnp.concatenate(first[1:], 1),
        first[0],
        norm_piece,
    )
    square = sum((jnp.sum(piece * piece) for piece in reduced))
    message = jnp.where(jnp.arange(128) == 0, square, jnp.where(jnp.arange(128) == 1, loss_part, 0.0))
    sums = exchange(jnp.broadcast_to(message, (n, 8, 128)), 4, "totals")
    sums = jnp.sum(sums[:, 0, :2], 0)
    loss = sums[1]
    grad_norm = jnp.sqrt(sums[0])
    factor = clip_limit / jnp.maximum(grad_norm, clip_limit)
    decay = min(average_cap, (1.0 + STEP) / (10.0 + STEP))
    masters = (vocabulary, geometry, mixing, relative, merging, widening, narrowing, scaling)
    moments = (
        moment_vocabulary,
        moment_geometry,
        moment_mixing,
        moment_relative,
        moment_merging,
        moment_widening,
        moment_narrowing,
        moment_scaling,
    )
    averages = (
        average_vocabulary,
        average_geometry,
        average_mixing,
        average_relative,
        average_merging,
        average_widening,
        average_narrowing,
        average_scaling,
    )
    rates = (table_rate,) + (learn_rate,) * 7
    fresh, speeds, smooths = ([], [], [])
    for master, moment, average, piece, rate in zip(masters, moments, averages, reduced, rates):
        clipped = piece * factor
        velocity = momentum_decay * moment + clipped
        updated = master - rate * (clipped + momentum_decay * velocity)
        fresh.append(updated)
        speeds.append(velocity)
        smooths.append(decay * average + (1.0 - decay) * updated)
    return (loss, grad_norm, *fresh, *speeds, *smooths)


ROWS = P("dp", None)
COLS = P(None, "dp")
WEIGHTS = (ROWS, COLS, ROWS, COLS, ROWS, ROWS, ROWS, COLS)


def solution(mesh):
    return jax.shard_map(
        partial(per_device, mesh.shape["dp"]),
        mesh=mesh,
        in_specs=(P("dp"), COLS, P("dp"), P("dp"), COLS, COLS, P("dp", None, None)) + 3 * WEIGHTS,
        out_specs=(P(), P()) + 3 * WEIGHTS,
        check_vma=False,
    )
```

time: 2500 us -> 855 us (0.34)
  waiting for transfers between devices: 1590 us -> 228 us
  other arithmetic: 273 us -> 118 us
  local copies, waits for them, and re-layouts: 193 us -> 71.1 us
  Pallas kernels: 0 us -> 84.6 us
  blocking collectives: 171 us -> 102 us
    reduce_scatter x7 -> x2, waiting for transfers between devices: 1170 us -> 211 us  [scatter(): lax.psum_scatter(joined, 'dp', scatter_dimension=0, tiled=True)]
    all_gather x8 -> x2, waiting for transfers between devices: 420 us -> 15.3 us  [gather(): lax.all_gather(jnp.concatenate(pieces, 0), 'dp', axis=0, tiled=False)]
    scatter-add x2 -> x0, other arithmetic: 132 us -> none  [the longest x1 66.7 us: per_device(): jnp.zeros(weights_back[0].shape, jnp.float32).at[cache['entry']]]
    pallas_call x0 -> x5, Pallas kernels: none -> 84.6 us  [the longest x4 82.6 us: exchange(): pl.pallas_call(partial(exchange_kernel, n), name=name, out_shape=jax.Shap...]
    psum x2 -> x0, blocking collectives: 78 us -> none  [the longest x1 39.4 us: per_device(): norm_total = lax.psum(square, 'dp')]
    gather x7 -> x0, local copies, waits for them, and re-layouts: 70.4 us -> none  [the longest x5 58 us: per_device(): jnp.take_along_axis(raw, jnp.clip(local, 0, rows.shape[0] - 1).T, axis=1)]
    broadcast_in_dim x1 -> x3, local copies, waits for them, and re-layouts: 30.1 us -> 1.49 us  [the longest x1 0.82 us: make_plan(): tokens[:, None]]
    dot_general x28 -> x60, matrix products: 235 us -> 216 us  [the longest x15 54.4 us: dot_nn(): lax.dot_general(left, right, (((1,), (0,)), ((), ())), preferred_element_...]
  transfers between devices with their start and end apart: 15 -> 4, of which waited for: 10 -> 3; matrix products, arithmetic and copies ran while one was open for 20% -> 18% of each run, Pallas kernels for 0% -> 0%
where the time goes in v1:
time: 855 us; the launch traced here: 848 us
  waiting for transfers between devices  228 us (27%)
  matrix products  216 us (25%)
  other arithmetic  118 us (14%)
  blocking collectives  102 us (12%)
  Pallas kernels  84.6 us (10%)
  local copies, waits for them, and re-layouts  71.1 us (8%)
  between operations  27.7 us (3%)
    reduce_scatter x2, waiting for transfers between devices, scatter(): lax.psum_scatter(joined, 'dp', scatter_dimension=0, tiled=True)  211 us
    pallas_call x4, Pallas kernels, exchange(): pl.pallas_call(partial(exchange_kernel, n), name=name, out_shape=jax.Shap...  82.6 us
    another operation x6, other arithmetic  66 us
    dot_general x15, matrix products, dot_nn(): lax.dot_general(left, right, (((1,), (0,)), ((), ())), preferred_element_...  54.4 us
    all_gather x1, blocking collectives, per_device(): norm_rows = lax.all_gather(scaling.astype(low), 'dp', axis=1, tiled=True)  51 us
    unnamed x1, blocking collectives  50.7 us
    unnamed x275, local copies, waits for them, and re-layouts  32.6 us
    add x8, other arithmetic, per_device(): smooths.append(decay * average + (1.0 - decay) * updated)  19.4 us
  transfers between devices with their start and end apart: 4, of which 3 were waited for; matrix products, arithmetic and copies ran while one was open for 18% of the time, Pallas kernels for 0%

profile of v1, /device:TPU:0, one launch (start us, length us, event | category | flops | bytes accessed | tf_op | source)
XLA Modules:
  0.0 847.6 jit_solution(12519215158487477900)
XLA Ops:
  12.1 11.0 %ask.1 = f32[32,8,128]{2,1,0:T(8,128)} custom-call(f32[32,8,128]{2,1,0:T(8,128)} %copy-done), custom_call_target="tpu_custom_call" | custom-call | bytes 262144 | tf_op jit(solution)/shard_map/ask/pallas_call | solution.py:144
  29.0 32.8 %rows.1 = bf16[32,32,768]{2,1,0:T(8,128)(2,1)} custom-call(bf16[32,32,768]{2,1,0:T(8,128)(2,1)} %bitcast.265), custom_call_target="tpu_custom_call" | custom-call | bytes 3145728 | tf_op jit(solution)/shard_map/rows/pallas_call | solution.py:144
  72.0 51.0 %all-gather.2 = bf16[32,24,6]{1,2,0:T(8,128)(2,1)S(1)} all-gather(bf16[1,24,6]{1,2,0:T(8,128)(2,1)S(1)} %convert_bitcast_fusion), channel_id=1, replica_groups=mesh['dp'=32] {'dp'}, dimensions={0}, use_global_device_ids=true | all-gather | bytes 9504 | tf_op jit(solution)/shard_map/all_gather | solution.py:426
  125.9 6.0 copy.102
  140.1 15.3 %all-gather.9.cloned.1.call-done = bf16[4608,768]{1,0:T(8,128)(2,1)} async-done(((bf16[144,768]{1,0:T(8,128)(2,1)}), bf16[4608,768]{1,0:T(8,128)(2,1)}) %all-gather.9.cloned.1.call-update) | async-done | bytes 7077904 | tf_op jit(solution)/shard_map/all_gather | solution.py:417
  179.0 8.2 fusion.115
  187.2 8.0 fusion.116
  195.2 15.8 %add_convert_fusion.7 = (bf16[12,512,192]{2,1,0:T(8,128)(2,1)S(1)}, bf16[12,512,192]{2,1,0:T(8,128)(2,1)}, bf16[12,512,192]{2,1,0:T(8,128)(2,1)}, bf16[12,512,192]{2,1,0:T(8,128)(2,1)}) fusion(f32[12,512,768]{2,1,0:T(8,128)} %fusion.115, f32[512,192]{1,0:T(8,128)S(1)} %get-tuple-element.194, f32[512,192]{1,0:T(8,128)S(1)} %get-tuple-element.191, ...), kind=kLoop, calls=%fused_computation.60 | loop fusion | flops 18874368 | bytes 29884416 | tf_op jit(solution)/shard_map/convert.28
  211.0 17.9 %add_convert_fusion.5 = (bf16[12,512,192]{2,1,0:T(8,128)(2,1)}, bf16[12,512,192]{2,1,0:T(8,128)(2,1)}, bf16[12,512,192]{2,1,0:T(8,128)(2,1)}, bf16[12,512,192]{2,1,0:T(8,128)(2,1)}) fusion(f32[12,512,768]{2,1,0:T(8,128)} %fusion.116, f32[512,192]{1,0:T(8,128)S(1)} %get-tuple-element.194, f32[512,192]{1,0:T(8,128)S(1)} %get-tuple-element.191, ...), kind=kLoop, calls=%fused_computation.56 | loop fusion | flops 18874368 | bytes 29884416 | tf_op jit(solution)/shard_map/convert.20
  229.0 13.2 %fusion.4 = f32[12,512,512]{1,2,0:T(8,128)} fusion(bf16[12,512,192]{2,1,0:T(8,128)(2,1)} %get-tuple-element.160, bf16[12,512,192]{2,1,0:T(8,128)(2,1)} %get-tuple-element.149, bf16[12,512,192]{2,1,0:T(8,128)(2,1)} %get-tuple-element.161, bf16[12,512,192]{2,1,0:T(8,128)(2,1)S(1)} %get-tuple-element.148, bf16[512,192]{1,0:T(8,128)(2,1)} %copy-done.75, ...), kind=kOutput, calls=%fused_computation.25 | convolution fusion | flops 4872732672 | bytes 22806528 | tf_op jit(solution)/shard_map/htf,sf->hts/dot_general | solution.py:249
  242.2 13.2 %fusion.12 = f32[12,512,512]{2,1,0:T(8,128)} fusion(bf16[12,512,192]{2,1,0:T(8,128)(2,1)} %get-tuple-element.162, bf16[12,512,192]{2,1,0:T(8,128)(2,1)} %get-tuple-element.153, bf16[12,512,192]{2,1,0:T(8,128)(2,1)} %get-tuple-element.163, bf16[12,512,192]{2,1,0:T(8,128)(2,1)S(1)} %copy-done.28, bf16[512,192]{1,0:T(8,128)(2,1)} %copy-done.75, ...), kind=kOutput, calls=%fused_computation.33 | convolution fusion | flops 4872732672 | bytes 22806528 | tf_op jit(solution)/shard_map/tf,hsf->hts/dot_general | solution.py:250
  255.4 10.9 %fusion.111 = (f32[12,512]{1,0:T(8,128)S(1)}, f32[12,512,512]{1,2,0:T(8,128)S(1)}) fusion(f32[12,512,512]{2,1,0:T(8,128)} %fusion.12, f32[12,512,512]{1,2,0:T(8,128)} %fusion.4, bf16[12,512,64]{1,2,0:T(8,128)(2,1)} %bitcast.229, bf16[12,512,64]{1,2,0:T(8,128)(2,1)} %bitcast.232), kind=kOutput, calls=%fused_computation.345 | convolution fusion | flops 415229952 | bytes 39346176 | tf_op jit(solution)/shard_map/htd,hsd->hts/dot_general | solution.py:248
  283.9 9.1 %multiply_convert_fusion.5 = (bf16[512,768]{1,0:T(8,128)(2,1)S(1)}, f32[512,768]{1,0:T(8,128)S(1)}, f32[512,768]{1,0:T(8,128)S(1)}) fusion(bf16[512,768]{1,0:T(8,128)(2,1)S(1)} %fusion.71, bf16[768,768]{1,0:T(8,128)(2,1)S(1)} %bitcast.274), kind=kOutput, calls=%fused_computation.145 | convolution fusion | flops 629538816 | bytes 5898240 | tf_op jit(solution)/shard_map/dot_general | solution.py:86
  293.0 5.8 multiply_convert_fusion.6
  304.1 9.2 %multiply_convert_fusion.3 = (bf16[512,768]{1,0:T(8,128)(2,1)S(1)}, f32[512,768]{1,0:T(8,128)S(1)}, f32[512,768]{1,0:T(8,128)S(1)}) fusion(bf16[512,768]{1,0:T(8,128)(2,1)S(1)} %fusion.71, bf16[768,768]{1,0:T(8,128)(2,1)S(1)} %bitcast.251), kind=kOutput, calls=%fused_computation.119 | convolution fusion | flops 629538816 | bytes 5898240 | tf_op jit(solution)/shard_map/dot_general | solution.py:86
  341.3 12.2 %multiply_reduce_fusion.3 = (f32[12,512]{1,0:T(8,128)S(1)}, f32[12,512,512]{1,2,0:T(8,128)}) fusion(f32[12,512,512]{1,2,0:T(8,128)} %copy-done.1, f32[12,512]{1,0:T(8,128)S(1)} %log_add_fusion, bf16[12,512,64]{1,2,0:T(8,128)(2,1)} %bitcast.240, bf16[12,512,64]{1,2,0:T(8,128)(2,1)} %bitcast.238), kind=kOutput, calls=%fused_computation.21 | convolution fusion | flops 412084224 | bytes 26787840 | tf_op jit(solution)/shard_map/htd,hsd->hts/dot_general | solution.py:310
  353.6 6.9 multiply_convert_fusion
  360.5 9.2 %broadcast_multiply_fusion = f32[12,512,768]{2,1,0:T(8,128)} fusion(bf16[12,512,512]{1,2,0:T(8,128)(2,1)S(1)} %multiply_convert_fusion, bf16[512,192]{1,0:T(8,128)(2,1)S(1)} %copy-done.76, bf16[512,192]{1,0:T(8,128)(2,1)S(1)} %copy-done.73, bf16[512,192]{1,0:T(8,128)(2,1)S(1)} %copy-done.79, bf16[512,192]{1,0:T(8,128)(2,1)S(1)} %get-tuple-element.192), kind=kOutput, calls=%fused_computation.43 | convolution fusion | flops 4839702528 | bytes 25952256 | tf_op jit(solution)/shard_map/hts,tf->hsf/dot_general | solution.py:321
  369.8 9.6 %broadcast_multiply_fusion.1 = f32[12,512,768]{2,1,0:T(8,128)} fusion(bf16[12,512,512]{1,2,0:T(8,128)(2,1)S(1)} %multiply_convert_fusion, bf16[512,192]{1,0:T(8,128)(2,1)S(1)} %copy-done.76, bf16[512,192]{1,0:T(8,128)(2,1)S(1)} %copy-done.73, bf16[512,192]{1,0:T(8,128)(2,1)S(1)} %copy-done.79, bf16[512,192]{1,0:T(8,128)(2,1)S(1)} %get-tuple-element.192), kind=kOutput, calls=%fused_computation.44 | convolution fusion | flops 4839702528 | bytes 25952256 | tf_op jit(solution)/shard_map/hts,sf->htf/dot_general | solution.py:320
  383.5 16.4 %subtract_convert_fusion.3 = (bf16[12,512,192]{2,1,0:T(8,128)(2,1)S(1)}, bf16[12,512,192]{2,1,0:T(8,128)(2,1)}, bf16[12,512,192]{2,1,0:T(8,128)(2,1)}, bf16[12,512,192]{2,1,0:T(8,128)(2,1)}) fusion(f32[12,512,768]{2,1,0:T(8,128)} %broadcast_multiply_fusion.1, f32[512,192]{1,0:T(8,128)} %copy-done.8, f32[512,192]{1,0:T(8,128)} %copy-done.6, ...), kind=kLoop, calls=%fused_computation.52 | loop fusion | flops 18874368 | bytes 29884416 | tf_op jit(solution)/shard_map/convert.12
  401.6 7.6 fusion.85
  409.3 8.0 convolution_convert_fusion.14
  417.3 15.8 %subtract_convert_fusion.1 = (bf16[12,512,192]{2,1,0:T(8,128)(2,1)}, bf16[12,512,192]{2,1,0:T(8,128)(2,1)}, bf16[12,512,192]{2,1,0:T(8,128)(2,1)}, bf16[12,512,192]{2,1,0:T(8,128)(2,1)}) fusion(f32[12,512,768]{2,1,0:T(8,128)} %broadcast_multiply_fusion, f32[512,192]{1,0:T(8,128)S(1)} %copy-done.9, f32[512,192]{1,0:T(8,128)S(1)} %copy-done.7, ...), kind=kLoop, calls=%fused_computation.48 | loop fusion | flops 18874368 | bytes 29884416 | tf_op jit(solution)/shard_map/convert.8
  433.1 8.0 fusion.84
  441.1 8.4 convolution_convert_fusion.13
  471.1 40.2 %conditional.3 = (f32[960,768]{1,0:T(8,128)}, f32[]{:T(128)}) conditional(s32[]{:T(128)} %convert_element_type.263, (f32[512]{0:T(512)S(1)}, f32[512,768]{1,0:T(8,128)S(1)}, f32[512,768]{1,0:T(8,128)}, bf16[512,1024]{1,0:T(8,128)(2,1)S(1)}, bf16[1024,960]{1,0:T(8,128)(2,1)}) %tuple.153, (s32[512]{0:T(512)S(1)}, s32[512]{0:T(512)S(1)}, ...), branch_computations={%region_22.25_spmd, %region_25.30_spmd} | conditional | flops 2318697216 | bytes 398733376 | solution.py:498
  475.4 30.3 %grads.1 = bf16[32,32,768]{2,1,0:T(8,128)(2,1)} custom-call(bf16[32,32,768]{2,1,0:T(8,128)(2,1)} %bitcast.244), custom_call_target="tpu_custom_call" | custom-call | bytes 3145728 | tf_op jit(solution)/shard_map/cond/branch_0_fun/grads/pallas_call | solution.py:144
  529.9 50.7 %all-reduce = f32[6,768]{1,0:T(8,128)S(1)} all-reduce(f32[6,768]{1,0:T(8,128)S(1)} %stack.27), channel_id=7, replica_groups=mesh['dp'=32] {'dp'}, use_global_device_ids=true, to_apply=%region_44.45.clone | all-reduce | flops 4608 | bytes 36864
  581.3 78.7 %reduce-scatter.7.cloned.1.call-done = bf16[168,768]{1,0:T(8,128)(2,1)} async-done(((bf16[5376,768]{1,0:T(8,128)(2,1)}), bf16[168,768]{1,0:T(8,128)(2,1)}) %reduce-scatter.7.cloned.1.call-update) | async-done | bytes 258064 | tf_op jit(solution)/shard_map/reduce_scatter | solution.py:507
  667.7 132.8 %reduce-scatter.9.cloned.1.call-done = bf16[192,768]{1,0:T(8,128)(2,1)} async-done(((bf16[6144,768]{1,0:T(8,128)(2,1)}), bf16[192,768]{1,0:T(8,128)(2,1)}) %reduce-scatter.9.cloned.1.call-update) | async-done | bytes 294928 | tf_op jit(solution)/shard_map/reduce_scatter | solution.py:507
  808.0 8.6 %totals.1 = f32[32,8,128]{2,1,0:T(8,128)} custom-call(f32[32,8,128]{2,1,0:T(8,128)} %broadcast_in_dim.83.src), custom_call_target="tpu_custom_call" | custom-call | bytes 262144 | tf_op jit(solution)/shard_map/totals/pallas_call | solution.py:144
  832.2 6.1 multiply_add_fusion
  (437 shorter events, 182.8 us)
Async XLA Ops:
  68.7 54.6 %copy-start.98 = (s32[8,512]{1,0:T(8,128)S(1)}, s32[8,512]{1,0:T(8,128)}, u32[]{:S(2)}) copy-start(s32[8,512]{1,0:T(8,128)} %param.40) | copy-start | bytes 49156
  68.7 54.6 %copy-start.99 = (s32[8,512]{1,0:T(8,128)S(1)}, s32[8,512]{1,0:T(8,128)}, u32[]{:S(2)}) copy-start(s32[8,512]{1,0:T(8,128)} %param.39) | copy-start | bytes 49156
  68.7 86.6 %all-gather.9.cloned.1.call-start = ((), (), s32[]{:S(2)}) async-start(), calls=%async_computation.7 | async-start | bytes 7299072 | tf_op jit(solution)/shard_map/all_gather | solution.py:417
  69.3 204.6 %all-gather.11.cloned.1.call-start = ((), (), s32[]{:S(2)}) async-start(), calls=%async_computation.8 | async-start | bytes 14192640 | tf_op jit(solution)/shard_map/all_gather | solution.py:417
  133.3 148.7 %copy-start.82 = (f32[768]{0:T(1024)}, f32[768]{0:T(1024)S(1)}, u32[]{:S(2)}) copy-start(f32[768]{0:T(1024)S(1)} %get-tuple-element.97) | copy-start | bytes 9220
  140.0 19.5 %copy-start.72 = (bf16[512,192]{1,0:T(8,128)(2,1)}, bf16[512,192]{1,0:T(8,128)(2,1)S(1)}, u32[]{:S(2)}) copy-start(bf16[512,192]{1,0:T(8,128)(2,1)S(1)} %get-tuple-element.193) | copy-start | bytes 589828
  140.0 19.5 %copy-start.75 = (bf16[512,192]{1,0:T(8,128)(2,1)}, bf16[512,192]{1,0:T(8,128)(2,1)S(1)}, u32[]{:S(2)}) copy-start(bf16[512,192]{1,0:T(8,128)(2,1)S(1)} %get-tuple-element.200) | copy-start | bytes 589828
  140.0 19.5 %copy-start.78 = (bf16[512,192]{1,0:T(8,128)(2,1)}, bf16[512,192]{1,0:T(8,128)(2,1)S(1)}, u32[]{:S(2)}) copy-start(bf16[512,192]{1,0:T(8,128)(2,1)S(1)} %get-tuple-element.201) | copy-start | bytes 589828
  140.0 71.0 %copy-start.6 = (f32[512,192]{1,0:T(8,128)}, f32[512,192]{1,0:T(8,128)S(1)}, u32[]{:S(2)}) copy-start(f32[512,192]{1,0:T(8,128)S(1)} %get-tuple-element.191) | copy-start | bytes 1179652
  140.0 71.0 %copy-start.8 = (f32[512,192]{1,0:T(8,128)}, f32[512,192]{1,0:T(8,128)S(1)}, u32[]{:S(2)}) copy-start(f32[512,192]{1,0:T(8,128)S(1)} %get-tuple-element.194) | copy-start | bytes 1179652
  140.0 71.0 %copy-start.10 = (f32[512,192]{1,0:T(8,128)}, f32[512,192]{1,0:T(8,128)S(1)}, u32[]{:S(2)}) copy-start(f32[512,192]{1,0:T(8,128)S(1)} %get-tuple-element.199) | copy-start | bytes 1179652
  140.1 71.0 %copy-start.12 = (f32[512,192]{1,0:T(8,128)}, f32[512,192]{1,0:T(8,128)S(1)}, u32[]{:S(2)}) copy-start(f32[512,192]{1,0:T(8,128)S(1)} %get-tuple-element.202) | copy-start | bytes 1179652
  160.5 121.4 %copy-start.84 = (f32[512]{0:T(512)}, f32[512]{0:T(512)S(1)}, u32[]{:S(2)}) copy-start(f32[512]{0:T(512)S(1)} %broadcast_multiply_fusion.10) | copy-start | bytes 6148
  160.8 121.1 %copy-start.91 = (f32[512]{0:T(512)}, f32[512]{0:T(512)S(1)}, u32[]{:S(2)}) copy-start(f32[512]{0:T(512)S(1)} %add_rsqrt_fusion.2) | copy-start | bytes 6148
  165.7 13.3 %copy-start.14 = (bf16[512,768]{0,1:T(8,128)(2,1)}, bf16[512,768]{0,1:T(8,128)(2,1)S(1)}, u32[]{:S(2)}) copy-start(bf16[512,768]{0,1:T(8,128)(2,1)S(1)} %copy.99) | copy-start | bytes 2359300
  229.0 13.2 %copy-start.28 = (bf16[12,512,192]{2,1,0:T(8,128)(2,1)S(1)}, bf16[12,512,192]{2,1,0:T(8,128)(2,1)}, u32[]{:S(2)}) copy-start(bf16[12,512,192]{2,1,0:T(8,128)(2,1)} %get-tuple-element.152) | copy-start | bytes 7077892
  283.9 20.3 %copy-start.56 = (bf16[512,768]{1,0:T(8,128)(2,1)}, bf16[512,768]{1,0:T(8,128)(2,1)S(1)}, u32[]{:S(2)}) copy-start(bf16[512,768]{1,0:T(8,128)(2,1)S(1)} %fusion.71) | copy-start | bytes 2359300
  292.9 20.4 %copy-start.110 = (bf16[512,768]{1,0:T(8,128)(2,1)}, bf16[512,768]{1,0:T(8,128)(2,1)S(1)}, u32[]{:S(2)}) copy-start(bf16[512,768]{1,0:T(8,128)(2,1)S(1)} %get-tuple-element.130) | copy-start | bytes 2359300
  298.8 15.4 %copy-start.112 = (bf16[512,768]{1,0:T(8,128)(2,1)}, bf16[512,768]{1,0:T(8,128)(2,1)S(1)}, u32[]{:S(2)}) copy-start(bf16[512,768]{1,0:T(8,128)(2,1)S(1)} %get-tuple-element.132) | copy-start | bytes 2359300
  341.3 12.2 %slice-start.2 = ((s8[12582912]{0:T(1024)(128)(4,1)}), s8[4194304]{0:T(1024)(128)(4,1)S(1)}, s32[]{:S(2)}) async-start(s8[12582912]{0:T(1024)(128)(4,1)} %bitcast.220), calls=%async_computation.11 | async-start | bytes 8388608
  383.5 18.1 %copy-start.26 = (bf16[16,48,768]{2,1,0:T(8,128)(2,1)S(1)}, bf16[16,48,768]{2,1,0:T(8,128)(2,1)}, u32[]{:S(2)}) copy-start(bf16[16,48,768]{2,1,0:T(8,128)(2,1)} %copy-done.25) | copy-start | bytes 3538948
  417.3 15.8 %copy-start.24 = (bf16[16,48,768]{2,1,0:T(8,128)(2,1)S(1)}, bf16[16,48,768]{2,1,0:T(8,128)(2,1)}, u32[]{:S(2)}) copy-start(bf16[16,48,768]{2,1,0:T(8,128)(2,1)} %copy-done.23) | copy-start | bytes 3538948
  417.3 33.1 %slice-start.3 = ((s8[6291456]{0:T(1024)(128)(4,1)}), s8[2097152]{0:T(1024)(128)(4,1)S(1)}, s32[]{:S(2)}) async-start(s8[6291456]{0:T(1024)(128)(4,1)} %bitcast.222), calls=%async_computation.12 | async-start | bytes 4194304
  433.1 17.3 %slice-start.4 = ((s8[6291456]{0:T(1024)(128)(4,1)}), s8[4194304]{0:T(1024)(128)(4,1)S(1)}, s32[]{:S(2)}) async-start(s8[6291456]{0:T(1024)(128)(4,1)} %bitcast.222), calls=%async_computation.13 | async-start | bytes 8388608
  475.4 30.3 %copy-start.40 = (bf16[1024,960]{1,0:T(8,128)(2,1)S(1)}, bf16[1024,960]{1,0:T(8,128)(2,1)}, u32[]{:S(2)}) copy-start(bf16[1024,960]{1,0:T(8,128)(2,1)} %get-tuple-element.35) | copy-start | bytes 5898244 | tf_op jit(solution)/shard_map/cond
  511.3 148.7 %reduce-scatter.7.cloned.1.call-start = ((), (), s32[]{:S(2)}) async-start(), calls=%async_computation.5 | async-start | bytes 8515584 | tf_op jit(solution)/shard_map/reduce_scatter | solution.py:507
  511.8 288.6 %reduce-scatter.9.cloned.1.call-start = ((), (), s32[]{:S(2)}) async-start(), calls=%async_computation.6 | async-start | bytes 9732096 | tf_op jit(solution)/shard_map/reduce_scatter | solution.py:507
  580.6 220.9 %copy-start.89 = (f32[6,768]{1,0:T(8,128)}, f32[6,768]{1,0:T(8,128)S(1)}, u32[]{:S(2)}) copy-start(f32[6,768]{1,0:T(8,128)S(1)} %all-reduce) | copy-start | bytes 55300
  662.9 155.9 %copy-start.101 = (f32[6,24]{1,0:T(8,128)S(1)}, f32[6,24]{1,0:T(8,128)}, u32[]{:S(2)}) copy-start(f32[6,24]{1,0:T(8,128)} %param.49) | copy-start | bytes 1732
  662.9 155.9 %copy-start.108 = (f32[6,24]{1,0:T(8,128)S(1)}, f32[6,24]{1,0:T(8,128)}, u32[]{:S(2)}) copy-start(f32[6,24]{1,0:T(8,128)} %param.65) | copy-start | bytes 1732
  662.9 155.9 %copy-start.109 = (f32[6,24]{1,0:T(8,128)S(1)}, f32[6,24]{1,0:T(8,128)}, u32[]{:S(2)}) copy-start(f32[6,24]{1,0:T(8,128)} %param.57) | copy-start | bytes 1732
  803.0 29.2 %copy-start.38 = (f32[960,768]{1,0:T(8,128)S(1)}, f32[960,768]{1,0:T(8,128)}, u32[]{:S(2)}) copy-start(f32[960,768]{1,0:T(8,128)} %param.50) | copy-start | bytes 8847364
  (103 other events, 353.4 us)
Sparse Core Ops, SparseCore 1:
  73.1 82.2 all-gather.8
  158.6 99.6 all-gather.10
  518.6 141.3 reduce-scatter.6
  665.9 134.5 reduce-scatter.8

commit v2 on v1

v2 whole, which is shorter than its diff:
```python
from functools import partial

import jax
import jax.numpy as jnp
from jax import lax
from jax.experimental import pallas as pl
from jax.experimental.pallas import tpu as pltpu
from jax.sharding import PartitionSpec as P

HD = 64
DOCS = 8
STEP = 10
MESH = pl.DeviceIdType.MESH

mask_token = 103
ln_epsilon = 1e-06
momentum_decay = 0.9
learn_rate = 5000.0
table_rate = 1000000.0
clip_limit = 0.01
average_cap = 0.999


def sinusoids(positions, count):
    ranks = jnp.arange(count).astype(jnp.float32)
    omegas = jnp.power(10000.0, -ranks / count)
    angle_x = positions[0].astype(jnp.float32)[:, None] * omegas[None, :]
    angle_y = positions[1].astype(jnp.float32)[:, None] * omegas[None, :]
    return (jnp.sin(angle_x), jnp.cos(angle_x), jnp.sin(angle_y), jnp.cos(angle_y))


def layer_norm(rows, gain, bias):
    centred = rows - jnp.mean(rows, -1, keepdims=True)
    rescale = lax.rsqrt(jnp.mean(centred * centred, -1, keepdims=True) + ln_epsilon)
    whitened = centred * rescale
    return (whitened * gain + bias, whitened, rescale)


def norm_back(upstream, whitened, rescale, gain):
    scaled = upstream * gain
    inner = (
        scaled
        - jnp.mean(scaled, -1, keepdims=True)
        - whitened * jnp.mean(scaled * whitened, -1, keepdims=True)
    )
    return (rescale * inner, jnp.sum(upstream * whitened, 0), jnp.sum(upstream, 0))


def dot_nn(left, right):
    return lax.dot_general(
        left, right, (((1,), (0,)), ((), ())), preferred_element_type=jnp.float32
    )


def dot_tn(left, right):
    return lax.dot_general(
        left, right, (((0,), (0,)), ((), ())), preferred_element_type=jnp.float32
    )


def dot_nt(left, right):
    return lax.dot_general(
        left, right, (((1,), (1,)), ((), ())), preferred_element_type=jnp.float32
    )


def exchange_kernel(n, count, *refs):
    srcs, dsts = refs[:count], refs[count : 2 * count]
    send_sem, recv_sem, own_sem = refs[2 * count :]
    me = lax.axis_index("dp")
    barrier = pltpu.get_barrier_semaphore()

    def greet(step, carry):
        pl.semaphore_signal(
            barrier, inc=1, device_id=(lax.rem(me + step, n),), device_id_type=MESH
        )
        return carry

    lax.fori_loop(1, n, greet, 0)
    for k in range(count):
        pltpu.make_async_copy(srcs[k].at[me], dsts[k].at[me], own_sem.at[k]).start()
    pl.semaphore_wait(barrier, n - 1)

    def copy(k, step):
        peer = lax.rem(me + step, n)
        return pltpu.make_async_remote_copy(
            src_ref=srcs[k].at[peer],
            dst_ref=dsts[k].at[me],
            send_sem=send_sem.at[k, step],
            recv_sem=recv_sem.at[k, step],
            device_id=(peer,),
            device_id_type=MESH,
        )

    def start(step, carry):
        for k in range(count):
            copy(k, step).start()
        return carry

    def finish(step, carry):
        for k in range(count):
            copy(k, step).wait()
        return carry

    lax.fori_loop(1, n, start, 0)
    lax.fori_loop(1, n, finish, 0)
    for k in range(count):
        pltpu.make_async_copy(srcs[k].at[me], dsts[k].at[me], own_sem.at[k]).wait()


def exchange(arrays, ident, name):
    count, n = len(arrays), arrays[0].shape[0]
    anywhere = pl.BlockSpec(memory_space=pl.ANY)
    return pl.pallas_call(
        partial(exchange_kernel, n, count),
        name=name,
        out_shape=tuple(jax.ShapeDtypeStruct(rows.shape, rows.dtype) for rows in arrays),
        in_specs=[anywhere] * count,
        out_specs=(anywhere,) * count,
        scratch_shapes=[
            pltpu.SemaphoreType.DMA((count, n)),
            pltpu.SemaphoreType.DMA((count, n)),
            pltpu.SemaphoreType.DMA((count,)),
        ],
        compiler_params=pltpu.CompilerParams(collective_id=ident, has_side_effects=True),
        cost_estimate=pl.CostEstimate(
            flops=0, bytes_accessed=2 * 2**20, transcendentals=0
        ),
    )(*arrays)


def plan_kernel(
    n, rows_own, capacity, fold, tok_col, tok_row, mask_row, own, info, lists, place
):
    size = tok_col.shape[0]
    ids_col = tok_col[...]
    ids_row = tok_row[...]
    owner_col = lax.div(ids_col, rows_own)
    owner_row = lax.div(ids_row, rows_own)
    at_col = lax.broadcasted_iota(jnp.int32, (size, size), 0)
    at_row = lax.broadcasted_iota(jnp.int32, (size, size), 1)
    same = ids_col == ids_row
    first_col = jnp.min(jnp.where(same, at_row, size), 1, keepdims=True)
    first_row = jnp.min(jnp.where(same, at_col, size), 0, keepdims=True)
    leads_row = first_row == lax.broadcasted_iota(jnp.int32, (1, size), 1)
    leads_col = first_col == lax.broadcasted_iota(jnp.int32, (size, 1), 0)
    ahead = (owner_col == owner_row) & leads_row & (at_row < first_col)
    slot = jnp.sum(jnp.where(ahead, 1.0, 0.0), 1, keepdims=True).astype(jnp.int32)
    fits = slot < capacity - 1
    place[...] = jnp.where(fits, owner_col * capacity + slot, -1)
    over = jnp.max(jnp.where(fits, 0.0, 1.0), keepdims=True)
    local = ids_col - owner_col * rows_own + 1
    high = lax.div(local, 128)
    to_owner = lax.broadcasted_iota(jnp.int32, (size, n), 1) == owner_col
    to_owner = to_owner & leads_col & fits
    shift = capacity * lax.rem(own[1], fold)
    in_slot = lax.broadcasted_iota(jnp.int32, (size, 128), 1) == slot + shift
    in_slot = jnp.where(in_slot, 1.0, 0.0).astype(jnp.bfloat16)
    high_part = jnp.where(to_owner, high.astype(jnp.float32), 0.0).astype(jnp.bfloat16)
    low_part = jnp.where(to_owner, (local - high * 128).astype(jnp.float32), 0.0)
    table = dot_tn(high_part, in_slot) * 128.0 + dot_tn(low_part.astype(jnp.bfloat16), in_slot)
    lane = lax.broadcasted_iota(jnp.int32, (n, 128), 1)
    line = lax.broadcasted_iota(jnp.int32, (n, 128), 0)
    fixed = (line == mask_token // rows_own) & (lane == capacity - 1 + shift)
    table = jnp.where(fixed, float(mask_token % rows_own + 1), table)
    count = jnp.sum(mask_row[...].astype(jnp.float32), keepdims=True)
    lane = lax.broadcasted_iota(jnp.int32, (8, 128), 1)
    line = lax.broadcasted_iota(jnp.int32, (8, 128), 0)
    extra = jnp.where(lane == 0, count, jnp.where(lane == 1, own[0].astype(jnp.float32), over))
    extra = jnp.where(line == 7, extra, info[...])
    line = lax.broadcasted_iota(jnp.int32, lists.shape, 1)
    lists[...] = jnp.where(line == 0, table[:, None, :], extra[None])


def make_plan(tokens, masking, documents, info, n, rows_own, capacity, fold):
    size = tokens.shape[0]
    vmem = pl.BlockSpec(memory_space=pltpu.VMEM)
    return pl.pallas_call(
        partial(plan_kernel, n, rows_own, capacity, fold),
        name="plan",
        out_shape=(
            jax.ShapeDtypeStruct((n, 8, 128), jnp.float32),
            jax.ShapeDtypeStruct((size, 1), jnp.int32),
        ),
        in_specs=[vmem, vmem, vmem, pl.BlockSpec(memory_space=pltpu.SMEM), vmem],
        out_specs=(vmem, vmem),
        compiler_params=pltpu.CompilerParams(vmem_limit_bytes=32 * 2**20),
    )(
        tokens[:, None],
        tokens[None, :],
        masking[None, :],
        jnp.stack([documents[0], lax.axis_index("dp")]),
        info,
    )


def place_of(me):
    core = lax.rem(me, 2)
    chip = lax.div(me, 2)
    spot = lax.rem(chip, 4)
    layer = lax.div(chip, 4)
    along_a = 1 + core
    along_b = 2 - core
    step_a = along_a * (1 - 2 * lax.rem(lax.div(spot, along_a), 2))
    step_b = along_b * (1 - 2 * lax.rem(lax.div(spot, along_b), 2))
    return core, spot, layer, step_a, step_b


def remote_copy(src, dst, send, recv, device):
    return pltpu.make_async_remote_copy(
        src_ref=src, dst_ref=dst, send_sem=send, recv_sem=recv, device_id=(device,), device_id_type=MESH
    )


def greet_everyone(me, n):
    barrier = pltpu.get_barrier_semaphore()

    def greet(step, carry):
        pl.semaphore_signal(
            barrier, inc=1, device_id=(lax.rem(me + step, n),), device_id_type=MESH
        )
        return carry

    lax.fori_loop(1, n, greet, 0)
    pl.semaphore_wait(barrier, n - 1)


def front_kernel(n, units, capacity, *refs):
    count = len(units)
    lists, vocabulary, pages = refs[:3]
    weights = refs[3 : 3 + count]
    asked, rows, full = refs[3 + count : 6 + count]
    swap_out, swap_in, chip_rows, answers = refs[6 + count : 10 + count]
    ask_send, ask_recv, row_send, row_recv, own_sem, swap_send, swap_recv = refs[10 + count : 17 + count]
    hop_recv, core_recv, core_send, z_send, a_send, b_send = refs[17 + count :]
    me = lax.axis_index("dp")
    core, spot, layer, step_a, step_b = place_of(me)
    layers = n // 8
    half = chip_rows.shape[1]
    page_rows = pages.shape[0]
    here = pl.ds(pl.multiple_of(core * half, 128), half)
    there = pl.ds(pl.multiple_of((1 - core) * half, 128), half)
    partner = me + 1 - 2 * core
    to_a, to_b, up, down = me + 2 * step_a, me + 2 * step_b, me + 8, me - 8
    spot_a, spot_b, spot_ab = spot + step_a, spot + step_b, spot + step_a + step_b

    at = 0
    for ref, unit in zip(weights, units):
        swap_out[pl.ds(at, 24 * unit)] = ref[:, there]
        at += 24 * unit
    greet_everyone(me, n)
    swaps = [
        remote_copy(swap_out, swap_in, swap_send.at[0], swap_recv.at[0], partner),
        remote_copy(
            pages.at[:, there],
            chip_rows.at[pl.ds(2 * at + core * page_rows, page_rows)],
            swap_send.at[1],
            swap_recv.at[1],
            partner,
        ),
    ]
    for copy in swaps:
        copy.start()

    def ask(step):
        peer = lax.rem(me + step, n)
        return remote_copy(lists.at[peer], asked.at[me], ask_send.at[step], ask_recv.at[step], peer)

    def start_ask(step, carry):
        ask(step).start()
        return carry

    def wait_ask(step, carry):
        ask(step).wait()
        return carry

    lax.fori_loop(1, n, start_ask, 0)
    asked[me] = lists[me]
    chip_rows[pl.ds(2 * at + pl.multiple_of(core * page_rows, page_rows), page_rows)] = pages[:, here]
    for copy in swaps:
        copy.wait_recv()
    at = 0
    for ref, unit in zip(weights, units):
        mine, other = ref[:, here], swap_in[pl.ds(at, 24 * unit)]
        ordered = jnp.where(
            core == 0, jnp.concatenate([mine, other], 0), jnp.concatenate([other, mine], 0)
        )
        chip_rows[pl.ds(2 * at, 48 * unit)] = ordered.astype(chip_rows.dtype)
        at += 24 * unit

    def block(level, index):
        return full.at[level, index, :, here]

    def z_hop(way, level, src=None):
        return remote_copy(
            block(level, spot) if src is None else src, block(level, spot),
            z_send.at[way, level], hop_recv.at[level, spot], up if way == 0 else down,
        )

    def a_hop(level, src=None):
        return remote_copy(
            block(level, spot) if src is None else src, block(level, spot),
            a_send.at[level], hop_recv.at[level, spot], to_a,
        )

    def b_hop(kind, level, src=None):
        index = spot if kind == 0 else spot_a
        return remote_copy(
            block(level, index) if src is None else src, block(level, index),
            b_send.at[kind, level], hop_recv.at[level, index], to_b,
        )

    def core_hop(level, index, src=None):
        return remote_copy(
            block(level, index) if src is None else src, block(level, index),
            core_send.at[level, index], core_recv.at[level, index], partner,
        )

    def arrived(level, index):
        pltpu.make_async_copy(block(level, index), block(level, index), hop_recv.at[level, index]).wait()

    low_z, high_z = layer > 0, layer < layers - 1

    @pl.when(high_z)
    def _():
        z_hop(0, layer, chip_rows).start()

    @pl.when(low_z)
    def _():
        z_hop(1, layer, chip_rows).start()

    a_hop(layer, chip_rows).start()
    b_hop(0, layer, chip_rows).start()
    core_hop(layer, spot, chip_rows).start()
    own = pltpu.make_async_copy(chip_rows, block(layer, spot), own_sem.at[0])
    own.start()

    lax.fori_loop(1, n, wait_ask, 0)
    rows_own = vocabulary.shape[0]
    table = vocabulary[...].astype(jnp.bfloat16)
    group = 128 // capacity

    def row_copy(peer):
        return remote_copy(
            answers.at[peer], rows.at[me], row_send.at[peer], row_recv.at[me], peer
        )

    def answer(turn, carry):
        ids = jnp.zeros((8, 128), jnp.float32)
        for k in range(group):
            ids = ids + asked[turn * group + k]
        ids = ids.T[:, 0:1]
        wanted = lax.broadcasted_iota(jnp.int32, (128, rows_own), 1) + 1
        picks = jnp.where(ids.astype(jnp.int32) == wanted, 1.0, 0.0).astype(jnp.bfloat16)
        found = dot_nn(picks, table).astype(jnp.bfloat16)
        for k in range(group):
            peer = turn * group + k
            answers[peer] = found[k * capacity : (k + 1) * capacity]

            @pl.when(peer != me)
            def _():
                row_copy(peer).start()

        return carry

    lax.fori_loop(0, n // group, answer, 0)
    own_rows = pltpu.make_async_copy(answers.at[me], rows.at[me], own_sem.at[1])
    own_rows.start()

    def relay_column(gap):
        for way, level, there_is, further in (
            (0, layer - gap, layer - gap >= 0, high_z),
            (1, layer + gap, layer + gap < layers, low_z),
        ):

            @pl.when(there_is)
            def _():
                arrived(level, spot)

                @pl.when(further)
                def _():
                    z_hop(way, level).start()

                a_hop(level).start()
                b_hop(0, level).start()
                core_hop(level, spot).start()

    def at_gap(gap, visit):
        if gap == 0:
            visit(layer)
            return

        @pl.when(layer - gap >= 0)
        def _():
            visit(layer - gap)

        @pl.when(layer + gap < layers)
        def _():
            visit(layer + gap)

    def relay_a(level):
        arrived(level, spot_a)
        b_hop(1, level).start()
        core_hop(level, spot_a).start()

    def relay_b(index):
        def visit(level):
            arrived(level, index)
            core_hop(level, index).start()

        return visit

    for gap in range(layers):
        if gap > 0:
            relay_column(gap)
        at_gap(gap, relay_a)
        if gap > 0:
            at_gap(gap - 1, relay_b(spot_b))
            at_gap(gap - 1, relay_b(spot_ab))
    at_gap(layers - 1, relay_b(spot_b))
    at_gap(layers - 1, relay_b(spot_ab))

    def finish(level, carry):
        for index in (spot, spot_a, spot_b, spot_ab):
            core_hop(level, index).wait_send()
        for index in range(4):
            other = full.at[level, index, :, there]
            pltpu.make_async_copy(other, other, core_recv.at[level, index]).wait()
        a_hop(level).wait_send()
        b_hop(0, level).wait_send()
        b_hop(1, level).wait_send()

        @pl.when((level <= layer) & high_z)
        def _():
            z_hop(0, level).wait_send()

        @pl.when((level >= layer) & low_z)
        def _():
            z_hop(1, level).wait_send()

        return carry

    lax.fori_loop(0, layers, finish, 0)
    own.wait()
    own_rows.wait()
    for copy in swaps:
        copy.wait_send()

    def finish_rows(step, carry):
        peer = lax.rem(me + step, n)
        pltpu.make_async_copy(answers.at[peer], answers.at[peer], row_send.at[peer]).wait()
        source = lax.rem(me - step + n, n)
        pltpu.make_async_copy(rows.at[source], rows.at[source], row_recv.at[source]).wait()
        return carry

    lax.fori_loop(1, n, finish_rows, 0)


def front(lists, vocabulary, pages, weights, n, capacity, ident):
    model = vocabulary.shape[1]
    layers = n // 8
    units = [weight.shape[0] // 24 for weight in weights]
    swap = 24 * sum(units)
    chip = 2 * (swap + pages.shape[0])
    low = jnp.bfloat16
    dma = pltpu.SemaphoreType.DMA
    vmem = pl.BlockSpec(memory_space=pltpu.VMEM)
    anywhere = pl.BlockSpec(memory_space=pl.ANY)
    return pl.pallas_call(
        partial(front_kernel, n, units, capacity),
        name="front",
        out_shape=(
            jax.ShapeDtypeStruct(lists.shape, lists.dtype),
            jax.ShapeDtypeStruct((n, capacity, model), low),
            jax.ShapeDtypeStruct((layers, 4, chip, model), low),
        ),
        in_specs=[vmem] * (3 + len(weights)),
        out_specs=(vmem, anywhere, anywhere),
        scratch_shapes=[
            pltpu.VMEM((swap, model // 2), jnp.float32),
            pltpu.VMEM((swap, model // 2), jnp.float32),
            pltpu.VMEM((chip, model // 2), low),
            pltpu.VMEM((n, capacity, model), low),
            dma((n,)),
            dma((n,)),
            dma((n,)),
            dma((n,)),
            dma((2,)),
            dma((2,)),
            dma((2,)),
            dma((layers, 4)),
            dma((layers, 4)),
            dma((layers, 4)),
            dma((2, layers)),
            dma((layers,)),
            dma((2, layers)),
        ],
        compiler_params=pltpu.CompilerParams(
            collective_id=ident, has_side_effects=True, vmem_limit_bytes=48 * 2**20
        ),
        cost_estimate=pl.CostEstimate(
            flops=0, bytes_accessed=100 * 2**20, transcendentals=0
        ),
    )(lists, vocabulary, pages, *weights)


def back_kernel(n, units, chunks, *refs):
    count = len(units)
    sent, small, grads = refs[0], refs[1], refs[2 : 2 + count]
    came, small_came, out = refs[2 + count : 5 + count]
    own, par, from_b, from_a, from_z, mine, gone, back = refs[5 + count : 13 + count]
    row_send, row_recv, own_sem, load_sem, pair_send, pair_recv = refs[13 + count : 19 + count]
    b_send, b_recv, a_send, a_recv, z_send, z_recv, f_send, f_recv = refs[19 + count :]
    layers = n // 8
    me = lax.axis_index("dp")
    core, spot, layer, step_a, step_b = place_of(me)
    half = own.shape[3]
    here = pl.ds(pl.multiple_of(core * half, 128), half)
    there = pl.ds(pl.multiple_of((1 - core) * half, 128), half)
    partner = me + 1 - 2 * core
    to_a, to_b = me + 2 * step_a, me + 2 * step_b
    offsets = [48 * sum(units[:k]) for k in range(count)]
    spot_a, spot_b, spot_ab = spot + step_a, spot + step_b, spot + step_a + step_b
    size = own.shape[2] // chunks

    greet_everyone(me, n)
    for index in (spot_ab, spot_a, spot_b, spot):
        for ref, at, unit in zip(grads, offsets, units):
            remote_copy(
                ref.at[:, index, :, there],
                par.at[:, index, pl.ds(at, 48 * unit)],
                pair_send.at[index],
                pair_recv.at[index],
                partner,
            ).start()
    for index in (spot_ab, spot_b, spot_a, spot):
        for ref, at, unit in zip(grads, offsets, units):
            pltpu.make_async_copy(
                ref.at[:, index, :, here], own.at[:, index, pl.ds(at, 48 * unit)], load_sem.at[index]
            ).start()

    def row_copies(step):
        peer = lax.rem(me + step, n)
        return [
            remote_copy(src.at[peer], dst.at[me], row_send.at[k, step], row_recv.at[k, step], peer)
            for k, (src, dst) in enumerate(((sent, came), (small, small_came)))
        ]

    def start_rows(step, carry):
        for copy in row_copies(step):
            copy.start()
        return carry

    def finish_rows(step, carry):
        for copy in row_copies(step):
            copy.wait()
        return carry

    lax.fori_loop(1, n, start_rows, 0)
    own_copies = [
        pltpu.make_async_copy(src.at[me], dst.at[me], own_sem.at[k])
        for k, (src, dst) in enumerate(((sent, came), (small, small_came)))
    ]
    for copy in own_copies:
        copy.start()

    def arrived(index):
        pltpu.make_async_copy(own.at[:, index], own.at[:, index], load_sem.at[index]).wait()
        pltpu.make_async_copy(par.at[:, index], par.at[:, index], pair_recv.at[index]).wait()

    def total(*parts):
        return sum(part[...].astype(jnp.float32) for part in parts)

    def b_copy(kind, level, part):
        cut = pl.ds(part * size, size)
        return remote_copy(
            own.at[level, spot_ab if kind == 0 else spot_b, cut], from_b.at[kind, level, cut],
            b_send.at[kind, level, part], b_recv.at[kind, level, part], to_b,
        )

    def a_copy(level, part):
        cut = pl.ds(part * size, size)
        return remote_copy(
            own.at[level, spot_a, cut], from_a.at[level, cut],
            a_send.at[level, part], a_recv.at[level, part], to_a,
        )

    def z_copy(level, part):
        cut = pl.ds(part * size, size)
        return remote_copy(
            own.at[level, spot, cut], from_z.at[layer, cut],
            z_send.at[level, part], z_recv.at[layer, part], me + 8 * (level - layer),
        )

    def cross_b(kind, index, part):
        cut = pl.ds(part * size, size)

        def step(level, carry):
            own[level, index, cut] = total(
                own.at[level, index, cut], par.at[level, index, cut]
            ).astype(own.dtype)
            b_copy(kind, level, part).start()
            return carry

        lax.fori_loop(0, layers, step, 0)

    def cross_a(part):
        cut = pl.ds(part * size, size)

        def step(level, carry):
            b_copy(0, level, part).wait_recv()
            own[level, spot_a, cut] = total(
                own.at[level, spot_a, cut], par.at[level, spot_a, cut], from_b.at[0, level, cut]
            ).astype(own.dtype)
            a_copy(level, part).start()
            return carry

        lax.fori_loop(0, layers, step, 0)

    def column(level, part):
        cut = pl.ds(part * size, size)
        b_copy(1, level, part).wait_recv()
        a_copy(level, part).wait_recv()
        return total(
            own.at[level, spot, cut], par.at[level, spot, cut],
            from_b.at[1, level, cut], from_a.at[level, cut],
        )

    def cross_z(part):
        cut = pl.ds(part * size, size)

        def step(gap, carry):
            level = lax.rem(layer + gap, layers)
            own[level, spot, cut] = column(level, part).astype(own.dtype)
            z_copy(level, part).start()
            return carry

        lax.fori_loop(1, layers, step, 0)
        mine[cut] = column(layer, part)

    arrived(spot_ab)
    cross_b(0, spot_ab, 0)
    arrived(spot_b)
    for part in range(chunks):
        if part > 0:
            cross_b(0, spot_ab, part)
        cross_b(1, spot_b, part)
    arrived(spot_a)
    arrived(spot)
    for part in range(chunks):
        cross_a(part)
        if part > 0:
            cross_z(part - 1)
    cross_z(chunks - 1)
    for part in range(chunks):
        cut = pl.ds(part * size, size)

        def step(gap, carry):
            level = lax.rem(layer + gap, layers)
            remote_copy(
                own.at[level, spot, cut], from_z.at[level, cut],
                z_send.at[level, part], z_recv.at[level, part], me,
            ).wait_recv()
            mine[cut] += total(from_z.at[level, cut])
            return carry

        lax.fori_loop(1, layers, step, 0)

    at = 0
    for offset, unit in zip(offsets, units):
        rows = 24 * unit
        gone[pl.ds(at, rows)] = mine[pl.ds(pl.multiple_of(offset + (1 - core) * rows, 8), rows)]
        out[pl.ds(at, rows), here] = mine[pl.ds(pl.multiple_of(offset + core * rows, 8), rows)]
        at += rows
    last = remote_copy(gone, back, f_send, f_recv, partner)
    last.start()
    last.wait()
    out[:, there] = back[...]
    for index in range(4):
        pltpu.make_async_copy(par.at[:, index], par.at[:, index], pair_send.at[index]).wait()

    def settle(level, carry):
        for part in range(chunks):
            b_copy(0, level, part).wait_send()
            b_copy(1, level, part).wait_send()
            a_copy(level, part).wait_send()

            @pl.when(level != layer)
            def _():
                z_copy(level, part).wait_send()

        return carry

    lax.fori_loop(0, layers, settle, 0)
    lax.fori_loop(1, n, finish_rows, 0)
    for copy in own_copies:
        copy.wait()


def to_owners(sent, small, grads, n, ident):
    model = grads[0].shape[1]
    layers = n // 8
    units = [grad.shape[0] // n // 24 for grad in grads]
    chunks = max(k for k in range(1, 6) if sum(units) % k == 0)
    rows = 48 * sum(units)
    half = model // 2
    low = jnp.bfloat16
    dma = pltpu.SemaphoreType.DMA
    anywhere = pl.BlockSpec(memory_space=pl.ANY)
    return pl.pallas_call(
        partial(back_kernel, n, units, chunks),
        name="back",
        out_shape=(
            jax.ShapeDtypeStruct(sent.shape, sent.dtype),
            jax.ShapeDtypeStruct(small.shape, small.dtype),
            jax.ShapeDtypeStruct((rows // 2, model), jnp.float32),
        ),
        in_specs=[anywhere] * (2 + len(grads)),
        out_specs=(anywhere, anywhere, pl.BlockSpec(memory_space=pltpu.VMEM)),
        scratch_shapes=[
            pltpu.VMEM((layers, 4, rows, half), low),
            pltpu.VMEM((layers, 4, rows, half), low),
            pltpu.VMEM((2, layers, rows, half), low),
            pltpu.VMEM((layers, rows, half), low),
            pltpu.VMEM((layers, rows, half), low),
            pltpu.VMEM((rows, half), jnp.float32),
            pltpu.VMEM((rows // 2, half), jnp.float32),
            pltpu.VMEM((rows // 2, half), jnp.float32),
            dma((2, n)),
            dma((2, n)),
            dma((2,)),
            dma((4,)),
            dma((4,)),
            dma((4,)),
            dma((2, layers, chunks)),
            dma((2, layers, chunks)),
            dma((layers, chunks)),
            dma((layers, chunks)),
            dma((layers, chunks)),
            dma((layers, chunks)),
            dma,
            dma,
        ],
        compiler_params=pltpu.CompilerParams(
            collective_id=ident, has_side_effects=True, vmem_limit_bytes=60 * 2**20
        ),
        cost_estimate=pl.CostEstimate(
            flops=0, bytes_accessed=100 * 2**20, transcendentals=0
        ),
    )(sent, small, *[grad.reshape(layers, 4, -1, model) for grad in grads])


def split_rows(packed, grads, n):
    out, at = [], 0
    for grad in grads:
        count = grad.shape[0] // n
        out.append(packed[at : at + count])
        at += count
    return out


def scatter(grads, n):
    model = grads[0].shape[1]
    joined = jnp.concatenate([grad.reshape(n, -1, model) for grad in grads], 1)
    joined = joined.reshape(-1, model)
    mine = lax.psum_scatter(joined, "dp", scatter_dimension=0, tiled=True)
    return split_rows(mine.astype(jnp.float32), grads, n)


def masked(rows, half):
    lane = lax.broadcasted_iota(jnp.int32, rows.shape, 1)
    keep = (lane < HD) if half == 0 else (lane >= HD)
    return jnp.where(keep, rows, jnp.zeros_like(rows))


def turn(terms, sines, cosines):
    half = sines.shape[1]
    sine, cosine = terms[:, :half], terms[:, half:]
    return jnp.concatenate(
        [sine * sines + cosine * cosines, cosine * sines - sine * cosines], 1
    ).astype(jnp.bfloat16)


def turn_back(upstream, sines, cosines):
    half = sines.shape[1]
    first, second = upstream[:, :half], upstream[:, half:]
    return jnp.concatenate(
        [first * sines - second * cosines, first * cosines + second * sines], 1
    ).astype(jnp.bfloat16)


def pick_halves(low_half, high_half):
    lane = lax.broadcasted_iota(jnp.int32, low_half.shape, 1)
    return jnp.where(lane < HD, low_half, high_half)


def attend_kernel(q, k, v, rel_text, rel_box, sines, cosines, bases, attended, probs):
    queries, keys, values = q[...], k[...], v[...]
    spread = bases[...]
    results = []
    for half in range(2):
        mine = masked(queries, half)
        terms = dot_nn(masked(keys, half), rel_box[...])
        box_rot = turn(terms, sines[...], cosines[...])
        terms = dot_nn(mine, rel_text[...])
        text_rot = turn(terms, sines[...], cosines[...])
        scores = dot_nt(mine, keys) + dot_nt(text_rot, spread) + dot_nt(spread, box_rot)
        scores = scores * HD ** (-0.5)
        powers = jnp.exp(scores - jnp.max(scores, -1, keepdims=True))
        shares = powers * (1.0 / jnp.sum(powers, -1, keepdims=True))
        probs[half] = shares
        results.append(dot_nn(shares.astype(jnp.bfloat16), values))
    attended[...] = pick_halves(*results).astype(jnp.bfloat16)


def attend(joined, rel_map, sines, cosines, bases):
    size, model = bases.shape
    pairs = model // (2 * HD)
    lanes = 2 * HD
    whole = lambda rows: pl.BlockSpec(rows.shape, lambda i: (0, 0))
    column = pl.BlockSpec((size, lanes), lambda i: (0, i))
    band = lambda part: pl.BlockSpec((lanes, model), lambda i: (i + part * pairs, 0))
    return pl.pallas_call(
        attend_kernel,
        name="attend",
        grid=(pairs,),
        out_shape=(
            jax.ShapeDtypeStruct((size, model), jnp.bfloat16),
            jax.ShapeDtypeStruct((2 * pairs, size, size), jnp.float32),
        ),
        in_specs=[column, column, column, band(0), band(1)]
        + [whole(sines), whole(cosines), whole(bases)],
        out_specs=(
            column,
            pl.BlockSpec((2, size, size), lambda i: (i, 0, 0)),
        ),
        compiler_params=pltpu.CompilerParams(vmem_limit_bytes=56 * 2**20),
        cost_estimate=pl.CostEstimate(
            flops=2 * 12 * size * (size * 1700 + 2 * 64 * 768),
            bytes_accessed=20 * 2**20,
            transcendentals=12 * size * size,
        ),
    )(*joined, rel_map, rel_map, sines, cosines, bases)


def attend_back_kernel(
    d_out, q, k, v, rel_text, rel_box, probs, sines, cosines, bases, dq, dk, dv, g_rel
):
    queries, keys, values, upstream = q[...], k[...], v[...], d_out[...]
    spread = bases[...]
    scale = HD ** (-0.5)
    low = jnp.bfloat16
    got = [[], [], []]
    for half in range(2):
        shares = probs[half]
        d_probs = dot_nt(masked(upstream, half), values)
        got[2].append(dot_tn(shares.astype(low), upstream))
        inner = jnp.sum(d_probs * shares, -1, keepdims=True)
        d_scores = (shares * (d_probs - inner)).astype(low)
        d_text = turn_back(dot_nn(d_scores, spread) * scale, sines[...], cosines[...])
        got[0].append(dot_nn(d_scores, keys) * scale + dot_nt(d_text, rel_text[...]))
        part = dot_tn(masked(queries, half), d_text)
        text_sum = part if half == 0 else text_sum + part
        turned = d_scores.T
        d_box = turn_back(dot_nn(turned, spread) * scale, sines[...], cosines[...])
        got[1].append(dot_nn(turned, queries) * scale + dot_nt(d_box, rel_box[...]))
        part = dot_tn(masked(keys, half), d_box)
        box_sum = part if half == 0 else box_sum + part
    for ref, halves in zip((dq, dk, dv), got):
        ref[...] = pick_halves(*halves).astype(low)
    g_rel[0] = text_sum.astype(low)
    g_rel[1] = box_sum.astype(low)


def attend_back(d_attended, joined, rel_map, probs, sines, cosines, bases):
    size, model = bases.shape
    pairs = model // (2 * HD)
    lanes = 2 * HD
    low = jnp.bfloat16
    whole = lambda rows: pl.BlockSpec(rows.shape, lambda i: (0, 0))
    column = pl.BlockSpec((size, lanes), lambda i: (0, i))
    band = lambda part: pl.BlockSpec((lanes, model), lambda i: (i + part * pairs, 0))
    return pl.pallas_call(
        attend_back_kernel,
        name="attend_back",
        grid=(pairs,),
        out_shape=(jax.ShapeDtypeStruct((size, model), low),) * 3
        + (jax.ShapeDtypeStruct((2, model, model), low),),
        in_specs=[column, column, column, column, band(0), band(1)]
        + [pl.BlockSpec((2, size, size), lambda i: (i, 0, 0))]
        + [whole(sines), whole(cosines), whole(bases)],
        out_specs=(column,) * 3 + (pl.BlockSpec((2, lanes, model), lambda i: (0, i, 0)),),
        compiler_params=pltpu.CompilerParams(vmem_limit_bytes=56 * 2**20),
        cost_estimate=pl.CostEstimate(
            flops=2 * 12 * size * (size * 1800 + 4 * 64 * 768),
            bytes_accessed=25 * 2**20,
            transcendentals=0,
        ),
    )(d_attended, *joined, rel_map, rel_map, probs, sines, cosines, bases)


def swap_middle(rows):
    count = rows.shape[0] // 4
    return jnp.concatenate(
        [rows[:count], rows[2 * count : 3 * count], rows[count : 2 * count], rows[3 * count :]], 0
    )


def forward(weights, rows, positions):
    box_map, mix_map, rel_map, out_map, up_map, down_map, norm_rows = weights
    gains = norm_rows.astype(jnp.float32)
    sin_count = box_map.shape[1]
    sin_x, cos_x, sin_y, cos_y = sinusoids(positions, sin_count // 4)
    sines = jnp.concatenate([sin_x, sin_y], -1)
    cosines = jnp.concatenate([cos_x, cos_y], -1)
    boxes = jnp.concatenate([sines, cosines], -1).astype(jnp.bfloat16)
    bases = jnp.concatenate([cosines, sines], -1).astype(jnp.bfloat16)
    embedded = rows + dot_nt(boxes, box_map)
    first = layer_norm(embedded, gains[0], gains[1])
    normed = first[0].astype(jnp.bfloat16)
    joined = [dot_nn(normed, part).astype(jnp.bfloat16) for part in mix_map]
    attended, probs = attend(joined, rel_map, sines, cosines, bases)
    second = layer_norm(first[0] + dot_nn(attended, out_map), gains[2], gains[3])
    middle = second[0].astype(jnp.bfloat16)
    hidden_pre = [dot_nn(middle, part) for part in up_map]
    hidden = [jax.nn.gelu(part, approximate=False).astype(jnp.bfloat16) for part in hidden_pre]
    lowered = sum(dot_nn(part, weight) for part, weight in zip(hidden, down_map))
    third = layer_norm(second[0] + lowered, gains[4], gains[5])
    return {
        "sines": sines,
        "cosines": cosines,
        "boxes": boxes,
        "bases": bases,
        "first": first,
        "normed": normed,
        "joined": joined,
        "probs": probs,
        "attended": attended,
        "second": second,
        "middle": middle,
        "hidden_pre": hidden_pre,
        "hidden": hidden,
        "third": third,
    }


def backward_upper(weights, cache, d_states):
    _, _, _, out_map, up_map, down_map, norm_rows = weights
    gains = norm_rows.astype(jnp.float32)
    d_mid, gain_last, bias_last = norm_back(
        d_states, cache["third"][1], cache["third"][2], gains[4]
    )
    d_down = d_mid.astype(jnp.bfloat16)
    gelu_exact = partial(jax.nn.gelu, approximate=False)
    grad_down, grad_up, d_second = [], [], d_mid
    for pre, hidden, up, down in zip(cache["hidden_pre"], cache["hidden"], up_map, down_map):
        grad_down.append(dot_tn(hidden, d_down))
        d_pre = jax.vjp(gelu_exact, pre)[1](dot_nt(d_down, down))[0].astype(jnp.bfloat16)
        grad_up.append(dot_tn(cache["middle"], d_pre))
        d_second = d_second + dot_nt(d_pre, up)
    d_lower, gain_mid, bias_mid = norm_back(
        d_second, cache["second"][1], cache["second"][2], gains[2]
    )
    d_attn = d_lower.astype(jnp.bfloat16)
    grad_out = dot_tn(cache["attended"], d_attn)
    d_attended = dot_nt(d_attn, out_map).astype(jnp.bfloat16)
    return d_lower, d_attended, grad_out, grad_up, grad_down, [gain_mid, bias_mid, gain_last, bias_last]


def backward_lower(weights, cache, d_lower, d_attended):
    box_map, mix_map, rel_map, _, _, _, norm_rows = weights
    gains = norm_rows.astype(jnp.float32)
    *d_joined, grad_rel = attend_back(
        d_attended,
        cache["joined"],
        rel_map,
        cache["probs"],
        cache["sines"],
        cache["cosines"],
        cache["bases"],
    )
    grad_mix = [dot_tn(cache["normed"], part) for part in d_joined]
    d_first = d_lower + sum(dot_nt(part, weight) for part, weight in zip(d_joined, mix_map))
    d_embedded, gain_low, bias_low = norm_back(
        d_first, cache["first"][1], cache["first"][2], gains[0]
    )
    grad_box = dot_tn(d_embedded.astype(jnp.bfloat16), cache["boxes"])
    return d_embedded, grad_box, grad_mix, grad_rel, [gain_low, bias_low]


def per_device(
    n,
    tokens,
    positions,
    documents,
    masking,
    negative_page,
    negative_row,
    pages,
    vocabulary,
    geometry,
    mixing,
    relative,
    merging,
    widening,
    narrowing,
    scaling,
    moment_vocabulary,
    moment_geometry,
    moment_mixing,
    moment_relative,
    moment_merging,
    moment_widening,
    moment_narrowing,
    moment_scaling,
    average_vocabulary,
    average_geometry,
    average_mixing,
    average_relative,
    average_merging,
    average_widening,
    average_narrowing,
    average_scaling,
):
    me = lax.axis_index("dp")
    size = tokens.shape[0]
    rows_own, model = vocabulary.shape
    page_rows = pages.shape[1]
    capacity = max(16, -(-2 * size // n) // 16 * 16)
    slots = n * capacity
    mask_float = masking.astype(jnp.float32)
    low = jnp.bfloat16
    fits = n % 8 == 0 and merging.shape[0] == 24 and page_rows % 16 == 0

    fold = 128 // capacity if fits else 1
    pieces = [
        swap_middle(geometry).T,
        swap_middle(relative).T,
        *[mixing[:, k * model : (k + 1) * model] for k in range(3)],
        merging,
        *[widening[:, k * model : (k + 1) * model] for k in range(widening.shape[1] // model)],
        narrowing,
    ]
    cols = scaling.shape[1]
    info = jnp.pad(scaling, ((1, 1), (0, 128 - cols)))
    lists, place = make_plan(tokens, masking, documents, info, n, rows_own, capacity, fold)
    bank_piece = pages.reshape(-1, model)
    if fits:
        asked, table_rows, full = front(lists, vocabulary, bank_piece, pieces, n, capacity, 1)
        wanted = jnp.sum(asked[:, 0].reshape(n // fold, fold, 128), 1)
        weights, at = [], 0
        for piece in [*pieces, bank_piece]:
            count = 2 * piece.shape[0]
            weights.append(full[:, :, at : at + count].reshape(-1, model))
            at += count
    else:
        (asked,) = exchange([lists], 1, "ask")
        wanted = asked[:, 0, :capacity]
        pieces = [piece.astype(low) for piece in pieces] + [bank_piece]
        joined = lax.all_gather(jnp.concatenate(pieces, 0), "dp", axis=0, tiled=False)
        weights, at = [], 0
        for piece in pieces:
            weights.append(joined[:, at : at + piece.shape[0]].reshape(-1, model))
            at += piece.shape[0]
    wanted = wanted.reshape(slots, 1)
    picks = (wanted == (jnp.arange(rows_own) + 1).astype(jnp.float32)[None, :]).astype(low)
    if not fits:
        answer = dot_nn(picks, vocabulary.astype(low)).astype(low)
        (table_rows,) = exchange([answer.reshape(n, capacity, model)], 2, "rows")
    table_rows = table_rows.reshape(slots, model)
    box_map, rel_map, mix_map = weights[0], weights[1], weights[2:5]
    out_map, up_map, down_full, bank = weights[5], weights[6:-2], weights[-2], weights[-1]
    norm_rows = asked[:, 1:7, :cols].transpose(1, 0, 2).reshape(6, n * cols).astype(low)
    count_of, doc_of = asked[:, 7, 0], asked[:, 7, 1]
    overflow = jnp.max(asked[:, 7, 2]) > 0.0
    my_count = jnp.sum(jnp.where(doc_of == documents[0].astype(jnp.float32), count_of, 0.0))
    share = 1.0 / (DOCS * jnp.maximum(my_count, 1.0))
    fixed = (mask_token // rows_own) * capacity + capacity - 1
    seats = (place == jnp.arange(slots)[None, :]).astype(low)
    target_rows = dot_nn(seats, table_rows)
    mask_rows = table_rows[fixed : fixed + 1].astype(jnp.float32)

    def dense_rows():
        table = lax.all_gather(vocabulary.astype(low), "dp", axis=0, tiled=True)
        return (
            table[tokens].astype(jnp.float32),
            table[mask_token : mask_token + 1].astype(jnp.float32),
        )

    target_rows, mask_rows = lax.cond(overflow, dense_rows, lambda: (target_rows, mask_rows))
    entry_rows = jnp.where(masking[:, None] == 1, mask_rows, target_rows)

    ff = len(up_map)
    down_map = [down_full[k * model : (k + 1) * model] for k in range(ff)]
    weights = (box_map, mix_map, rel_map, out_map, up_map, down_map, norm_rows)
    cache = forward(weights, entry_rows, positions)

    states_low = cache["third"][0].astype(low)
    inv_root = model ** (-0.5)
    positive = jnp.sum(states_low.astype(jnp.float32) * target_rows, -1, keepdims=True) * inv_root
    flat_index = (negative_page * page_rows + negative_row).T
    count_neg = flat_index.shape[1]
    width = bank.shape[0]
    repeated = jnp.tile(flat_index, (1, width // count_neg))
    chosen = repeated == jnp.arange(width)[None, :]
    logits = jnp.where(chosen, dot_nt(states_low, bank) * inv_root, -jnp.inf)
    highest = jnp.maximum(jnp.max(logits, -1, keepdims=True), positive)
    powers = jnp.exp(logits - highest)
    lead = jnp.exp(positive - highest)
    total = jnp.sum(powers, -1, keepdims=True) + lead
    per_token = highest + jnp.log(total) - positive
    mask_col = mask_float[:, None]
    loss_part = share * jnp.sum(mask_col * per_token)
    weight_map = (powers * (share * mask_col / total) * inv_root).astype(low)
    positive_grad = share * mask_col * (lead / total - 1.0) * inv_root
    d_states = positive_grad * target_rows + dot_nn(weight_map, bank)

    d_lower, d_attended, grad_out, grad_up, grad_down, upper_norms = backward_upper(
        weights, cache, d_states
    )
    d_embedded, grad_box, grad_mix, grad_rel, lower_norms = backward_lower(
        weights, cache, d_lower, d_attended
    )
    grad_norms = jnp.stack(lower_norms + upper_norms, 0)

    positive_rows = positive_grad * states_low.astype(jnp.float32)

    token_grads = jnp.where(mask_col == 1.0, positive_rows, d_embedded).astype(low)
    mask_grad = jnp.sum(mask_col * d_embedded, 0, keepdims=True)
    sent = dot_tn(seats, token_grads)
    sent = jnp.where(jnp.arange(slots)[:, None] == fixed, mask_grad, sent).astype(low)
    norm_blocks = grad_norms.reshape(6, n, cols).transpose(1, 0, 2)
    norm_blocks = jnp.pad(norm_blocks, ((0, 0), (0, 2), (0, 128 - cols)))
    sent = sent.reshape(n, capacity, model)
    grads = [grad_box, grad_rel.reshape(-1, model), *grad_mix, grad_out, *grad_up]
    grads = [grad.astype(low) for grad in [*grads, jnp.concatenate(grad_down, 0)]]
    if fits:
        came, norm_came, sums = to_owners(sent, norm_blocks, grads, n, 2)
        sums = split_rows(sums, grads, n)
    else:
        came, norm_came = exchange([sent, norm_blocks], 3, "grads")
        sums = scatter(grads, n)
    norm_piece = jnp.sum(norm_came, 0)[:6, :cols]

    def sparse_table():
        return dot_tn(picks, came.reshape(slots, model))

    def dense_table():
        entry = jnp.where(masking == 1, mask_token, tokens)
        table_grad = jnp.zeros((rows_own * n, model), jnp.float32).at[entry].add(d_embedded)
        table_grad = table_grad.at[tokens].add(positive_rows)
        return lax.psum_scatter(table_grad, "dp", scatter_dimension=0, tiled=True)

    table_piece = lax.cond(overflow, dense_table, sparse_table)

    reduced = (
        table_piece,
        swap_middle(sums[0].T),
        jnp.concatenate(sums[2:5], 1),
        swap_middle(sums[1].T),
        sums[5],
        jnp.concatenate(sums[6:-1], 1),
        sums[-1],
        norm_piece,
    )
    square = sum((jnp.sum(piece * piece) for piece in reduced))
    message = jnp.where(jnp.arange(128) == 0, square, jnp.where(jnp.arange(128) == 1, loss_part, 0.0))
    (totals,) = exchange([jnp.broadcast_to(message, (n, 8, 128))], 4, "totals")
    totals = jnp.sum(totals[:, 0, :2], 0)
    loss = totals[1]
    grad_norm = jnp.sqrt(totals[0])
    factor = clip_limit / jnp.maximum(grad_norm, clip_limit)
    decay = min(average_cap, (1.0 + STEP) / (10.0 + STEP))
    masters = (vocabulary, geometry, mixing, relative, merging, widening, narrowing, scaling)
    moments = (
        moment_vocabulary,
        moment_geometry,
        moment_mixing,
        moment_relative,
        moment_merging,
        moment_widening,
        moment_narrowing,
        moment_scaling,
    )
    averages = (
        average_vocabulary,
        average_geometry,
        average_mixing,
        average_relative,
        average_merging,
        average_widening,
        average_narrowing,
        average_scaling,
    )
    rates = (table_rate,) + (learn_rate,) * 7
    fresh, speeds, smooths = ([], [], [])
    for master, moment, average, piece, rate in zip(masters, moments, averages, reduced, rates):
        clipped = piece * factor
        velocity = momentum_decay * moment + clipped
        updated = master - rate * (clipped + momentum_decay * velocity)
        fresh.append(updated)
        speeds.append(velocity)
        smooths.append(decay * average + (1.0 - decay) * updated)
    return (loss, grad_norm, *fresh, *speeds, *smooths)


ROWS = P("dp", None)
COLS = P(None, "dp")
WEIGHTS = (ROWS, COLS, ROWS, COLS, ROWS, ROWS, ROWS, COLS)


def solution(mesh):
    return jax.shard_map(
        partial(per_device, mesh.shape["dp"]),
        mesh=mesh,
        in_specs=(P("dp"), COLS, P("dp"), P("dp"), COLS, COLS, P("dp", None, None)) + 3 * WEIGHTS,
        out_specs=(P(), P()) + 3 * WEIGHTS,
        check_vma=False,
    )
```

time: 855 us -> 539 us (0.63)
  waiting for transfers between devices: 228 us -> 0 us
  Pallas kernels: 84.6 us -> 310 us
  matrix products: 216 us -> 92.8 us
  blocking collectives: 102 us -> 0 us
  other arithmetic: 118 us -> 48.2 us
  local copies, waits for them, and re-layouts: 71.1 us -> 55.6 us
    pallas_call x5 -> x6, Pallas kernels: 84.6 us -> 310 us  [the longest x1 121 us: front(): pl.pallas_call(partial(front_kernel, n, units, capacity), name='front', o...]
    reduce_scatter x2 -> x0, waiting for transfers between devices: 211 us -> none  [scatter(): lax.psum_scatter(joined, 'dp', scatter_dimension=0, tiled=True)]
    dot_general x16 -> x0, matrix products: 127 us -> none  [the longest x1 13.2 us: forward(): jnp.einsum('tf,hsf->hts', bases, box_rot, preferred_element_type=jnp.floa...]
    another operation x6 -> x1, other arithmetic: 66 us -> 0.08 us  [make_plan(): jnp.stack([documents[0], lax.axis_index('dp')])]
    all_gather x1 -> x0, blocking collectives: 51 us -> none  [per_device(): norm_rows = lax.all_gather(scaling.astype(low), 'dp', axis=1, tiled=True)]
    unnamed x1 -> x0, blocking collectives: 50.7 us -> none
    all_gather x2 -> x0, waiting for transfers between devices: 15.3 us -> none  [gather(): lax.all_gather(jnp.concatenate(pieces, 0), 'dp', axis=0, tiled=False)]
    unnamed x275 -> x286, local copies, waits for them, and re-layouts: 32.6 us -> 18.3 us
  transfers between devices with their start and end apart: 4 -> 0, of which waited for: 3 -> 0; matrix products, arithmetic and copies ran while one was open for 18% -> 0% of each run, Pallas kernels for 0% -> 0%
where the time goes in v2:
time: 539 us; the launch traced here: 532 us
  Pallas kernels  310 us (58%)
  matrix products  92.8 us (17%)
  local copies, waits for them, and re-layouts  55.6 us (10%)
  other arithmetic  48.2 us (9%)
  between operations  25.6 us (5%)
    pallas_call x1, Pallas kernels, front(): pl.pallas_call(partial(front_kernel, n, units, capacity), name='front', o...  121 us
    pallas_call x1, Pallas kernels, to_owners(): pl.pallas_call(partial(back_kernel, n, units, chunks), name='back', out_s...  113 us
    dot_general x14, matrix products, dot_nn(): lax.dot_general(left, right, (((1,), (0,)), ((), ())), preferred_element_...  42.9 us
    pallas_call x1, Pallas kernels, attend_back(): pl.pallas_call(attend_back_kernel, name='attend_back', grid=(pairs,), out...  32.2 us
    pallas_call x1, Pallas kernels, attend(): pl.pallas_call(attend_kernel, name='attend', grid=(pairs,), out_shape=(ja...  28.2 us
    dot_general x15, matrix products, dot_tn(): lax.dot_general(left, right, (((0,), (0,)), ((), ())), preferred_element_...  26.8 us
    dot_general x14, matrix products, dot_nt(): lax.dot_general(left, right, (((1,), (1,)), ((), ())), preferred_element_...  23.1 us
    unnamed x286, local copies, waits for them, and re-layouts  18.3 us

profile of v2, /device:TPU:0, one launch (start us, length us, event | category | flops | bytes accessed | tf_op | source)
XLA Modules:
  0.0 531.8 jit_solution(2910645034091232849)
XLA Ops:
  9.6 2.0 plan.1
  13.8 121.4 %front.1 = (f32[32,8,128]{2,1,0:T(8,128)S(1)}, bf16[32,32,768]{2,1,0:T(8,128)(2,1)S(1)}, bf16[4,4,848,768]{3,2,1,0:T(8,128)(2,1)}) custom-call(f32[32,8,128]{2,1,0:T(8,128)S(1)} %get-tuple-element.74.refs_0_, f32[960,768]{1,0:T(8,128)} %refs_1_.1, bf16[64,768]{1,0:T(8,128)(2,1)S(1)} %bitcast.139, f32[24,768]{1,0:T(8,128)S(1)} %maximum_bitcast_fusion.1.refs_3_, ...), custom_call_target="tpu_custom_call" | custom-call | bytes 104857600 | tf_op jit(solution)/shard_map/front/pallas_call | solution.py:469
  137.4 2.2 fusion.6
  141.9 7.9 %fusion.54 = (bf16[4,4,48,768]{3,2,1,0:T(8,128)(2,1)}, bf16[4,4,48,768]{3,2,1,0:T(8,128)(2,1)}, bf16[4,4,48,768]{3,2,1,0:T(8,128)(2,1)}, bf16[4,4,48,768]{3,2,1,...) fusion(bf16[4,4,848,768]{3,2,1,0:T(8,128)(2,1)} %get-tuple-elem, ...), kind=kLoop, calls=%fused_computation.248 | loop fusion | bytes 21233664 | tf_op jit(solution)/shard_map/slice | solution.py:1054
  149.8 5.5 %multiply_cosine_fusion.1 = (f32[512,192]{1,0:T(8,128)}, bf16[512,192]{1,0:T(8,128)(2,1)S(1)}, bf16[512,192]{1,0:T(8,128)(2,1)}, f32[512,192]{1,0:T(8,128)}, f32...) fusion(f32[192]{0:T(256)S(1)} %multiply_power_fusion, ...), kind=kLoop, calls=%fused_computation.158 | loop fusion | flops 589824 | bytes 2364160 | tf_op jit(solution)/shard_map/cos | solution.py:29
  156.0 3.0 fusion.63
  165.9 3.4 slice.257
  172.0 28.2 %attend.1 = (bf16[512,768]{1,0:T(8,128)(2,1)}, f32[12,512,512]{2,1,0:T(8,128)}) custom-call(bf16[512,768]{1,0:T(8,128)(2,1)} %convolution_convert_fusion.16.q, bf16[512,768]{1,0:T(8,128)(2,1)} %convolution_convert_fusion.15.k, bf16[512,768]{1,0:T(8,128)(2,1)} %convolution_convert_fusion.14.v, bf16[1536,768]{1,0:T(8,128)(2,1)} %bitcast.153, ...), custom_call_target="tpu_custom_call" | custom-call | flops 11903434752 | bytes 20971520 | tf_op jit(solution)/shard_map/attend/pallas_call | solution.py:823
  200.3 2.7 fusion.64
  206.1 5.7 %multiply_convert_fusion.2 = (bf16[512,768]{1,0:T(8,128)(2,1)S(1)}, f32[512,768]{1,0:T(8,128)}, f32[512,768]{1,0:T(8,128)}) fusion(bf16[512,768]{1,0:T(8,128)(2,1)S(1)} %fusion.33, bf16[768,768]{1,0:T(8,128)(2,1)S(1)} %bitcast.148), kind=kOutput, calls=%fused_computation.61 | convolution fusion | flops 629538816 | bytes 5898240 | tf_op jit(solution)/shard_map/dot_general | solution.py:50
  211.8 3.0 fusion.53
  214.8 5.5 %multiply_convert_fusion.3 = (bf16[512,768]{1,0:T(8,128)(2,1)S(1)}, f32[512,768]{1,0:T(8,128)}, f32[512,768]{1,0:T(8,128)}) fusion(bf16[512,768]{1,0:T(8,128)(2,1)S(1)} %fusion.33, bf16[768,768]{1,0:T(8,128)(2,1)S(1)} %bitcast.182), kind=kOutput, calls=%fused_computation.74 | convolution fusion | flops 629538816 | bytes 5898240 | tf_op jit(solution)/shard_map/dot_general | solution.py:50
  221.9 5.3 %multiply_convert_fusion.5 = (bf16[512,768]{1,0:T(8,128)(2,1)S(1)}, f32[512,768]{1,0:T(8,128)}, f32[512,768]{1,0:T(8,128)}) fusion(bf16[512,768]{1,0:T(8,128)(2,1)S(1)} %fusion.33, bf16[768,768]{1,0:T(8,128)(2,1)S(1)} %bitcast.178), kind=kOutput, calls=%fused_computation.100 | convolution fusion | flops 629538816 | bytes 5898240 | tf_op jit(solution)/shard_map/dot_general | solution.py:50
  228.8 5.5 %multiply_convert_fusion.4 = (bf16[512,768]{1,0:T(8,128)(2,1)S(1)}, f32[512,768]{1,0:T(8,128)}, f32[512,768]{1,0:T(8,128)}) fusion(bf16[512,768]{1,0:T(8,128)(2,1)S(1)} %fusion.33, bf16[768,768]{1,0:T(8,128)(2,1)S(1)} %bitcast.180), kind=kOutput, calls=%fused_computation.87 | convolution fusion | flops 629538816 | bytes 5898240 | tf_op jit(solution)/shard_map/dot_general | solution.py:50
  239.7 3.8 slice.277
  243.5 2.5 broadcast_bitcast_fusion
  246.0 5.5 %copy.59 = s32[512,2048]{1,0:T(8,128)} copy(s32[512,2048]{0,1:T(8,128)} %broadcast_bitcast_fusion) | data formatting | bytes 8388608 | tf_op jit(solution)/shard_map/tile | solution.py:1104
  251.6 5.5 %fusion.66 = (f32[512]{0:T(512)S(1)}, f32[512,2048]{1,0:T(8,128)S(1)}) fusion(bf16[512,768]{1,0:T(8,128)(2,1)} %get-tuple-element.141, bf16[2048,768]{1,0:T(8,128)(2,1)} %bitcast.150, s32[512,2048]{1,0:T(8,128)} %copy.59), kind=kOutput, calls=%fused_computation.260 | convolution fusion | flops 1614806528 | bytes 12322816 | tf_op jit(solution)/shard_map/dot_general | solution.py:62
  260.9 7.3 %multiply_reduce_fusion.2 = (f32[768]{0:T(1024)}, f32[512]{0:T(512)S(1)}, f32[512]{0:T(512)S(1)}, f32[768]{0:T(1024)}, f32[512,768]{1,0:T(8,128)S(1)}) fusion(f32[512,768]{1,0:T(8,128)} %copy-done.5, f32[512]{0:T(512)S(1)} %add_rsqrt_fusion, f32[512]{0:T(512)S(1)} %broadcast_multiply_fusion.6, f32[768]{0:T(1024)S(1)} %copy-done.100, ...), kind=kOutput, calls=%fused_computation.40 | convolution fusion | flops 1619129856 | bytes 12082176 | tf_op jit(solution)/shard_map/dot_general | solution.py:50
  288.0 32.2 %attend_back.1 = (bf16[512,768]{1,0:T(8,128)(2,1)}, bf16[512,768]{1,0:T(8,128)(2,1)}, bf16[512,768]{1,0:T(8,128)(2,1)}, bf16[2,768,768]{2,1,0:T(8,128)(2,1)}) custom-call(bf16[512,768]{1,0:T(8,128)(2,1)} %convolution_convert_fusion.13.d_out, bf16[512,768]{1,0:T(8,128)(2,1)} %convolution_convert_fusion.16.q, bf16[512,768]{1,0:T(8,128)(2,1)} %convolution_convert_fusion.15.k, ...), custom_call_target="tpu_custom_call" | custom-call | flops 13740539904 | bytes 26214400 | tf_op jit(solution)/shard_map/attend_back/pallas_call | solution.py:883
  320.3 2.1 fusion.73
  326.6 2.5 select_convert_fusion
  330.5 1.9 convolution_convert_fusion.12
  332.5 1.9 convolution_convert_fusion.11
  351.6 2.5 pad_maximum_fusion
  354.2 112.9 %back.1 = (bf16[32,32,768]{2,1,0:T(8,128)(2,1)}, f32[32,8,128]{2,1,0:T(8,128)}, f32[360,768]{1,0:T(8,128)}) custom-call(bf16[32,32,768]{2,1,0:T(8,128)(2,1)} %bitcast.157, f32[32,8,128]{2,1,0:T(8,128)} %pad.9.refs_1_, bf16[4,4,48,768]{3,2,1,0:T(8,128)(2,1)} %bitcast.164, bf16[4,4,96,768]{3,2,1,0:T(8,128)(2,1)} %bitcast.152, ...), custom_call_target="tpu_custom_call" | custom-call | bytes 104857600 | tf_op jit(solution)/shard_map/back/pallas_call | solution.py:710
  470.1 4.1 conditional.3
  470.1 4.1 multiply_reduce_fusion
  474.2 2.6 fusion.55
  492.0 12.9 %totals.1 = f32[32,8,128]{2,1,0:T(8,128)} custom-call(f32[32,8,128]{2,1,0:T(8,128)} %broadcast_in_dim.127.refs_0_), custom_call_target="tpu_custom_call" | custom-call | bytes 2097152 | tf_op jit(solution)/shard_map/totals/pallas_call | solution.py:114
  507.4 8.1 %multiply_add_fusion = (f32[960,768]{1,0:T(8,128)}, f32[960,768]{1,0:T(8,128)}, f32[960,768]{1,0:T(8,128)}) fusion(f32[960,768]{1,0:T(8,128)} %param.58, f32[960,768]{1,0:T(8,128)S(1)} %copy-done.4, f32[960,768]{1,0:T(8,128)} %get-tuple-element.91, f32[]{:T(128)S(6)} %div.75, f32[960,768]{1,0:T(8,128)} %param.50), kind=kLoop, calls=%fused_computation.18 | loop fusion | flops 7372800 | bytes 20643844 | tf_op jit(solution)/shard_map/add | solution.py:1203
  521.1 2.0 multiply_add_fusion.5
  (401 shorter events, 94.5 us)
Async XLA Ops:
  7.2 6.5 %copy-start.3 = (bf16[1,64,768]{2,1,0:T(8,128)(2,1)S(1)}, bf16[1,64,768]{2,1,0:T(8,128)(2,1)}, u32[]{:S(2)}) copy-start(bf16[1,64,768]{2,1,0:T(8,128)(2,1)} %param.41) | copy-start | bytes 294916
  7.2 6.4 %copy-start.28 = (f32[24,3072]{1,0:T(8,128)S(1)}, f32[24,3072]{1,0:T(8,128)}, u32[]{:S(2)}) copy-start(f32[24,3072]{1,0:T(8,128)} %param.47) | copy-start | bytes 884740
  7.2 6.4 %copy-start.50 = (f32[24,2304]{1,0:T(8,128)S(1)}, f32[24,2304]{1,0:T(8,128)}, u32[]{:S(2)}) copy-start(f32[24,2304]{1,0:T(8,128)} %param.44) | copy-start | bytes 663556
  7.2 6.5 %copy-start.1 = (f32[24,768]{1,0:T(8,128)S(1)}, f32[24,768]{1,0:T(8,128)}, u32[]{:S(2)}) copy-start(f32[24,768]{1,0:T(8,128)} %refs_8_.1) | copy-start | bytes 221188
  7.2 6.5 %copy-start = (f32[96,768]{1,0:T(8,128)S(1)}, f32[96,768]{1,0:T(8,128)}, u32[]{:S(2)}) copy-start(f32[96,768]{1,0:T(8,128)} %refs_13_.1) | copy-start | bytes 884740
  141.9 7.9 %copy-start.115 = (s32[2,512]{1,0:T(2,128)S(1)}, s32[2,512]{1,0:T(2,128)}, u32[]{:S(2)}) copy-start(s32[2,512]{1,0:T(2,128)} %param.36) | copy-start | bytes 12292
  149.8 14.4 %copy-start.11 = (bf16[4,4,48,768]{3,2,1,0:T(8,128)(2,1)}, bf16[4,4,48,768]{3,2,1,0:T(8,128)(2,1)S(1)}, u32[]{:S(2)}) copy-start(bf16[4,4,48,768]{3,2,1,0:T(8,128)(2,1)S(1)} %get-tuple-element.163) | copy-start | bytes 3538948
  149.8 5.6 %copy-start.99 = (s32[512]{0:T(512)S(1)}, s32[512]{0:T(512)}, u32[]{:S(2)}) copy-start(s32[512]{0:T(512)} %param.38) | copy-start | bytes 6148
  155.4 15.4 %copy-start.42 = (bf16[512,192]{1,0:T(8,128)(2,1)}, bf16[512,192]{1,0:T(8,128)(2,1)S(1)}, u32[]{:S(2)}) copy-start(bf16[512,192]{1,0:T(8,128)(2,1)S(1)} %get-tuple-element.205) | copy-start | bytes 589828
  159.5 40.8 %copy-start.101 = (f32[512]{0:T(512)}, f32[512]{0:T(512)S(1)}, u32[]{:S(2)}) copy-start(f32[512]{0:T(512)S(1)} %add_rsqrt_fusion.2) | copy-start | bytes 6148
  172.0 28.2 %copy-start.34 = (bf16[4,4,48,768]{3,2,1,0:T(8,128)(2,1)S(1)}, bf16[4,4,48,768]{3,2,1,0:T(8,128)(2,1)}, u32[]{:S(2)}) copy-start(bf16[4,4,48,768]{3,2,1,0:T(8,128)(2,1)} %get-tuple-element.162) | copy-start | bytes 3538948
  205.2 23.0 %copy-start.62 = (bf16[512,768]{1,0:T(8,128)(2,1)}, bf16[512,768]{1,0:T(8,128)(2,1)S(1)}, u32[]{:S(2)}) copy-start(bf16[512,768]{1,0:T(8,128)(2,1)S(1)} %fusion.33) | copy-start | bytes 2359300
  211.8 23.3 %copy-start.54 = (bf16[512,768]{1,0:T(8,128)(2,1)}, bf16[512,768]{1,0:T(8,128)(2,1)S(1)}, u32[]{:S(2)}) copy-start(bf16[512,768]{1,0:T(8,128)(2,1)S(1)} %get-tuple-element.142) | copy-start | bytes 2359300
  214.8 12.4 %copy-start.22 = (bf16[1,4,192,768]{3,2,1,0:T(8,128)(2,1)}, bf16[1,4,192,768]{3,2,1,0:T(8,128)(2,1)S(1)}, u32[]{:S(2)}) copy-start(bf16[1,4,192,768]{3,2,1,0:T(8,128)(2,1)S(1)} %get-tuple-element.157) | copy-start | bytes 3538948
  214.8 19.5 %copy-start.24 = (bf16[1,4,192,768]{3,2,1,0:T(8,128)(2,1)}, bf16[1,4,192,768]{3,2,1,0:T(8,128)(2,1)S(1)}, u32[]{:S(2)}) copy-start(bf16[1,4,192,768]{3,2,1,0:T(8,128)(2,1)S(1)} %get-tuple-element.156) | copy-start | bytes 3538948
  214.8 20.3 %copy-start.9 = (bf16[1,4,192,768]{3,2,1,0:T(8,128)(2,1)}, bf16[1,4,192,768]{3,2,1,0:T(8,128)(2,1)S(1)}, u32[]{:S(2)}) copy-start(bf16[1,4,192,768]{3,2,1,0:T(8,128)(2,1)S(1)} %get-tuple-element.154) | copy-start | bytes 3538948
  260.9 7.3 %copy-start.6 = (f32[512,768]{1,0:T(8,128)S(1)}, f32[512,768]{1,0:T(8,128)}, u32[]{:S(2)}) copy-start(f32[512,768]{1,0:T(8,128)} %copy-done.5) | copy-start | bytes 4718596
  268.7 10.1 %copy-start.56 = (bf16[512,768]{1,0:T(8,128)(2,1)}, bf16[512,768]{1,0:T(8,128)(2,1)S(1)}, u32[]{:S(2)}) copy-start(bf16[512,768]{1,0:T(8,128)(2,1)S(1)} %get-tuple-element.138) | copy-start | bytes 2359300
  271.8 11.1 %copy-start.64 = (bf16[512,768]{1,0:T(8,128)(2,1)}, bf16[512,768]{1,0:T(8,128)(2,1)S(1)}, u32[]{:S(2)}) copy-start(bf16[512,768]{1,0:T(8,128)(2,1)S(1)} %add_convert_fusion) | copy-start | bytes 2359300
  286.3 37.0 %copy-start.7 = (f32[512,768]{1,0:T(8,128)}, f32[512,768]{1,0:T(8,128)S(1)}, u32[]{:S(2)}) copy-start(f32[512,768]{1,0:T(8,128)S(1)} %subtract_multiply_fusion.1) | copy-start | bytes 4718596
  288.0 32.2 %copy-start.33 = (bf16[4,4,48,768]{3,2,1,0:T(8,128)(2,1)S(1)}, bf16[4,4,48,768]{3,2,1,0:T(8,128)(2,1)}, u32[]{:S(2)}) copy-start(bf16[4,4,48,768]{3,2,1,0:T(8,128)(2,1)} %get-tuple-element.165) | copy-start | bytes 3538948
  474.2 33.1 %copy-start.4 = (f32[960,768]{1,0:T(8,128)S(1)}, f32[960,768]{1,0:T(8,128)}, u32[]{:S(2)}) copy-start(f32[960,768]{1,0:T(8,128)} %refs_1_.1) | copy-start | bytes 8847364
  507.2 8.3 %copy-start.78 = (f32[768,24]{0,1:T(8,128)S(1)}, f32[768,24]{0,1:T(8,128)}, u32[]{:S(2)}) copy-start(f32[768,24]{0,1:T(8,128)} %param.43) | copy-start | bytes 221188
  507.3 8.3 %copy-start.84 = (f32[192,24]{0,1:T(8,128)S(1)}, f32[192,24]{0,1:T(8,128)}, u32[]{:S(2)}) copy-start(f32[192,24]{0,1:T(8,128)} %copy-done.83) | copy-start | bytes 55300
  507.3 8.3 %copy-start.86 = (f32[192,24]{0,1:T(8,128)S(1)}, f32[192,24]{0,1:T(8,128)}, u32[]{:S(2)}) copy-start(f32[192,24]{0,1:T(8,128)} %copy-done.85) | copy-start | bytes 55300
  507.3 8.3 %copy-start.88 = (f32[192,24]{0,1:T(8,128)S(1)}, f32[192,24]{0,1:T(8,128)}, u32[]{:S(2)}) copy-start(f32[192,24]{0,1:T(8,128)} %copy-done.87) | copy-start | bytes 55300
  507.3 8.3 %copy-start.90 = (f32[192,24]{0,1:T(8,128)S(1)}, f32[192,24]{0,1:T(8,128)}, u32[]{:S(2)}) copy-start(f32[192,24]{0,1:T(8,128)} %copy-done.89) | copy-start | bytes 55300
  507.3 8.3 %copy-start.95 = (f32[768,24]{0,1:T(8,128)S(1)}, f32[768,24]{0,1:T(8,128)}, u32[]{:S(2)}) copy-start(f32[768,24]{0,1:T(8,128)} %param.59) | copy-start | bytes 221188
  507.3 8.3 %copy-start.96 = (f32[768,24]{0,1:T(8,128)S(1)}, f32[768,24]{0,1:T(8,128)}, u32[]{:S(2)}) copy-start(f32[768,24]{0,1:T(8,128)} %param.51) | copy-start | bytes 221188
  507.3 9.1 %copy-start.51 = (f32[24,2304]{1,0:T(8,128)S(1)}, f32[24,2304]{1,0:T(8,128)}, u32[]{:S(2)}) copy-start(f32[24,2304]{1,0:T(8,128)} %param.44) | copy-start | bytes 663556
  507.3 9.1 %copy-start.91 = (f32[24,2304]{1,0:T(8,128)S(1)}, f32[24,2304]{1,0:T(8,128)}, u32[]{:S(2)}) copy-start(f32[24,2304]{1,0:T(8,128)} %param.60) | copy-start | bytes 663556
  507.4 9.1 %copy-start.92 = (f32[24,2304]{1,0:T(8,128)S(1)}, f32[24,2304]{1,0:T(8,128)}, u32[]{:S(2)}) copy-start(f32[24,2304]{1,0:T(8,128)} %param.52) | copy-start | bytes 663556
  (111 other events, 234.1 us)

commit v3 on v2

--- a/solution.py
+++ b/solution.py
@@ -43,7 +43,11 @@
         - jnp.mean(scaled, -1, keepdims=True)
         - whitened * jnp.mean(scaled * whitened, -1, keepdims=True)
     )
-    return (rescale * inner, jnp.sum(upstream * whitened, 0), jnp.sum(upstream, 0))
+    return (
+        rescale * inner,
+        jnp.sum(upstream * whitened, 0, keepdims=True),
+        jnp.sum(upstream, 0, keepdims=True),
+    )
 
 
 def dot_nn(left, right):
@@ -227,12 +231,12 @@
 
 def front_kernel(n, units, capacity, *refs):
     count = len(units)
-    lists, vocabulary, pages = refs[:3]
-    weights = refs[3 : 3 + count]
-    asked, rows, full = refs[3 + count : 6 + count]
-    swap_out, swap_in, chip_rows, answers = refs[6 + count : 10 + count]
-    ask_send, ask_recv, row_send, row_recv, own_sem, swap_send, swap_recv = refs[10 + count : 17 + count]
-    hop_recv, core_recv, core_send, z_send, a_send, b_send = refs[17 + count :]
+    lists, vocabulary, pages, points, omegas = refs[:5]
+    weights = refs[5 : 5 + count]
+    asked, rows, full, sines, cosines = refs[5 + count : 10 + count]
+    swap_out, swap_in, chip_rows, answers = refs[10 + count : 14 + count]
+    ask_send, ask_recv, row_send, row_recv, own_sem, swap_send, swap_recv = refs[14 + count : 21 + count]
+    hop_recv, core_recv, core_send, z_send, a_send, b_send = refs[21 + count :]
     me = lax.axis_index("dp")
     core, spot, layer, step_a, step_b = place_of(me)
     layers = n // 8
@@ -367,6 +371,11 @@
     own_rows = pltpu.make_async_copy(answers.at[me], rows.at[me], own_sem.at[1])
     own_rows.start()
 
+    lane = lax.broadcasted_iota(jnp.int32, sines.shape, 1)
+    angles = jnp.where(lane < sines.shape[1] // 2, points[:, 0:1], points[:, 1:2]) * omegas[...]
+    sines[...] = jnp.sin(angles)
+    cosines[...] = jnp.cos(angles)
+
     def relay_column(gap):
         for way, level, there_is, further in (
             (0, layer - gap, layer - gap >= 0, high_z),
@@ -456,10 +465,15 @@
     lax.fori_loop(1, n, finish_rows, 0)
 
 
-def front(lists, vocabulary, pages, weights, n, capacity, ident):
+def front(lists, vocabulary, pages, positions, weights, n, capacity, ident):
     model = vocabulary.shape[1]
     layers = n // 8
     units = [weight.shape[0] // 24 for weight in weights]
+    points = positions.astype(jnp.float32).T
+    waves = model // 4
+    omegas = jnp.power(10000.0, -jnp.arange(waves).astype(jnp.float32) / waves)
+    omegas = jnp.concatenate([omegas, omegas])[None]
+    angles = jax.ShapeDtypeStruct((points.shape[0], 2 * waves), jnp.float32)
     swap = 24 * sum(units)
     chip = 2 * (swap + pages.shape[0])
     low = jnp.bfloat16
@@ -473,9 +487,11 @@
             jax.ShapeDtypeStruct(lists.shape, lists.dtype),
             jax.ShapeDtypeStruct((n, capacity, model), low),
             jax.ShapeDtypeStruct((layers, 4, chip, model), low),
-        ),
-        in_specs=[vmem] * (3 + len(weights)),
-        out_specs=(vmem, anywhere, anywhere),
+            angles,
+            angles,
+        ),
+        in_specs=[vmem] * (5 + len(weights)),
+        out_specs=(vmem, anywhere, anywhere, vmem, vmem),
         scratch_shapes=[
             pltpu.VMEM((swap, model // 2), jnp.float32),
             pltpu.VMEM((swap, model // 2), jnp.float32),
@@ -501,10 +517,10 @@
         cost_estimate=pl.CostEstimate(
             flops=0, bytes_accessed=100 * 2**20, transcendentals=0
         ),
-    )(lists, vocabulary, pages, *weights)
-
-
-def back_kernel(n, units, chunks, *refs):
+    )(lists, vocabulary, pages, points, omegas, *weights)
+
+
+def back_kernel(n, units, pieces, chunks, *refs):
     count = len(units)
     sent, small, grads = refs[0], refs[1], refs[2 : 2 + count]
     came, small_came, out = refs[2 + count : 5 + count]
@@ -667,8 +683,8 @@
         lax.fori_loop(1, layers, step, 0)
 
     at = 0
-    for offset, unit in zip(offsets, units):
-        rows = 24 * unit
+    for piece in pieces:
+        offset, rows = 2 * at, 24 * piece
         gone[pl.ds(at, rows)] = mine[pl.ds(pl.multiple_of(offset + (1 - core) * rows, 8), rows)]
         out[pl.ds(at, rows), here] = mine[pl.ds(pl.multiple_of(offset + core * rows, 8), rows)]
         at += rows
@@ -697,10 +713,10 @@
         copy.wait()
 
 
-def to_owners(sent, small, grads, n, ident):
-    model = grads[0].shape[1]
+def to_owners(sent, small, grads, pieces, n, ident):
+    model = grads[0].shape[2]
     layers = n // 8
-    units = [grad.shape[0] // n // 24 for grad in grads]
+    units = [grad.shape[1] // 48 for grad in grads]
     chunks = max(k for k in range(1, 6) if sum(units) % k == 0)
     rows = 48 * sum(units)
     half = model // 2
@@ -708,7 +724,7 @@
     dma = pltpu.SemaphoreType.DMA
     anywhere = pl.BlockSpec(memory_space=pl.ANY)
     return pl.pallas_call(
-        partial(back_kernel, n, units, chunks),
+        partial(back_kernel, n, units, pieces, chunks),
         name="back",
         out_shape=(
             jax.ShapeDtypeStruct(sent.shape, sent.dtype),
@@ -748,6 +764,397 @@
             flops=0, bytes_accessed=100 * 2**20, transcendentals=0
         ),
     )(sent, small, *[grad.reshape(layers, 4, -1, model) for grad in grads])
+
+
+def flat(rows):
+    return rows.reshape(-1, rows.shape[-1])
+
+
+def enter_kernel(
+    full, target, mask_rows, mask_col, sines, cosines, gains, normed_out, white_out, scale_out, low_out, q, k, v, held, sem
+):
+    low = jnp.bfloat16
+    box_copy = pltpu.make_async_copy(full.at[:, pl.ds(0, 48)], held.at[:, pl.ds(0, 48)], sem.at[0])
+    mix_copy = pltpu.make_async_copy(full.at[:, pl.ds(144, 144)], held.at[:, pl.ds(48, 144)], sem.at[1])
+    box_copy.start()
+    mix_copy.start()
+    rows = jnp.where(mask_col[...] == 1.0, mask_rows[...], target[...])
+    boxes = jnp.concatenate([sines[...], cosines[...]], 1).astype(low)
+    box_copy.wait()
+    embedded = rows + dot_nt(boxes, flat(held[:, 0:48]))
+    normed, white, scale = layer_norm(embedded, gains[0:1], gains[1:2])
+    normed_out[...], white_out[...], scale_out[...] = normed, white, scale
+    normed = normed.astype(low)
+    low_out[...] = normed
+    mix_copy.wait()
+    for third, ref in enumerate((q, k, v)):
+        part = flat(held[:, 48 + 48 * third : 96 + 48 * third])
+        ref[...] = dot_nn(normed, part).astype(low)
+
+
+def enter(full, target, mask_rows, mask_col, sines, cosines, gains):
+    size, model = target.shape
+    low, wide = jnp.bfloat16, jnp.float32
+    vmem = pl.BlockSpec(memory_space=pltpu.VMEM)
+    shape = jax.ShapeDtypeStruct
+    return pl.pallas_call(
+        enter_kernel,
+        name="enter",
+        out_shape=(
+            shape((size, model), wide),
+            shape((size, model), wide),
+            shape((size, 1), wide),
+            shape((size, model), low),
+        )
+        + (shape((size, model), low),) * 3,
+        in_specs=[pl.BlockSpec(memory_space=pl.ANY)] + [vmem] * 6,
+        out_specs=(vmem,) * 7,
+        scratch_shapes=[
+            pltpu.VMEM((full.shape[0], 192, model), low),
+            pltpu.SemaphoreType.DMA((2,)),
+        ],
+        compiler_params=pltpu.CompilerParams(vmem_limit_bytes=56 * 2**20),
+        cost_estimate=pl.CostEstimate(
+            flops=8 * size * model * model, bytes_accessed=16 * 2**20, transcendentals=0
+        ),
+    )(full, target, mask_rows, mask_col, sines, cosines, gains)
+
+
+def upper_kernel(
+    page_rows, full, attended, normed, target, mask_col, page, row, share, gains,
+    grads, d_attended, d_lower, pos_rows, norms, loss_part,
+    held, bank, slopes, hidden, scores, load_sem, store_sem,
+):
+    low = jnp.bfloat16
+    chips, used, model = held.shape
+    size = attended.shape[0]
+    blocks = hidden.shape[0]
+    first_row = 288
+    span = model // (used - 48 - 48 * blocks)
+    down_at = 48 + 48 * blocks
+    loads = [
+        pltpu.make_async_copy(full.at[:, pl.ds(first_row + at, many)], held.at[:, pl.ds(at, many)], load_sem.at[k])
+        for k, (at, many) in enumerate(((0, 48), (48, 48 * blocks), (down_at, used - down_at)))
+    ]
+    loads.append(
+        pltpu.make_async_copy(full.at[:, pl.ds(first_row + used, bank.shape[1])], bank, load_sem.at[3])
+    )
+    for copy in loads:
+        copy.start()
+
+    def up_map(k):
+        return flat(held[:, 48 + 48 * k : 96 + 48 * k])
+
+    def down_map(k):
+        return flat(held[span * k : span * (k + 1), down_at:])
+
+    loads[0].wait()
+    second, white_mid, scale_mid = layer_norm(
+        normed[...] + dot_nn(attended[...], flat(held[:, 0:48])), gains[2:3], gains[3:4]
+    )
+    middle = second.astype(low)
+    loads[1].wait()
+    loads[2].wait()
+    for k in range(blocks):
+        pre = dot_nn(middle, up_map(k))
+        normal = 0.5 + 0.5 * lax.erf(pre * (0.5**0.5))
+        active = (pre * normal).astype(low)
+        slopes[k] = normal + pre * (jnp.exp(-0.5 * pre * pre) * 0.3989422804014327)
+        hidden[k] = active
+        part = dot_nn(active, down_map(k))
+        lowered = part if k == 0 else lowered + part
+    states, white_last, scale_last = layer_norm(second + lowered, gains[4:5], gains[5:6])
+    states = states.astype(low)
+
+    inv_root = model ** (-0.5)
+    positive = jnp.sum(states.astype(jnp.float32) * target[...], -1, keepdims=True) * inv_root
+    many = page.shape[0]
+    seat = lax.broadcasted_iota(jnp.int32, (many, 128), 0)
+    lane = lax.broadcasted_iota(jnp.int32, (many, 128), 1)
+    spread = jnp.where(lax.rem(lane, many) == seat, 1.0, 0.0).astype(low)
+    wanted = page_rows * dot_tn(page[...].astype(jnp.float32).astype(low), spread) + dot_tn(
+        row[...].astype(jnp.float32).astype(low), spread
+    )
+    wanted = jnp.concatenate([wanted.astype(jnp.int32)] * 4, 1)
+    column = lax.broadcasted_iota(jnp.int32, wanted.shape, 1)
+    width = wanted.shape[1]
+    per = width // bank.shape[1]
+    parts = chips // per
+    loads[3].wait()
+    highest = positive
+    for c in range(parts):
+        raw = dot_nt(states, flat(bank[per * c : per * (c + 1)])) * inv_root
+        raw = jnp.where(wanted == column + c * width, raw, -jnp.inf)
+        scores[:, c * width : (c + 1) * width] = raw
+        highest = jnp.maximum(highest, jnp.max(raw, -1, keepdims=True))
+    lead = jnp.exp(positive - highest)
+    total = lead
+    for c in range(parts):
+        powers = jnp.exp(scores[:, c * width : (c + 1) * width] - highest)
+        scores[:, c * width : (c + 1) * width] = powers
+        total = total + jnp.sum(powers, -1, keepdims=True)
+    mask = mask_col[...]
+    loss_part[...] = share[0, 0] * jnp.sum(
+        mask * (highest + jnp.log(total) - positive), keepdims=True
+    )
+    factor = share[0, 0] * mask * inv_root
+    positive_grad = factor * (lead / total - 1.0)
+    factor = factor / total
+    pos_rows[...] = (positive_grad * states.astype(jnp.float32)).astype(pos_rows.dtype)
+    d_states = positive_grad * target[...]
+    for c in range(parts):
+        weights = (scores[:, c * width : (c + 1) * width] * factor).astype(low)
+        d_states = d_states + dot_nn(weights, flat(bank[per * c : per * (c + 1)]))
+
+    d_mid, gain_last, bias_last = norm_back(d_states, white_last, scale_last, gains[4:5])
+    d_down = d_mid.astype(low)
+    d_second = d_mid
+    stores = []
+    for k in range(blocks):
+        d_pre = (dot_nt(d_down, down_map(k)) * slopes[k]).astype(low)
+        d_second = d_second + dot_nt(d_pre, up_map(k))
+        grad = dot_tn(hidden[k], d_down).astype(low)
+        held[span * k : span * (k + 1), down_at:] = grad.reshape(span, -1, model)
+        grad = dot_tn(middle, d_pre).astype(low)
+        held[:, 48 + 48 * k : 96 + 48 * k] = grad.reshape(chips, 48, model)
+        for j, cut in enumerate(
+            (
+                (pl.ds(span * k, span), pl.ds(down_at, used - down_at)),
+                (pl.ds(0, chips), pl.ds(48 + 48 * k, 48)),
+            )
+        ):
+            stores.append(pltpu.make_async_copy(held.at[cut], grads.at[cut], store_sem.at[2 * k + j]))
+            stores[-1].start()
+    d_low, gain_mid, bias_mid = norm_back(d_second, white_mid, scale_mid, gains[2:3])
+    d_lower[...] = d_low
+    d_attn = d_low.astype(low)
+    d_attended[...] = dot_nt(d_attn, flat(held[:, 0:48])).astype(low)
+    held[:, 0:48] = dot_tn(attended[...], d_attn).astype(low).reshape(chips, 48, model)
+    cut = (pl.ds(0, chips), pl.ds(0, 48))
+    stores.append(pltpu.make_async_copy(held.at[cut], grads.at[cut], store_sem.at[2 * blocks]))
+    stores[-1].start()
+    for at, line in enumerate((gain_mid, bias_mid, gain_last, bias_last)):
+        norms[at : at + 1] = line
+    for copy in stores:
+        copy.wait()
+
+
+def upper(full, attended, normed, target, mask_col, page, row, share, gains, blocks, page_rows):
+    size, model = normed.shape
+    chips = full.shape[0]
+    used = full.shape[1] - 288 - 2 * page_rows
+    low, wide = jnp.bfloat16, jnp.float32
+    vmem = pl.BlockSpec(memory_space=pltpu.VMEM)
+    anywhere = pl.BlockSpec(memory_space=pl.ANY)
+    shape = jax.ShapeDtypeStruct
+    return pl.pallas_call(
+        partial(upper_kernel, page_rows),
+        name="upper",
+        out_shape=(
+            shape((chips, used, model), low),
+            shape((size, model), low),
+            shape((size, model), wide),
+            shape((size, model), low),
+            shape((4, model), wide),
+            shape((1, 1), wide),
+        ),
+        in_specs=[anywhere]
+        + [vmem] * 6
+        + [pl.BlockSpec(memory_space=pltpu.SMEM), vmem],
+        out_specs=(anywhere,) + (vmem,) * 5,
+        scratch_shapes=[
+            pltpu.VMEM((chips, used, model), low),
+            pltpu.VMEM((chips, 2 * page_rows, model), low),
+            pltpu.VMEM((blocks, size, model), wide),
+            pltpu.VMEM((blocks, size, model), low),
+            pltpu.VMEM((size, chips * 2 * page_rows), wide),
+            pltpu.SemaphoreType.DMA((4,)),
+            pltpu.SemaphoreType.DMA((2 * blocks + 1,)),
+        ],
+        compiler_params=pltpu.CompilerParams(vmem_limit_bytes=63 * 2**20),
+        cost_estimate=pl.CostEstimate(
+            flops=20 * 10**9, bytes_accessed=32 * 2**20, transcendentals=4 * size * model * 2
+        ),
+    )(full, attended, normed, target, mask_col, page, row, share, gains)
+
+
+def lower_kernel(
+    fixed, full, dq, dk, dv, d_lower, white, scale, gains, normed, sines, cosines, mask_col, pos_rows, place,
+    grads, d_embedded, sent, norms, held, sem,
+):
+    low = jnp.bfloat16
+    chips, _, model = held.shape
+    load = pltpu.make_async_copy(full.at[:, pl.ds(144, 144)], held.at[:, pl.ds(48, 144)], sem.at[0])
+    load.start()
+    mask = mask_col[...]
+    d_first = d_lower[...]
+    load.wait()
+    stores = []
+    for third, ref in enumerate((dq, dk, dv)):
+        at = 48 + 48 * third
+        upstream = ref[...]
+        d_first = d_first + dot_nt(upstream, flat(held[:, at : at + 48]))
+        held[:, at : at + 48] = dot_tn(normed[...], upstream).astype(low).reshape(chips, 48, model)
+        stores.append(
+            pltpu.make_async_copy(held.at[:, pl.ds(at, 48)], grads.at[:, pl.ds(at, 48)], sem.at[1 + third])
+        )
+        stores[-1].start()
+    d_rows, gain, bias = norm_back(d_first, white[...], scale[...], gains[0:1])
+    d_embedded[...] = d_rows
+    boxes = jnp.concatenate([sines[...], cosines[...]], 1).astype(low)
+    held[:, 0:48] = dot_tn(d_rows.astype(low), boxes).astype(low).reshape(chips, 48, model)
+    stores.append(pltpu.make_async_copy(held.at[:, pl.ds(0, 48)], grads.at[:, pl.ds(0, 48)], sem.at[4]))
+    stores[-1].start()
+    norms[0:1], norms[1:2] = gain, bias
+    token_grads = jnp.where(mask == 1.0, pos_rows[...].astype(jnp.float32), d_rows).astype(low)
+    mask_grad = jnp.sum(mask * d_rows, 0, keepdims=True)
+    slots = sent.shape[0]
+    seats = lax.broadcasted_iota(jnp.int32, (place.shape[0], slots), 1) == place[...]
+    found = dot_tn(jnp.where(seats, 1.0, 0.0).astype(low), token_grads)
+    line = lax.broadcasted_iota(jnp.int32, (slots, 1), 0)
+    sent[...] = jnp.where(line == fixed, mask_grad, found).astype(low)
+    for copy in stores:
+        copy.wait()
+
+
+def lower(
+    full, d_joined, d_lower, white, scale, gains, normed, sines, cosines, mask_col, pos_rows, place, slots, fixed
+):
+    size, model = d_lower.shape
+    chips = full.shape[0]
+    low, wide = jnp.bfloat16, jnp.float32
+    vmem = pl.BlockSpec(memory_space=pltpu.VMEM)
+    anywhere = pl.BlockSpec(memory_space=pl.ANY)
+    shape = jax.ShapeDtypeStruct
+    return pl.pallas_call(
+        partial(lower_kernel, fixed),
+        name="lower",
+        out_shape=(
+            shape((chips, 192, model), low),
+            shape((size, model), wide),
+            shape((slots, model), low),
+            shape((2, model), wide),
+        ),
+        in_specs=[anywhere] + [vmem] * 13,
+        out_specs=(anywhere,) + (vmem,) * 3,
+        scratch_shapes=[
+            pltpu.VMEM((chips, 192, model), low),
+            pltpu.SemaphoreType.DMA((5,)),
+        ],
+        compiler_params=pltpu.CompilerParams(vmem_limit_bytes=60 * 2**20),
+        cost_estimate=pl.CostEstimate(
+            flops=6 * 10**9, bytes_accessed=24 * 2**20, transcendentals=0
+        ),
+    )(full, *d_joined, d_lower, white, scale, gains, normed, sines, cosines, mask_col, pos_rows, place)
+
+
+def totals_kernel(n, table, sums, norm_came, loss_part, out, norm_piece, message, came, send_sem, recv_sem):
+    me = lax.axis_index("dp")
+    square = jnp.sum(sums[...] * sums[...], keepdims=True)
+    for part in range(4):
+        rows = table.shape[0] // 4
+        piece = table[part * rows : (part + 1) * rows]
+        square = square + jnp.sum(piece * piece, keepdims=True)
+    norm = norm_came[0]
+    for k in range(1, n):
+        norm = norm + norm_came[k]
+    norm_piece[...] = norm
+    square = square + jnp.sum(norm * norm, keepdims=True)
+    lane = lax.broadcasted_iota(jnp.int32, message.shape, 1)
+    message[...] = jnp.where(lane == 0, square, jnp.where(lane == 1, loss_part[...], 0.0))
+    greet_everyone(me, n)
+
+    def copy(step):
+        peer = lax.rem(me + step, n)
+        return remote_copy(message, came.at[me], send_sem.at[step], recv_sem.at[step], peer)
+
+    def start(step, carry):
+        copy(step).start()
+        return carry
+
+    def finish(step, carry):
+        copy(step).wait()
+        return carry
+
+    lax.fori_loop(1, n, start, 0)
+    came[me] = message[...]
+    lax.fori_loop(1, n, finish, 0)
+    total = came[0]
+    for k in range(1, n):
+        total = total + came[k]
+    out[...] = total
+
+
+def sum_totals(table, sums, norm_came, loss_part, n, ident):
+    vmem = pl.BlockSpec(memory_space=pltpu.VMEM)
+    tile = jax.ShapeDtypeStruct((8, 128), jnp.float32)
+    return pl.pallas_call(
+        partial(totals_kernel, n),
+        name="totals",
+        out_shape=(tile, tile),
+        in_specs=[vmem] * 4,
+        out_specs=(vmem,) * 2,
+        scratch_shapes=[
+            pltpu.VMEM((8, 128), jnp.float32),
+            pltpu.VMEM((n, 8, 128), jnp.float32),
+            pltpu.SemaphoreType.DMA((n,)),
+            pltpu.SemaphoreType.DMA((n,)),
+        ],
+        compiler_params=pltpu.CompilerParams(
+            collective_id=ident, has_side_effects=True, vmem_limit_bytes=32 * 2**20
+        ),
+        cost_estimate=pl.CostEstimate(flops=0, bytes_accessed=8 * 2**20, transcendentals=0),
+    )(table, sums, norm_came, loss_part)
+
+
+def update_kernel(decay, layout, factor, table, sums, *refs):
+    masters, moments, averages = refs[0:7], refs[7:14], refs[14:21]
+    fresh, speeds, smooths = refs[21:28], refs[28:35], refs[35:42]
+    scale = factor[0, 0]
+
+    def update(k, piece, rate, cut):
+        clipped = piece * scale
+        velocity = momentum_decay * moments[k][cut] + clipped
+        updated = masters[k][cut] - rate * (clipped + momentum_decay * velocity)
+        fresh[k][cut] = updated
+        speeds[k][cut] = velocity
+        smooths[k][cut] = decay * averages[k][cut] + (1.0 - decay) * updated
+
+    update(0, table[...], table_rate, (slice(None), slice(None)))
+
+    @pl.when(pl.program_id(0) == 0)
+    def _():
+        model = sums.shape[1]
+        for k, at, blocks, rows, turned in layout:
+            for block in range(blocks):
+                piece = sums[at + block * rows : at + (block + 1) * rows]
+                if turned:
+                    update(k, swap_middle(piece.T), learn_rate, (slice(None), slice(None)))
+                else:
+                    cut = (slice(None), slice(block * model, (block + 1) * model))
+                    update(k, piece, learn_rate, cut)
+
+
+def update_all(factor, table, sums, masters, moments, averages, decay, layout):
+    steps = 6
+    rows, model = table.shape
+    banded = pl.BlockSpec((rows // steps, model), lambda i: (i, 0))
+    whole = lambda array: pl.BlockSpec(array.shape, lambda i: (0, 0))
+    group = lambda arrays: [banded] + [whole(array) for array in arrays[1:]]
+    shapes = tuple(jax.ShapeDtypeStruct(array.shape, jnp.float32) for array in masters)
+    return pl.pallas_call(
+        partial(update_kernel, decay, layout),
+        name="update",
+        grid=(steps,),
+        out_shape=shapes * 3,
+        in_specs=[pl.BlockSpec(memory_space=pltpu.SMEM), banded, whole(sums)]
+        + group(masters)
+        + group(moments)
+        + group(averages),
+        out_specs=tuple(group(masters) * 3),
+        compiler_params=pltpu.CompilerParams(vmem_limit_bytes=56 * 2**20),
+        cost_estimate=pl.CostEstimate(flops=0, bytes_accessed=28 * 2**20, transcendentals=0),
+    )(factor, table, sums, *masters, *moments, *averages)
 
 
 def split_rows(packed, grads, n):
@@ -1046,13 +1453,11 @@
     lists, place = make_plan(tokens, masking, documents, info, n, rows_own, capacity, fold)
     bank_piece = pages.reshape(-1, model)
     if fits:
-        asked, table_rows, full = front(lists, vocabulary, bank_piece, pieces, n, capacity, 1)
+        asked, table_rows, full, sines, cosines = front(
+            lists, vocabulary, bank_piece, positions, pieces, n, capacity, 1
+        )
+        full = full.reshape(-1, *full.shape[2:])
         wanted = jnp.sum(asked[:, 0].reshape(n // fold, fold, 128), 1)
-        weights, at = [], 0
-        for piece in [*pieces, bank_piece]:
-            count = 2 * piece.shape[0]
-            weights.append(full[:, :, at : at + count].reshape(-1, model))
-            at += count
     else:
         (asked,) = exchange([lists], 1, "ask")
         wanted = asked[:, 0, :capacity]
@@ -1068,8 +1473,6 @@
         answer = dot_nn(picks, vocabulary.astype(low)).astype(low)
         (table_rows,) = exchange([answer.reshape(n, capacity, model)], 2, "rows")
     table_rows = table_rows.reshape(slots, model)
-    box_map, rel_map, mix_map = weights[0], weights[1], weights[2:5]
-    out_map, up_map, down_full, bank = weights[5], weights[6:-2], weights[-2], weights[-1]
     norm_rows = asked[:, 1:7, :cols].transpose(1, 0, 2).reshape(6, n * cols).astype(low)
     count_of, doc_of = asked[:, 7, 0], asked[:, 7, 1]
     overflow = jnp.max(asked[:, 7, 2]) > 0.0
@@ -1088,59 +1491,106 @@
         )
 
     target_rows, mask_rows = lax.cond(overflow, dense_rows, lambda: (target_rows, mask_rows))
-    entry_rows = jnp.where(masking[:, None] == 1, mask_rows, target_rows)
-
-    ff = len(up_map)
-    down_map = [down_full[k * model : (k + 1) * model] for k in range(ff)]
-    weights = (box_map, mix_map, rel_map, out_map, up_map, down_map, norm_rows)
-    cache = forward(weights, entry_rows, positions)
-
-    states_low = cache["third"][0].astype(low)
-    inv_root = model ** (-0.5)
-    positive = jnp.sum(states_low.astype(jnp.float32) * target_rows, -1, keepdims=True) * inv_root
-    flat_index = (negative_page * page_rows + negative_row).T
-    count_neg = flat_index.shape[1]
-    width = bank.shape[0]
-    repeated = jnp.tile(flat_index, (1, width // count_neg))
-    chosen = repeated == jnp.arange(width)[None, :]
-    logits = jnp.where(chosen, dot_nt(states_low, bank) * inv_root, -jnp.inf)
-    highest = jnp.maximum(jnp.max(logits, -1, keepdims=True), positive)
-    powers = jnp.exp(logits - highest)
-    lead = jnp.exp(positive - highest)
-    total = jnp.sum(powers, -1, keepdims=True) + lead
-    per_token = highest + jnp.log(total) - positive
     mask_col = mask_float[:, None]
-    loss_part = share * jnp.sum(mask_col * per_token)
-    weight_map = (powers * (share * mask_col / total) * inv_root).astype(low)
-    positive_grad = share * mask_col * (lead / total - 1.0) * inv_root
-    d_states = positive_grad * target_rows + dot_nn(weight_map, bank)
-
-    d_lower, d_attended, grad_out, grad_up, grad_down, upper_norms = backward_upper(
-        weights, cache, d_states
-    )
-    d_embedded, grad_box, grad_mix, grad_rel, lower_norms = backward_lower(
-        weights, cache, d_lower, d_attended
-    )
-    grad_norms = jnp.stack(lower_norms + upper_norms, 0)
-
-    positive_rows = positive_grad * states_low.astype(jnp.float32)
-
-    token_grads = jnp.where(mask_col == 1.0, positive_rows, d_embedded).astype(low)
-    mask_grad = jnp.sum(mask_col * d_embedded, 0, keepdims=True)
-    sent = dot_tn(seats, token_grads)
-    sent = jnp.where(jnp.arange(slots)[:, None] == fixed, mask_grad, sent).astype(low)
+    if fits:
+        gains = norm_rows.astype(jnp.float32)
+        rel_map = full[:, 48:144].reshape(-1, model)
+        bases = jnp.concatenate([cosines, sines], -1).astype(low)
+        normed, white, scale, normed_low, *joined = enter(
+            full, target_rows, mask_rows, mask_col, sines, cosines, gains
+        )
+        attended, probs = attend(joined, rel_map, sines, cosines, bases)
+        blocks = widening.shape[1] // model
+        upper_grads, d_attended, d_lower, positive_rows, upper_norms, loss_part = upper(
+            full,
+            attended,
+            normed,
+            target_rows,
+            mask_col,
+            negative_page,
+            negative_row,
+            share.reshape(1, 1),
+            gains,
+            blocks,
+            page_rows,
+        )
+        *d_joined, grad_rel = attend_back(
+            d_attended, joined, rel_map, probs, sines, cosines, bases
+        )
+        lower_grads, d_embedded, sent, lower_norms = lower(
+            full,
+            d_joined,
+            d_lower,
+            white,
+            scale,
+            gains,
+            normed_low,
+            sines,
+            cosines,
+            mask_col,
+            positive_rows,
+            place,
+            slots,
+            fixed,
+        )
+        grad_norms = jnp.concatenate([lower_norms, upper_norms], 0)
+        positive_rows = positive_rows.astype(jnp.float32)
+    else:
+        box_map, rel_map, mix_map = weights[0], weights[1], weights[2:5]
+        out_map, up_map, down_full, bank = weights[5], weights[6:-2], weights[-2], weights[-1]
+        entry_rows = jnp.where(masking[:, None] == 1, mask_rows, target_rows)
+
+        ff = len(up_map)
+        down_map = [down_full[k * model : (k + 1) * model] for k in range(ff)]
+        weights = (box_map, mix_map, rel_map, out_map, up_map, down_map, norm_rows)
+        cache = forward(weights, entry_rows, positions)
+
+        states_low = cache["third"][0].astype(low)
+        inv_root = model ** (-0.5)
+        positive = jnp.sum(states_low.astype(jnp.float32) * target_rows, -1, keepdims=True) * inv_root
+        flat_index = (negative_page * page_rows + negative_row).T
+        count_neg = flat_index.shape[1]
+        width = bank.shape[0]
+        repeated = jnp.tile(flat_index, (1, width // count_neg))
+        chosen = repeated == jnp.arange(width)[None, :]
+        logits = jnp.where(chosen, dot_nt(states_low, bank) * inv_root, -jnp.inf)
+        highest = jnp.maximum(jnp.max(logits, -1, keepdims=True), positive)
+        powers = jnp.exp(logits - highest)
+        lead = jnp.exp(positive - highest)
+        total = jnp.sum(powers, -1, keepdims=True) + lead
+        per_token = highest + jnp.log(total) - positive
+        mask_col = mask_float[:, None]
+        loss_part = share * jnp.sum(mask_col * per_token)
+        weight_map = (powers * (share * mask_col / total) * inv_root).astype(low)
+        positive_grad = share * mask_col * (lead / total - 1.0) * inv_root
+        d_states = positive_grad * target_rows + dot_nn(weight_map, bank)
+
+        d_lower, d_attended, grad_out, grad_up, grad_down, upper_norms = backward_upper(
+            weights, cache, d_states
+        )
+        d_embedded, grad_box, grad_mix, grad_rel, lower_norms = backward_lower(
+            weights, cache, d_lower, d_attended
+        )
+        grad_norms = jnp.concatenate(lower_norms + upper_norms, 0)
+
+        positive_rows = positive_grad * states_low.astype(jnp.float32)
+        token_grads = jnp.where(mask_col == 1.0, positive_rows, d_embedded).astype(low)
+        mask_grad = jnp.sum(mask_col * d_embedded, 0, keepdims=True)
+        sent = dot_tn(seats, token_grads)
+        sent = jnp.where(jnp.arange(slots)[:, None] == fixed, mask_grad, sent).astype(low)
+
     norm_blocks = grad_norms.reshape(6, n, cols).transpose(1, 0, 2)
     norm_blocks = jnp.pad(norm_blocks, ((0, 0), (0, 2), (0, 128 - cols)))
     sent = sent.reshape(n, capacity, model)
-    grads = [grad_box, grad_rel.reshape(-1, model), *grad_mix, grad_out, *grad_up]
-    grads = [grad.astype(low) for grad in [*grads, jnp.concatenate(grad_down, 0)]]
     if fits:
-        came, norm_came, sums = to_owners(sent, norm_blocks, grads, n, 2)
-        sums = split_rows(sums, grads, n)
+        grads = [lower_grads, grad_rel.reshape(n // 2, -1, model), upper_grads]
+        parts = (1, 1, 1, 1, 2, 1) + (1,) * blocks + (narrowing.shape[0] // 24,)
+        came, norm_came, sums = to_owners(sent, norm_blocks, grads, parts, n, 2)
     else:
         came, norm_came = exchange([sent, norm_blocks], 3, "grads")
+        grads = [grad_box, grad_rel.reshape(-1, model), *grad_mix, grad_out, *grad_up]
+        grads = [grad.astype(low) for grad in [*grads, jnp.concatenate(grad_down, 0)]]
         sums = scatter(grads, n)
-    norm_piece = jnp.sum(norm_came, 0)[:6, :cols]
 
     def sparse_table():
         return dot_tn(picks, came.reshape(slots, model))
@@ -1153,24 +1603,6 @@
 
     table_piece = lax.cond(overflow, dense_table, sparse_table)
 
-    reduced = (
-        table_piece,
-        swap_middle(sums[0].T),
-        jnp.concatenate(sums[2:5], 1),
-        swap_middle(sums[1].T),
-        sums[5],
-        jnp.concatenate(sums[6:-1], 1),
-        sums[-1],
-        norm_piece,
-    )
-    square = sum((jnp.sum(piece * piece) for piece in reduced))
-    message = jnp.where(jnp.arange(128) == 0, square, jnp.where(jnp.arange(128) == 1, loss_part, 0.0))
-    (totals,) = exchange([jnp.broadcast_to(message, (n, 8, 128))], 4, "totals")
-    totals = jnp.sum(totals[:, 0, :2], 0)
-    loss = totals[1]
-    grad_norm = jnp.sqrt(totals[0])
-    factor = clip_limit / jnp.maximum(grad_norm, clip_limit)
-    decay = min(average_cap, (1.0 + STEP) / (10.0 + STEP))
     masters = (vocabulary, geometry, mixing, relative, merging, widening, narrowing, scaling)
     moments = (
         moment_vocabulary,
@@ -1192,16 +1624,58 @@
         average_narrowing,
         average_scaling,
     )
-    rates = (table_rate,) + (learn_rate,) * 7
-    fresh, speeds, smooths = ([], [], [])
-    for master, moment, average, piece, rate in zip(masters, moments, averages, reduced, rates):
+    decay = min(average_cap, (1.0 + STEP) / (10.0 + STEP))
+    if fits:
+        totals, norm_piece = sum_totals(table_piece, sums, norm_came, loss_part, n, 4)
+        norm_piece = norm_piece[:6, :cols]
+    else:
+        norm_piece = jnp.sum(norm_came, 0)[:6, :cols]
+        reduced = (
+            table_piece,
+            swap_middle(sums[0].T),
+            jnp.concatenate(sums[2:5], 1),
+            swap_middle(sums[1].T),
+            sums[5],
+            jnp.concatenate(sums[6:-1], 1),
+            sums[-1],
+            norm_piece,
+        )
+        square = sum((jnp.sum(piece * piece) for piece in reduced))
+        lane = jnp.arange(128)
+        message = jnp.where(lane == 0, square, jnp.where(lane == 1, loss_part, 0.0))
+        (totals,) = exchange([jnp.broadcast_to(message, (n, 8, 128))], 4, "totals")
+        totals = jnp.sum(totals, 0)
+    loss = totals[0, 1]
+    grad_norm = jnp.sqrt(totals[0, 0])
+    factor = clip_limit / jnp.maximum(grad_norm, clip_limit)
+
+    def update(master, moment, average, piece, rate):
         clipped = piece * factor
         velocity = momentum_decay * moment + clipped
         updated = master - rate * (clipped + momentum_decay * velocity)
-        fresh.append(updated)
-        speeds.append(velocity)
-        smooths.append(decay * average + (1.0 - decay) * updated)
-    return (loss, grad_norm, *fresh, *speeds, *smooths)
+        return updated, velocity, decay * average + (1.0 - decay) * updated
+
+    last = update(scaling, moment_scaling, average_scaling, norm_piece, learn_rate)
+    if fits:
+        row = sums.shape[0] - narrowing.shape[0]
+        layout = (
+            (1, 0, 1, 24, True),
+            (2, 24, 3, 24, False),
+            (3, 96, 1, 48, True),
+            (4, 144, 1, 24, False),
+            (5, 168, blocks, 24, False),
+            (6, row, 1, narrowing.shape[0], False),
+        )
+        groups = [group[:7] for group in (masters, moments, averages)]
+        done = update_all(factor.reshape(1, 1), table_piece, sums, *groups, decay, layout)
+        fresh, speeds, smooths = done[:7], done[7:14], done[14:]
+    else:
+        rates = (table_rate,) + (learn_rate,) * 6
+        done = [
+            update(*group) for group in zip(masters[:7], moments[:7], averages[:7], reduced[:7], rates)
+        ]
+        fresh, speeds, smooths = zip(*done)
+    return (loss, grad_norm, *fresh, last[0], *speeds, last[1], *smooths, last[2])
 
 
 ROWS = P("dp", None)

time: 539 us -> 445 us (0.83)
  matrix products: 92.8 us -> 6.06 us
  Pallas kernels: 310 us -> 379 us
  other arithmetic: 48.2 us -> 4.71 us
  local copies, waits for them, and re-layouts: 55.6 us -> 28.2 us
  between operations: 25.6 us -> 18.8 us
    pallas_call x2 -> x6, Pallas kernels: 126 us -> 195 us  [the longest x1 113 us: to_owners(): pl.pallas_call(partial(back_kernel, n, units, pieces, chunks), name='back...]
    dot_general x14 -> x1, matrix products: 42.9 us -> 2.48 us  [dot_nn(): lax.dot_general(left, right, (((1,), (0,)), ((), ())), preferred_element_...]
    dot_general x15 -> x1, matrix products: 26.8 us -> 3.57 us  [dot_tn(): lax.dot_general(left, right, (((0,), (0,)), ((), ())), preferred_element_...]
    dot_general x14 -> x0, matrix products: 23.1 us -> none  [dot_nt(): lax.dot_general(left, right, (((1,), (1,)), ((), ())), preferred_element_...]
    slice x6 -> x2, local copies, waits for them, and re-layouts: 19.4 us -> 3.81 us  [the longest x1 3.22 us: per_device(): rel_map = full[:, 48:144].reshape(-1, model)]
    add x8 -> x1, other arithmetic: 15.9 us -> 0.61 us  [update(): return (updated, velocity, decay * average + (1.0 - decay) * updated)]
    reduce_sum x14 -> x1, other arithmetic: 11.4 us -> 0.74 us  [per_device(): jnp.sum(jnp.where(doc_of == documents[0].astype(jnp.float32), count_of, 0...]
    another operation x9 -> x0, local copies, waits for them, and re-layouts: 8.64 us -> none  [the longest x2 8.01 us: per_device(): repeated = jnp.tile(flat_index, (1, width // count_neg))]
where the time goes in v3:
time: 445 us; the launch traced here: 437 us
  Pallas kernels  379 us (85%)
  local copies, waits for them, and re-layouts  28.2 us (6%)
  between operations  18.8 us (4%)
  matrix products  6.06 us (1%)
  other arithmetic  4.71 us (1%)
    pallas_call x1, Pallas kernels, front(): pl.pallas_call(partial(front_kernel, n, units, capacity), name='front', o...  121 us
    pallas_call x1, Pallas kernels, to_owners(): pl.pallas_call(partial(back_kernel, n, units, pieces, chunks), name='back...  113 us
    pallas_call x1, Pallas kernels, upper(): pl.pallas_call(partial(upper_kernel, page_rows), name='upper', out_shape=...  32.9 us
    pallas_call x1, Pallas kernels, attend_back(): pl.pallas_call(attend_back_kernel, name='attend_back', grid=(pairs,), out...  32.4 us
    pallas_call x1, Pallas kernels, attend(): pl.pallas_call(attend_kernel, name='attend', grid=(pairs,), out_shape=(ja...  28.4 us
    unnamed x70, local copies, waits for them, and re-layouts  18.4 us
    pallas_call x1, Pallas kernels, sum_totals(): pl.pallas_call(partial(totals_kernel, n), name='totals', out_shape=(tile,...  15.4 us
    pallas_call x1, Pallas kernels, lower(): pl.pallas_call(partial(lower_kernel, fixed), name='lower', out_shape=(sha...  13.4 us

profile of v3, /device:TPU:0, one launch (start us, length us, event | category | flops | bytes accessed | tf_op | source)
XLA Modules:
  0.0 437.3 jit_solution(10143177537860933321)
XLA Ops:
  7.3 1.0 fusion.5
  8.4 0.9 fusion.6
  9.4 1.1 fusion.3
  11.5 1.8 plan.1
  13.6 121.4 %front.1 = (f32[32,8,128]{2,1,0:T(8,128)S(1)}, bf16[32,32,768]{2,1,0:T(8,128)(2,1)S(1)}, bf16[4,4,848,768]{3,2,1,0:T(8,128)(2,1)}, f32[512,384]{1,0:T(8,128)S(1)}, f32[512,384]{1,0:T(8,128)S(1)}) custom-call(f32[32,8,128]{2,1,0:T(8,128)S(1)} %get-tuple-element.115.refs_0_, f32[960,768]{1,0:T(8,128)} %refs_0_.1, bf16[64,768]{1,0:T(8,128)(2,1)S(1)} %bitcast.35, ...), custom_call_target="tpu_custom_call" | custom-call | bytes 104857600 | tf_op jit(solution)/shard_map/front/pallas_call | solution.py:483
  135.9 0.9 copy-done.2
  136.8 1.1 copy-done.10
  138.1 2.5 fusion
  143.0 0.9 reshape.112.gains
  144.8 7.5 %enter.1 = (f32[512,768]{1,0:T(8,128)}, f32[512,768]{1,0:T(8,128)}, f32[512,1]{1,0:T(8,128)}, bf16[512,768]{1,0:T(8,128)(2,1)}, bf16[512,768]{1,0:T(8,128)(2,1)}...) custom-call(bf16[16,848,768]{2,1,0:T(8,128)(2,1)} %bitcast.38, f32[512,768]{1,0:T(8,128)S(1)} %get-tuple-element.120.target, ...), custom_call_target="tpu_custom_call" | custom-call | flops 2415919104 | bytes 16777216 | tf_op jit(solution)/shard_map/enter/pallas_call | solution.py:800
  152.4 0.9 pad_maximum_fusion.bases
  153.3 3.2 slice.109
  156.5 28.4 %attend.1 = (bf16[512,768]{1,0:T(8,128)(2,1)}, f32[12,512,512]{2,1,0:T(8,128)}) custom-call(bf16[512,768]{1,0:T(8,128)(2,1)} %get-tuple-element.124.q, bf16[512,768]{1,0:T(8,128)(2,1)} %get-tuple-element.125.k, bf16[512,768]{1,0:T(8,128)(2,1)} %get-tuple-element.126.v, bf16[1536,768]{1,0:T(8,128)(2,1)} %bitcast.45, bf16[1536,768]{1,0:T(8,128)(2,1)} %bitcast.46, ...), custom_call_target="tpu_custom_call" | custom-call | flops 11903434752 | bytes 20971520 | tf_op jit(solution)/shard_map/attend/pallas_call | solution.py:1230
  185.7 32.9 %upper.1 = (bf16[16,432,768]{2,1,0:T(8,128)(2,1)}, bf16[512,768]{1,0:T(8,128)(2,1)}, f32[512,768]{1,0:T(8,128)}, bf16[512,768]{1,0:T(8,128)(2,1)S(1)}, f32[4,768]{1,0:T(4,128)}, /*index=5*/f32[1,1]{1,0:T(1,128)}) custom-call(bf16[16,848,768]{2,1,0:T(8,128)(2,1)} %bitcast.40, bf16[512,768]{1,0:T(8,128)(2,1)} %get-tuple-element.127.attended, ...), custom_call_target="tpu_custom_call" | custom-call | flops 20000000000 | bytes 33554432 | tf_op jit(solution)/shard_map/upper/pallas_call | solution.py:950
  218.6 32.4 %attend_back.1 = (bf16[512,768]{1,0:T(8,128)(2,1)}, bf16[512,768]{1,0:T(8,128)(2,1)}, bf16[512,768]{1,0:T(8,128)(2,1)}, bf16[2,768,768]{2,1,0:T(8,128)(2,1)}) custom-call(bf16[512,768]{1,0:T(8,128)(2,1)} %get-tuple-element.129.d_out, bf16[512,768]{1,0:T(8,128)(2,1)} %get-tuple-element.124.q, bf16[512,768]{1,0:T(8,128)(2,1)} %get-tuple-element.125.k, ...), custom_call_target="tpu_custom_call" | custom-call | flops 13740539904 | bytes 26214400 | tf_op jit(solution)/shard_map/attend_back/pallas_call | solution.py:1290
  251.0 13.4 %lower.1 = (bf16[16,192,768]{2,1,0:T(8,128)(2,1)}, f32[512,768]{1,0:T(8,128)}, bf16[1024,768]{1,0:T(8,128)(2,1)}, f32[2,768]{1,0:T(2,128)}) custom-call(bf16[16,848,768]{2,1,0:T(8,128)(2,1)} %bitcast.41, bf16[512,768]{1,0:T(8,128)(2,1)} %get-tuple-element.131.dq, bf16[512,768]{1,0:T(8,128)(2,1)} %get-tuple-element.132.dk, ...), custom_call_target="tpu_custom_call" | custom-call | flops 6000000000 | bytes 25165824 | tf_op jit(solution)/shard_map/lower/pallas_call | solution.py:1029
  266.0 112.9 %back.1 = (bf16[32,32,768]{2,1,0:T(8,128)(2,1)}, f32[32,8,128]{2,1,0:T(8,128)}, f32[360,768]{1,0:T(8,128)}) custom-call(bf16[32,32,768]{2,1,0:T(8,128)(2,1)} %bitcast.49, f32[32,8,128]{2,1,0:T(8,128)} %pad.9.refs_1_, bf16[4,4,192,768]{3,2,1,0:T(8,128)(2,1)} %bitcast.43, bf16[4,4,96,768]{3,2,1,0:T(8,128)(2,1)} %bitcast.44, bf16[4,4,432,768]{3,2,1,0:T(8,128)(2,1)} %bitcast.42), custom_call_target="tpu_custom_call" | custom-call | bytes 104857600 | tf_op jit(solution)/shard_map/back/pallas_call | solution.py:726
  379.3 1.0 copy-done.29
  380.3 3.6 conditional.3
  380.3 3.6 fusion.8
  384.0 15.4 %totals.1 = (f32[8,128]{1,0:T(8,128)S(1)}, f32[8,128]{1,0:T(8,128)S(1)}) custom-call(f32[960,768]{1,0:T(8,128)} %get-tuple-element.258.table, f32[360,768]{1,0:T(8,128)S(1)} %copy-done.4, f32[32,8,128]{2,1,0:T(8,128)S(1)} %copy-done.8, f32[1,1]{1,0:T(1,128)} %get-tuple-element.149.loss_part), custom_call_target="tpu_custom_call" | custom-call | bytes 8388608 | tf_op jit(solution)/shard_map/totals/pallas_call | solution.py:1091
  401.3 0.9 copy.78.refs_1_
  402.3 0.9 copy.79.refs_3_
  403.2 0.9 copy.80.refs_8_
  404.1 0.9 copy.81.refs_10_
  405.0 0.9 copy.82.refs_15_
  406.0 0.9 copy.83.refs_17_
  406.9 13.2 %update.1 = (f32[960,768]{1,0:T(8,128)}, f32[768,24]{1,0:T(8,128)}, f32[24,2304]{1,0:T(8,128)}, f32[768,48]{1,0:T(8,128)}, f32[24,768]{1,0:T(8,128)}, /*index=5*...) custom-call(f32[1,1]{1,0:T(1,128)} %bitcast.25.factor, ...), custom_call_target="tpu_custom_call" | custom-call | bytes 29360128 | tf_op jit(solution)/shard_map/update/pallas_call | solution.py:1145
  420.1 1.9 copy.85
  422.0 1.8 copy.87
  423.8 1.8 copy.89
  425.6 1.8 copy.84
  (87 shorter events, 9.2 us)
Async XLA Ops:
  7.2 4.1 copy-start.21
  7.2 4.2 copy-start.23
  7.2 4.3 copy-start.22
  7.2 6.1 %copy-start.28 = (s32[2,512]{1,0:T(2,128)S(1)}, s32[2,512]{1,0:T(2,128)}, u32[]{:S(2)}) copy-start(s32[2,512]{1,0:T(2,128)} %param.36) | copy-start | bytes 12292
  7.2 6.4 %copy-start.9 = (bf16[1,64,768]{2,1,0:T(8,128)(2,1)S(1)}, bf16[1,64,768]{2,1,0:T(8,128)(2,1)}, u32[]{:S(2)}) copy-start(bf16[1,64,768]{2,1,0:T(8,128)(2,1)} %param.41) | copy-start | bytes 294916
  7.3 6.3 %copy-start.7 = (f32[24,768]{1,0:T(8,128)S(1)}, f32[24,768]{1,0:T(8,128)}, u32[]{:S(2)}) copy-start(f32[24,768]{1,0:T(8,128)} %refs_4_.1) | copy-start | bytes 221188
  7.3 6.3 %copy-start.5 = (f32[96,768]{1,0:T(8,128)S(1)}, f32[96,768]{1,0:T(8,128)}, u32[]{:S(2)}) copy-start(f32[96,768]{1,0:T(8,128)} %refs_6_.1) | copy-start | bytes 884740
  13.3 124.6 %copy-start.6 = (s32[512,1]{1,0:T(8,128)}, s32[512,1]{1,0:T(8,128)S(1)}, u32[]{:S(2)}) copy-start(s32[512,1]{1,0:T(8,128)S(1)} %get-tuple-element.118.place) | copy-start | bytes 6148
  135.0 0.9 copy-start
  135.9 0.9 copy-start.2
  136.8 1.1 copy-start.10
  142.9 9.3 %copy-start.12 = (f32[512,768]{1,0:T(8,128)}, f32[512,768]{1,0:T(8,128)S(1)}, u32[]{:S(2)}) copy-start(f32[512,768]{1,0:T(8,128)S(1)} %get-tuple-element.120.target) | copy-start | bytes 4718596
  144.8 7.5 %copy-start.3 = (f32[512,384]{1,0:T(8,128)S(1)}, f32[512,384]{1,0:T(8,128)}, u32[]{:S(2)}) copy-start(f32[512,384]{1,0:T(8,128)} %copy-done.2) | copy-start | bytes 2359300
  144.8 7.5 %copy-start.1 = (f32[512,384]{1,0:T(8,128)S(1)}, f32[512,384]{1,0:T(8,128)}, u32[]{:S(2)}) copy-start(f32[512,384]{1,0:T(8,128)} %copy-done) | copy-start | bytes 2359300
  251.0 13.4 %copy-start.25 = (f32[4,768]{1,0:T(4,128)S(1)}, f32[4,768]{1,0:T(4,128)}, u32[]{:S(2)}) copy-start(f32[4,768]{1,0:T(4,128)} %get-tuple-element.141) | copy-start | bytes 36868
  378.9 1.4 copy-start.29
  380.3 3.6 copy-start.4
  380.3 3.6 copy-start.8
  383.9 16.8 %copy-start.24 = (f32[6,24]{1,0:T(8,128)S(1)}, f32[6,24]{1,0:T(8,128)}, u32[]{:S(2)}) copy-start(f32[6,24]{1,0:T(8,128)} %param.49) | copy-start | bytes 1732
  383.9 16.8 %copy-start.26 = (f32[6,24]{1,0:T(8,128)S(1)}, f32[6,24]{1,0:T(8,128)}, u32[]{:S(2)}) copy-start(f32[6,24]{1,0:T(8,128)} %param.65) | copy-start | bytes 1732
  383.9 16.8 %copy-start.27 = (f32[6,24]{1,0:T(8,128)S(1)}, f32[6,24]{1,0:T(8,128)}, u32[]{:S(2)}) copy-start(f32[6,24]{1,0:T(8,128)} %param.57) | copy-start | bytes 1732
  383.9 17.4 %copy-start.14 = (f32[768,24]{0,1:T(8,128)S(1)}, f32[768,24]{0,1:T(8,128)}, u32[]{:S(2)}) copy-start(f32[768,24]{0,1:T(8,128)} %param.43) | copy-start | bytes 221188
  383.9 18.3 %copy-start.13 = (f32[768,48]{0,1:T(8,128)S(1)}, f32[768,48]{0,1:T(8,128)}, u32[]{:S(2)}) copy-start(f32[768,48]{0,1:T(8,128)} %param.45) | copy-start | bytes 442372
  383.9 19.3 %copy-start.19 = (f32[768,24]{0,1:T(8,128)S(1)}, f32[768,24]{0,1:T(8,128)}, u32[]{:S(2)}) copy-start(f32[768,24]{0,1:T(8,128)} %param.51) | copy-start | bytes 221188
  383.9 20.2 %copy-start.17 = (f32[768,48]{0,1:T(8,128)S(1)}, f32[768,48]{0,1:T(8,128)}, u32[]{:S(2)}) copy-start(f32[768,48]{0,1:T(8,128)} %param.53) | copy-start | bytes 442372
  384.0 21.1 %copy-start.20 = (f32[768,24]{0,1:T(8,128)S(1)}, f32[768,24]{0,1:T(8,128)}, u32[]{:S(2)}) copy-start(f32[768,24]{0,1:T(8,128)} %param.59) | copy-start | bytes 221188
  399.4 6.6 %copy-start.18 = (f32[768,48]{0,1:T(8,128)S(1)}, f32[768,48]{0,1:T(8,128)}, u32[]{:S(2)}) copy-start(f32[768,48]{0,1:T(8,128)} %param.61) | copy-start | bytes 442372
  420.1 7.3 %copy-start.16 = (f32[768,24]{1,0:T(8,128)S(1)}, f32[768,24]{1,0:T(8,128)}, u32[]{:S(2)}) copy-start(f32[768,24]{1,0:T(8,128)} %get-tuple-element.211) | copy-start | bytes 221188
  420.1 8.0 %copy-start.15 = (f32[768,24]{1,0:T(8,128)S(1)}, f32[768,24]{1,0:T(8,128)}, u32[]{:S(2)}) copy-start(f32[768,24]{1,0:T(8,128)} %get-tuple-element.219) | copy-start | bytes 221188

commit v4 on v3

--- a/solution.py
+++ b/solution.py
@@ -50,6 +50,12 @@
     )
 
 
+def swap_middle(rows, axis=0):
+    count = rows.shape[axis] // 4
+    cuts = [lax.slice_in_dim(rows, k * count, (k + 1) * count, axis=axis) for k in (0, 2, 1, 3)]
+    return jnp.concatenate(cuts, axis)
+
+
 def dot_nn(left, right):
     return lax.dot_general(
         left, right, (((1,), (0,)), ((), ())), preferred_element_type=jnp.float32
@@ -66,71 +72,6 @@
     return lax.dot_general(
         left, right, (((1,), (1,)), ((), ())), preferred_element_type=jnp.float32
     )
-
-
-def exchange_kernel(n, count, *refs):
-    srcs, dsts = refs[:count], refs[count : 2 * count]
-    send_sem, recv_sem, own_sem = refs[2 * count :]
-    me = lax.axis_index("dp")
-    barrier = pltpu.get_barrier_semaphore()
-
-    def greet(step, carry):
-        pl.semaphore_signal(
-            barrier, inc=1, device_id=(lax.rem(me + step, n),), device_id_type=MESH
-        )
-        return carry
-
-    lax.fori_loop(1, n, greet, 0)
-    for k in range(count):
-        pltpu.make_async_copy(srcs[k].at[me], dsts[k].at[me], own_sem.at[k]).start()
-    pl.semaphore_wait(barrier, n - 1)
-
-    def copy(k, step):
-        peer = lax.rem(me + step, n)
-        return pltpu.make_async_remote_copy(
-            src_ref=srcs[k].at[peer],
-            dst_ref=dsts[k].at[me],
-            send_sem=send_sem.at[k, step],
-            recv_sem=recv_sem.at[k, step],
-            device_id=(peer,),
-            device_id_type=MESH,
-        )
-
-    def start(step, carry):
-        for k in range(count):
-            copy(k, step).start()
-        return carry
-
-    def finish(step, carry):
-        for k in range(count):
-            copy(k, step).wait()
-        return carry
-
-    lax.fori_loop(1, n, start, 0)
-    lax.fori_loop(1, n, finish, 0)
-    for k in range(count):
-        pltpu.make_async_copy(srcs[k].at[me], dsts[k].at[me], own_sem.at[k]).wait()
-
-
-def exchange(arrays, ident, name):
-    count, n = len(arrays), arrays[0].shape[0]
-    anywhere = pl.BlockSpec(memory_space=pl.ANY)
-    return pl.pallas_call(
-        partial(exchange_kernel, n, count),
-        name=name,
-        out_shape=tuple(jax.ShapeDtypeStruct(rows.shape, rows.dtype) for rows in arrays),
-        in_specs=[anywhere] * count,
-        out_specs=(anywhere,) * count,
-        scratch_shapes=[
-            pltpu.SemaphoreType.DMA((count, n)),
-            pltpu.SemaphoreType.DMA((count, n)),
-            pltpu.SemaphoreType.DMA((count,)),
-        ],
-        compiler_params=pltpu.CompilerParams(collective_id=ident, has_side_effects=True),
-        cost_estimate=pl.CostEstimate(
-            flops=0, bytes_accessed=2 * 2**20, transcendentals=0
-        ),
-    )(*arrays)
 
 
 def plan_kernel(
@@ -173,7 +114,7 @@
     extra = jnp.where(lane == 0, count, jnp.where(lane == 1, own[0].astype(jnp.float32), over))
     extra = jnp.where(line == 7, extra, info[...])
     line = lax.broadcasted_iota(jnp.int32, lists.shape, 1)
-    lists[...] = jnp.where(line == 0, table[:, None, :], extra[None])
+    lists[...] = jnp.where(line == 6, table[:, None, :], extra[None])
 
 
 def make_plan(tokens, masking, documents, info, n, rows_own, capacity, fold):
@@ -229,304 +170,14 @@
     pl.semaphore_wait(barrier, n - 1)
 
 
-def front_kernel(n, units, capacity, *refs):
+def back_kernel(n, units, pieces, chunks, fold, *refs):
     count = len(units)
-    lists, vocabulary, pages, points, omegas = refs[:5]
-    weights = refs[5 : 5 + count]
-    asked, rows, full, sines, cosines = refs[5 + count : 10 + count]
-    swap_out, swap_in, chip_rows, answers = refs[10 + count : 14 + count]
-    ask_send, ask_recv, row_send, row_recv, own_sem, swap_send, swap_recv = refs[14 + count : 21 + count]
-    hop_recv, core_recv, core_send, z_send, a_send, b_send = refs[21 + count :]
-    me = lax.axis_index("dp")
-    core, spot, layer, step_a, step_b = place_of(me)
-    layers = n // 8
-    half = chip_rows.shape[1]
-    page_rows = pages.shape[0]
-    here = pl.ds(pl.multiple_of(core * half, 128), half)
-    there = pl.ds(pl.multiple_of((1 - core) * half, 128), half)
-    partner = me + 1 - 2 * core
-    to_a, to_b, up, down = me + 2 * step_a, me + 2 * step_b, me + 8, me - 8
-    spot_a, spot_b, spot_ab = spot + step_a, spot + step_b, spot + step_a + step_b
-
-    at = 0
-    for ref, unit in zip(weights, units):
-        swap_out[pl.ds(at, 24 * unit)] = ref[:, there]
-        at += 24 * unit
-    greet_everyone(me, n)
-    swaps = [
-        remote_copy(swap_out, swap_in, swap_send.at[0], swap_recv.at[0], partner),
-        remote_copy(
-            pages.at[:, there],
-            chip_rows.at[pl.ds(2 * at + core * page_rows, page_rows)],
-            swap_send.at[1],
-            swap_recv.at[1],
-            partner,
-        ),
-    ]
-    for copy in swaps:
-        copy.start()
-
-    def ask(step):
-        peer = lax.rem(me + step, n)
-        return remote_copy(lists.at[peer], asked.at[me], ask_send.at[step], ask_recv.at[step], peer)
-
-    def start_ask(step, carry):
-        ask(step).start()
-        return carry
-
-    def wait_ask(step, carry):
-        ask(step).wait()
-        return carry
-
-    lax.fori_loop(1, n, start_ask, 0)
-    asked[me] = lists[me]
-    chip_rows[pl.ds(2 * at + pl.multiple_of(core * page_rows, page_rows), page_rows)] = pages[:, here]
-    for copy in swaps:
-        copy.wait_recv()
-    at = 0
-    for ref, unit in zip(weights, units):
-        mine, other = ref[:, here], swap_in[pl.ds(at, 24 * unit)]
-        ordered = jnp.where(
-            core == 0, jnp.concatenate([mine, other], 0), jnp.concatenate([other, mine], 0)
-        )
-        chip_rows[pl.ds(2 * at, 48 * unit)] = ordered.astype(chip_rows.dtype)
-        at += 24 * unit
-
-    def block(level, index):
-        return full.at[level, index, :, here]
-
-    def z_hop(way, level, src=None):
-        return remote_copy(
-            block(level, spot) if src is None else src, block(level, spot),
-            z_send.at[way, level], hop_recv.at[level, spot], up if way == 0 else down,
-        )
-
-    def a_hop(level, src=None):
-        return remote_copy(
-            block(level, spot) if src is None else src, block(level, spot),
-            a_send.at[level], hop_recv.at[level, spot], to_a,
-        )
-
-    def b_hop(kind, level, src=None):
-        index = spot if kind == 0 else spot_a
-        return remote_copy(
-            block(level, index) if src is None else src, block(level, index),
-            b_send.at[kind, level], hop_recv.at[level, index], to_b,
-        )
-
-    def core_hop(level, index, src=None):
-        return remote_copy(
-            block(level, index) if src is None else src, block(level, index),
-            core_send.at[level, index], core_recv.at[level, index], partner,
-        )
-
-    def arrived(level, index):
-        pltpu.make_async_copy(block(level, index), block(level, index), hop_recv.at[level, index]).wait()
-
-    low_z, high_z = layer > 0, layer < layers - 1
-
-    @pl.when(high_z)
-    def _():
-        z_hop(0, layer, chip_rows).start()
-
-    @pl.when(low_z)
-    def _():
-        z_hop(1, layer, chip_rows).start()
-
-    a_hop(layer, chip_rows).start()
-    b_hop(0, layer, chip_rows).start()
-    core_hop(layer, spot, chip_rows).start()
-    own = pltpu.make_async_copy(chip_rows, block(layer, spot), own_sem.at[0])
-    own.start()
-
-    lax.fori_loop(1, n, wait_ask, 0)
-    rows_own = vocabulary.shape[0]
-    table = vocabulary[...].astype(jnp.bfloat16)
-    group = 128 // capacity
-
-    def row_copy(peer):
-        return remote_copy(
-            answers.at[peer], rows.at[me], row_send.at[peer], row_recv.at[me], peer
-        )
-
-    def answer(turn, carry):
-        ids = jnp.zeros((8, 128), jnp.float32)
-        for k in range(group):
-            ids = ids + asked[turn * group + k]
-        ids = ids.T[:, 0:1]
-        wanted = lax.broadcasted_iota(jnp.int32, (128, rows_own), 1) + 1
-        picks = jnp.where(ids.astype(jnp.int32) == wanted, 1.0, 0.0).astype(jnp.bfloat16)
-        found = dot_nn(picks, table).astype(jnp.bfloat16)
-        for k in range(group):
-            peer = turn * group + k
-            answers[peer] = found[k * capacity : (k + 1) * capacity]
-
-            @pl.when(peer != me)
-            def _():
-                row_copy(peer).start()
-
-        return carry
-
-    lax.fori_loop(0, n // group, answer, 0)
-    own_rows = pltpu.make_async_copy(answers.at[me], rows.at[me], own_sem.at[1])
-    own_rows.start()
-
-    lane = lax.broadcasted_iota(jnp.int32, sines.shape, 1)
-    angles = jnp.where(lane < sines.shape[1] // 2, points[:, 0:1], points[:, 1:2]) * omegas[...]
-    sines[...] = jnp.sin(angles)
-    cosines[...] = jnp.cos(angles)
-
-    def relay_column(gap):
-        for way, level, there_is, further in (
-            (0, layer - gap, layer - gap >= 0, high_z),
-            (1, layer + gap, layer + gap < layers, low_z),
-        ):
-
-            @pl.when(there_is)
-            def _():
-                arrived(level, spot)
-
-                @pl.when(further)
-                def _():
-                    z_hop(way, level).start()
-
-                a_hop(level).start()
-                b_hop(0, level).start()
-                core_hop(level, spot).start()
-
-    def at_gap(gap, visit):
-        if gap == 0:
-            visit(layer)
-            return
-
-        @pl.when(layer - gap >= 0)
-        def _():
-            visit(layer - gap)
-
-        @pl.when(layer + gap < layers)
-        def _():
-            visit(layer + gap)
-
-    def relay_a(level):
-        arrived(level, spot_a)
-        b_hop(1, level).start()
-        core_hop(level, spot_a).start()
-
-    def relay_b(index):
-        def visit(level):
-            arrived(level, index)
-            core_hop(level, index).start()
-
-        return visit
-
-    for gap in range(layers):
-        if gap > 0:
-            relay_column(gap)
-        at_gap(gap, relay_a)
-        if gap > 0:
-            at_gap(gap - 1, relay_b(spot_b))
-            at_gap(gap - 1, relay_b(spot_ab))
-    at_gap(layers - 1, relay_b(spot_b))
-    at_gap(layers - 1, relay_b(spot_ab))
-
-    def finish(level, carry):
-        for index in (spot, spot_a, spot_b, spot_ab):
-            core_hop(level, index).wait_send()
-        for index in range(4):
-            other = full.at[level, index, :, there]
-            pltpu.make_async_copy(other, other, core_recv.at[level, index]).wait()
-        a_hop(level).wait_send()
-        b_hop(0, level).wait_send()
-        b_hop(1, level).wait_send()
-
-        @pl.when((level <= layer) & high_z)
-        def _():
-            z_hop(0, level).wait_send()
-
-        @pl.when((level >= layer) & low_z)
-        def _():
-            z_hop(1, level).wait_send()
-
-        return carry
-
-    lax.fori_loop(0, layers, finish, 0)
-    own.wait()
-    own_rows.wait()
-    for copy in swaps:
-        copy.wait_send()
-
-    def finish_rows(step, carry):
-        peer = lax.rem(me + step, n)
-        pltpu.make_async_copy(answers.at[peer], answers.at[peer], row_send.at[peer]).wait()
-        source = lax.rem(me - step + n, n)
-        pltpu.make_async_copy(rows.at[source], rows.at[source], row_recv.at[source]).wait()
-        return carry
-
-    lax.fori_loop(1, n, finish_rows, 0)
-
-
-def front(lists, vocabulary, pages, positions, weights, n, capacity, ident):
-    model = vocabulary.shape[1]
-    layers = n // 8
-    units = [weight.shape[0] // 24 for weight in weights]
-    points = positions.astype(jnp.float32).T
-    waves = model // 4
-    omegas = jnp.power(10000.0, -jnp.arange(waves).astype(jnp.float32) / waves)
-    omegas = jnp.concatenate([omegas, omegas])[None]
-    angles = jax.ShapeDtypeStruct((points.shape[0], 2 * waves), jnp.float32)
-    swap = 24 * sum(units)
-    chip = 2 * (swap + pages.shape[0])
-    low = jnp.bfloat16
-    dma = pltpu.SemaphoreType.DMA
-    vmem = pl.BlockSpec(memory_space=pltpu.VMEM)
-    anywhere = pl.BlockSpec(memory_space=pl.ANY)
-    return pl.pallas_call(
-        partial(front_kernel, n, units, capacity),
-        name="front",
-        out_shape=(
-            jax.ShapeDtypeStruct(lists.shape, lists.dtype),
-            jax.ShapeDtypeStruct((n, capacity, model), low),
-            jax.ShapeDtypeStruct((layers, 4, chip, model), low),
-            angles,
-            angles,
-        ),
-        in_specs=[vmem] * (5 + len(weights)),
-        out_specs=(vmem, anywhere, anywhere, vmem, vmem),
-        scratch_shapes=[
-            pltpu.VMEM((swap, model // 2), jnp.float32),
-            pltpu.VMEM((swap, model // 2), jnp.float32),
-            pltpu.VMEM((chip, model // 2), low),
-            pltpu.VMEM((n, capacity, model), low),
-            dma((n,)),
-            dma((n,)),
-            dma((n,)),
-            dma((n,)),
-            dma((2,)),
-            dma((2,)),
-            dma((2,)),
-            dma((layers, 4)),
-            dma((layers, 4)),
-            dma((layers, 4)),
-            dma((2, layers)),
-            dma((layers,)),
-            dma((2, layers)),
-        ],
-        compiler_params=pltpu.CompilerParams(
-            collective_id=ident, has_side_effects=True, vmem_limit_bytes=48 * 2**20
-        ),
-        cost_estimate=pl.CostEstimate(
-            flops=0, bytes_accessed=100 * 2**20, transcendentals=0
-        ),
-    )(lists, vocabulary, pages, points, omegas, *weights)
-
-
-def back_kernel(n, units, pieces, chunks, *refs):
-    count = len(units)
-    sent, small, grads = refs[0], refs[1], refs[2 : 2 + count]
-    came, small_came, out = refs[2 + count : 5 + count]
-    own, par, from_b, from_a, from_z, mine, gone, back = refs[5 + count : 13 + count]
-    row_send, row_recv, own_sem, load_sem, pair_send, pair_recv = refs[13 + count : 19 + count]
-    b_send, b_recv, a_send, a_recv, z_send, z_recv, f_send, f_recv = refs[19 + count :]
+    sent, small, asked, loss_part, grads = *refs[:4], refs[4 : 4 + count]
+    out, table, norm_piece, totals = refs[4 + count : 8 + count]
+    own, par, from_b, from_a, from_z, mine, gone, back = refs[8 + count : 16 + count]
+    came, small_came, picks, message, told = refs[16 + count : 21 + count]
+    row_send, row_recv, own_sem, load_sem, pair_send, pair_recv = refs[21 + count : 27 + count]
+    b_send, b_recv, a_send, a_recv, z_send, z_recv, f_send, f_recv, t_send, t_recv = refs[27 + count :]
     layers = n // 8
     me = lax.axis_index("dp")
     core, spot, layer, step_a, step_b = place_of(me)
@@ -661,6 +312,13 @@
         if part > 0:
             cross_b(0, spot_ab, part)
         cross_b(1, spot_b, part)
+    wanted = lax.broadcasted_iota(jnp.int32, (table.shape[0], 128), 0) + 1
+    for turn in range(n // fold):
+        ids = asked[turn * fold]
+        for k in range(1, fold):
+            ids = ids + asked[turn * fold + k]
+        found = ids[6:7].astype(jnp.int32) == wanted
+        picks[:, turn * 128 : (turn + 1) * 128] = jnp.where(found, 1.0, 0.0).astype(picks.dtype)
     arrived(spot_a)
     arrived(spot)
     for part in range(chunks):
@@ -668,6 +326,20 @@
         if part > 0:
             cross_z(part - 1)
     cross_z(chunks - 1)
+    lax.fori_loop(1, n, finish_rows, 0)
+    for copy in own_copies:
+        copy.wait()
+    table[...] = dot_nn(picks[...], came[...].reshape(picks.shape[1], -1))
+    squares = jnp.zeros((1, 1), jnp.float32)
+    for part in range(4):
+        rows = table.shape[0] // 4
+        piece = table[part * rows : (part + 1) * rows]
+        squares = squares + jnp.sum(piece * piece, keepdims=True)
+    norm = small_came[0]
+    for k in range(1, n):
+        norm = norm + small_came[k]
+    norm_piece[...] = norm
+    squares = squares + jnp.sum(norm * norm, keepdims=True)
     for part in range(chunks):
         cut = pl.ds(part * size, size)
 
@@ -690,8 +362,27 @@
         at += rows
     last = remote_copy(gone, back, f_send, f_recv, partner)
     last.start()
+    squares = squares + jnp.sum(out[:, here] * out[:, here], keepdims=True)
     last.wait()
     out[:, there] = back[...]
+    squares = squares + jnp.sum(back[...] * back[...], keepdims=True)
+    lane = lax.broadcasted_iota(jnp.int32, message.shape, 1)
+    message[...] = jnp.where(lane == 0, squares, jnp.where(lane == 1, loss_part[...], 0.0))
+
+    def tell(step):
+        peer = lax.rem(me + step, n)
+        return remote_copy(message, told.at[me], t_send.at[step], t_recv.at[step], peer)
+
+    def start_told(step, carry):
+        tell(step).start()
+        return carry
+
+    def wait_told(step, carry):
+        tell(step).wait()
+        return carry
+
+    lax.fori_loop(1, n, start_told, 0)
+    told[me] = message[...]
     for index in range(4):
         pltpu.make_async_copy(par.at[:, index], par.at[:, index], pair_send.at[index]).wait()
 
@@ -708,12 +399,14 @@
         return carry
 
     lax.fori_loop(0, layers, settle, 0)
-    lax.fori_loop(1, n, finish_rows, 0)
-    for copy in own_copies:
-        copy.wait()
-
-
-def to_owners(sent, small, grads, pieces, n, ident):
+    lax.fori_loop(1, n, wait_told, 0)
+    total_line = told[0]
+    for k in range(1, n):
+        total_line = total_line + told[k]
+    totals[...] = total_line
+
+
+def to_owners(sent, small, asked, loss_part, grads, pieces, rows_own, fold, n, ident):
     model = grads[0].shape[2]
     layers = n // 8
     units = [grad.shape[1] // 48 for grad in grads]
@@ -723,16 +416,18 @@
     low = jnp.bfloat16
     dma = pltpu.SemaphoreType.DMA
     anywhere = pl.BlockSpec(memory_space=pl.ANY)
+    vmem = pl.BlockSpec(memory_space=pltpu.VMEM)
     return pl.pallas_call(
-        partial(back_kernel, n, units, pieces, chunks),
+        partial(back_kernel, n, units, pieces, chunks, fold),
         name="back",
         out_shape=(
-            jax.ShapeDtypeStruct(sent.shape, sent.dtype),
-            jax.ShapeDtypeStruct(small.shape, small.dtype),
             jax.ShapeDtypeStruct((rows // 2, model), jnp.float32),
+            jax.ShapeDtypeStruct((rows_own, model), jnp.float32),
+            jax.ShapeDtypeStruct((8, 128), jnp.float32),
+            jax.ShapeDtypeStruct((8, 128), jnp.float32),
         ),
-        in_specs=[anywhere] * (2 + len(grads)),
-        out_specs=(anywhere, anywhere, pl.BlockSpec(memory_space=pltpu.VMEM)),
+        in_specs=[anywhere, anywhere, vmem, vmem] + [anywhere] * len(grads),
+        out_specs=(vmem,) * 4,
         scratch_shapes=[
             pltpu.VMEM((layers, 4, rows, half), low),
             pltpu.VMEM((layers, 4, rows, half), low),
@@ -742,6 +437,11 @@
             pltpu.VMEM((rows, half), jnp.float32),
             pltpu.VMEM((rows // 2, half), jnp.float32),
             pltpu.VMEM((rows // 2, half), jnp.float32),
+            pltpu.VMEM(sent.shape, low),
+            pltpu.VMEM(small.shape, jnp.float32),
+            pltpu.VMEM((rows_own, sent.shape[0] * sent.shape[1]), low),
+            pltpu.VMEM((8, 128), jnp.float32),
+            pltpu.VMEM((n, 8, 128), jnp.float32),
             dma((2, n)),
             dma((2, n)),
             dma((2,)),
@@ -756,6 +456,8 @@
             dma((layers, chunks)),
             dma,
             dma,
+            dma((n,)),
+            dma((n,)),
         ],
         compiler_params=pltpu.CompilerParams(
             collective_id=ident, has_side_effects=True, vmem_limit_bytes=60 * 2**20
@@ -763,65 +465,15 @@
         cost_estimate=pl.CostEstimate(
             flops=0, bytes_accessed=100 * 2**20, transcendentals=0
         ),
-    )(sent, small, *[grad.reshape(layers, 4, -1, model) for grad in grads])
+    )(sent, small, asked, loss_part, *[grad.reshape(layers, 4, -1, model) for grad in grads])
 
 
 def flat(rows):
     return rows.reshape(-1, rows.shape[-1])
 
 
-def enter_kernel(
-    full, target, mask_rows, mask_col, sines, cosines, gains, normed_out, white_out, scale_out, low_out, q, k, v, held, sem
-):
-    low = jnp.bfloat16
-    box_copy = pltpu.make_async_copy(full.at[:, pl.ds(0, 48)], held.at[:, pl.ds(0, 48)], sem.at[0])
-    mix_copy = pltpu.make_async_copy(full.at[:, pl.ds(144, 144)], held.at[:, pl.ds(48, 144)], sem.at[1])
-    box_copy.start()
-    mix_copy.start()
-    rows = jnp.where(mask_col[...] == 1.0, mask_rows[...], target[...])
-    boxes = jnp.concatenate([sines[...], cosines[...]], 1).astype(low)
-    box_copy.wait()
-    embedded = rows + dot_nt(boxes, flat(held[:, 0:48]))
-    normed, white, scale = layer_norm(embedded, gains[0:1], gains[1:2])
-    normed_out[...], white_out[...], scale_out[...] = normed, white, scale
-    normed = normed.astype(low)
-    low_out[...] = normed
-    mix_copy.wait()
-    for third, ref in enumerate((q, k, v)):
-        part = flat(held[:, 48 + 48 * third : 96 + 48 * third])
-        ref[...] = dot_nn(normed, part).astype(low)
-
-
-def enter(full, target, mask_rows, mask_col, sines, cosines, gains):
-    size, model = target.shape
-    low, wide = jnp.bfloat16, jnp.float32
-    vmem = pl.BlockSpec(memory_space=pltpu.VMEM)
-    shape = jax.ShapeDtypeStruct
-    return pl.pallas_call(
-        enter_kernel,
-        name="enter",
-        out_shape=(
-            shape((size, model), wide),
-            shape((size, model), wide),
-            shape((size, 1), wide),
-            shape((size, model), low),
-        )
-        + (shape((size, model), low),) * 3,
-        in_specs=[pl.BlockSpec(memory_space=pl.ANY)] + [vmem] * 6,
-        out_specs=(vmem,) * 7,
-        scratch_shapes=[
-            pltpu.VMEM((full.shape[0], 192, model), low),
-            pltpu.SemaphoreType.DMA((2,)),
-        ],
-        compiler_params=pltpu.CompilerParams(vmem_limit_bytes=56 * 2**20),
-        cost_estimate=pl.CostEstimate(
-            flops=8 * size * model * model, bytes_accessed=16 * 2**20, transcendentals=0
-        ),
-    )(full, target, mask_rows, mask_col, sines, cosines, gains)
-
-
 def upper_kernel(
-    page_rows, full, attended, normed, target, mask_col, page, row, share, gains,
+    page_rows, full, attended, normed, target, mask_col, page, row, asked, doc, gains,
     grads, d_attended, d_lower, pos_rows, norms, loss_part,
     held, bank, slopes, hidden, scores, load_sem, store_sem,
 ):
@@ -894,10 +546,13 @@
         scores[:, c * width : (c + 1) * width] = powers
         total = total + jnp.sum(powers, -1, keepdims=True)
     mask = mask_col[...]
-    loss_part[...] = share[0, 0] * jnp.sum(
+    facts = asked[:, 7, :]
+    counted = jnp.where(facts[:, 1:2] == doc[0].astype(jnp.float32), facts[:, 0:1], 0.0)
+    share = 1.0 / (DOCS * jnp.maximum(jnp.sum(counted, keepdims=True), 1.0))
+    loss_part[...] = share * jnp.sum(
         mask * (highest + jnp.log(total) - positive), keepdims=True
     )
-    factor = share[0, 0] * mask * inv_root
+    factor = share * mask * inv_root
     positive_grad = factor * (lead / total - 1.0)
     factor = factor / total
     pos_rows[...] = (positive_grad * states.astype(jnp.float32)).astype(pos_rows.dtype)
@@ -939,7 +594,7 @@
         copy.wait()
 
 
-def upper(full, attended, normed, target, mask_col, page, row, share, gains, blocks, page_rows):
+def upper(full, attended, normed, target, mask_col, page, row, asked, doc, gains, blocks, page_rows):
     size, model = normed.shape
     chips = full.shape[0]
     used = full.shape[1] - 288 - 2 * page_rows
@@ -959,7 +614,7 @@
             shape((1, 1), wide),
         ),
         in_specs=[anywhere]
-        + [vmem] * 6
+        + [vmem] * 7
         + [pl.BlockSpec(memory_space=pltpu.SMEM), vmem],
         out_specs=(anywhere,) + (vmem,) * 5,
         scratch_shapes=[
@@ -975,16 +630,16 @@
         cost_estimate=pl.CostEstimate(
             flops=20 * 10**9, bytes_accessed=32 * 2**20, transcendentals=4 * size * model * 2
         ),
-    )(full, attended, normed, target, mask_col, page, row, share, gains)
+    )(full, attended, normed, target, mask_col, page, row, asked, doc, gains)
 
 
 def lower_kernel(
-    fixed, full, dq, dk, dv, d_lower, white, scale, gains, normed, sines, cosines, mask_col, pos_rows, place,
-    grads, d_embedded, sent, norms, held, sem,
+    fixed, full, dq, dk, dv, d_lower, white, scale, gains, normed, sines, cosines, mask_col, pos_rows, place, upper_norms,
+    grads, sent, norms, held, sem,
 ):
     low = jnp.bfloat16
     chips, _, model = held.shape
-    load = pltpu.make_async_copy(full.at[:, pl.ds(144, 144)], held.at[:, pl.ds(48, 144)], sem.at[0])
+    load = pltpu.make_async_copy(full.at[:, pl.ds(48, 144)], held.at[:, pl.ds(48, 144)], sem.at[0])
     load.start()
     mask = mask_col[...]
     d_first = d_lower[...]
@@ -1000,12 +655,16 @@
         )
         stores[-1].start()
     d_rows, gain, bias = norm_back(d_first, white[...], scale[...], gains[0:1])
-    d_embedded[...] = d_rows
     boxes = jnp.concatenate([sines[...], cosines[...]], 1).astype(low)
     held[:, 0:48] = dot_tn(d_rows.astype(low), boxes).astype(low).reshape(chips, 48, model)
     stores.append(pltpu.make_async_copy(held.at[:, pl.ds(0, 48)], grads.at[:, pl.ds(0, 48)], sem.at[4]))
     stores[-1].start()
-    norms[0:1], norms[1:2] = gain, bias
+    count = norms.shape[0]
+    lines = jnp.concatenate([gain, bias, upper_norms[...]], 0)
+    cols = model // count
+    norms[...] = jnp.zeros_like(norms)
+    for owner in range(count):
+        norms[owner, 0:6, 0:cols] = lines[:, owner * cols : (owner + 1) * cols]
     token_grads = jnp.where(mask == 1.0, pos_rows[...].astype(jnp.float32), d_rows).astype(low)
     mask_grad = jnp.sum(mask * d_rows, 0, keepdims=True)
     slots = sent.shape[0]
@@ -1018,7 +677,8 @@
 
 
 def lower(
-    full, d_joined, d_lower, white, scale, gains, normed, sines, cosines, mask_col, pos_rows, place, slots, fixed
+    full, d_joined, d_lower, white, scale, gains, normed, sines, cosines, mask_col, pos_rows, place,
+    upper_norms, n, slots, fixed,
 ):
     size, model = d_lower.shape
     chips = full.shape[0]
@@ -1031,12 +691,11 @@
         name="lower",
         out_shape=(
             shape((chips, 192, model), low),
-            shape((size, model), wide),
             shape((slots, model), low),
-            shape((2, model), wide),
+            shape((n, 8, 128), wide),
         ),
-        in_specs=[anywhere] + [vmem] * 13,
-        out_specs=(anywhere,) + (vmem,) * 3,
+        in_specs=[anywhere] + [vmem] * 14,
+        out_specs=(anywhere,) + (vmem,) * 2,
         scratch_shapes=[
             pltpu.VMEM((chips, 192, model), low),
             pltpu.SemaphoreType.DMA((5,)),
@@ -1045,66 +704,7 @@
         cost_estimate=pl.CostEstimate(
             flops=6 * 10**9, bytes_accessed=24 * 2**20, transcendentals=0
         ),
-    )(full, *d_joined, d_lower, white, scale, gains, normed, sines, cosines, mask_col, pos_rows, place)
-
-
-def totals_kernel(n, table, sums, norm_came, loss_part, out, norm_piece, message, came, send_sem, recv_sem):
-    me = lax.axis_index("dp")
-    square = jnp.sum(sums[...] * sums[...], keepdims=True)
-    for part in range(4):
-        rows = table.shape[0] // 4
-        piece = table[part * rows : (part + 1) * rows]
-        square = square + jnp.sum(piece * piece, keepdims=True)
-    norm = norm_came[0]
-    for k in range(1, n):
-        norm = norm + norm_came[k]
-    norm_piece[...] = norm
-    square = square + jnp.sum(norm * norm, keepdims=True)
-    lane = lax.broadcasted_iota(jnp.int32, message.shape, 1)
-    message[...] = jnp.where(lane == 0, square, jnp.where(lane == 1, loss_part[...], 0.0))
-    greet_everyone(me, n)
-
-    def copy(step):
-        peer = lax.rem(me + step, n)
-        return remote_copy(message, came.at[me], send_sem.at[step], recv_sem.at[step], peer)
-
-    def start(step, carry):
-        copy(step).start()
-        return carry
-
-    def finish(step, carry):
-        copy(step).wait()
-        return carry
-
-    lax.fori_loop(1, n, start, 0)
-    came[me] = message[...]
-    lax.fori_loop(1, n, finish, 0)
-    total = came[0]
-    for k in range(1, n):
-        total = total + came[k]
-    out[...] = total
-
-
-def sum_totals(table, sums, norm_came, loss_part, n, ident):
-    vmem = pl.BlockSpec(memory_space=pltpu.VMEM)
-    tile = jax.ShapeDtypeStruct((8, 128), jnp.float32)
-    return pl.pallas_call(
-        partial(totals_kernel, n),
-        name="totals",
-        out_shape=(tile, tile),
-        in_specs=[vmem] * 4,
-        out_specs=(vmem,) * 2,
-        scratch_shapes=[
-            pltpu.VMEM((8, 128), jnp.float32),
-            pltpu.VMEM((n, 8, 128), jnp.float32),
-            pltpu.SemaphoreType.DMA((n,)),
-            pltpu.SemaphoreType.DMA((n,)),
-        ],
-        compiler_params=pltpu.CompilerParams(
-            collective_id=ident, has_side_effects=True, vmem_limit_bytes=32 * 2**20
-        ),
-        cost_estimate=pl.CostEstimate(flops=0, bytes_accessed=8 * 2**20, transcendentals=0),
-    )(table, sums, norm_came, loss_part)
+    )(full, *d_joined, d_lower, white, scale, gains, normed, sines, cosines, mask_col, pos_rows, place, upper_norms)
 
 
 def update_kernel(decay, layout, factor, table, sums, *refs):
@@ -1129,7 +729,7 @@
             for block in range(blocks):
                 piece = sums[at + block * rows : at + (block + 1) * rows]
                 if turned:
-                    update(k, swap_middle(piece.T), learn_rate, (slice(None), slice(None)))
+                    update(k, swap_middle(piece, 1), learn_rate, (slice(None), slice(None)))
                 else:
                     cut = (slice(None), slice(block * model, (block + 1) * model))
                     update(k, piece, learn_rate, cut)
@@ -1201,9 +801,7 @@
     return jnp.where(lane < HD, low_half, high_half)
 
 
-def attend_kernel(q, k, v, rel_text, rel_box, sines, cosines, bases, attended, probs):
-    queries, keys, values = q[...], k[...], v[...]
-    spread = bases[...]
+def attend_pair(queries, keys, values, rel_text, rel_box, sines, cosines, spread, probs):
     results = []
     for half in range(2):
         mine = masked(queries, half)
@@ -1217,7 +815,13 @@
         shares = powers * (1.0 / jnp.sum(powers, -1, keepdims=True))
         probs[half] = shares
         results.append(dot_nn(shares.astype(jnp.bfloat16), values))
-    attended[...] = pick_halves(*results).astype(jnp.bfloat16)
+    return pick_halves(*results).astype(jnp.bfloat16)
+
+
+def attend_kernel(q, k, v, rel_text, rel_box, sines, cosines, bases, attended, probs):
+    attended[...] = attend_pair(
+        q[...], k[...], v[...], rel_text, rel_box, sines, cosines, bases[...], probs
+    )
 
 
 def attend(joined, rel_map, sines, cosines, bases):
@@ -1306,11 +910,421 @@
     )(d_attended, *joined, rel_map, rel_map, probs, sines, cosines, bases)
 
 
-def swap_middle(rows):
-    count = rows.shape[0] // 4
-    return jnp.concatenate(
-        [rows[:count], rows[2 * count : 3 * count], rows[count : 2 * count], rows[3 * count :]], 0
-    )
+def ahead_kernel(n, units, early, capacity, *refs):
+    count = len(units)
+    lists, vocabulary, pages, points, omegas, place, mask_col = refs[:7]
+    weights = refs[7 : 7 + count]
+    outs = refs[7 + count : 23 + count]
+    asked, full, probs, sines, cosines, bases, target_out, normed_out, white_out, scale_out, low_out = outs[:11]
+    q, k, v, attended, gains = outs[11:]
+    swap_out, swap_in, chip_rows, answers, rows, held, rel_map, shares = refs[23 + count : 31 + count]
+    ask_send, ask_recv, row_send, row_recv, own_sem, swap_send, swap_recv = refs[31 + count : 38 + count]
+    hop_recv, core_recv, core_send, z_send, a_send, b_send, load_sem, out_sem = refs[38 + count :]
+    low = jnp.bfloat16
+    me = lax.axis_index("dp")
+    core, spot, layer, step_a, step_b = place_of(me)
+    layers = n // 8
+    half = chip_rows.shape[1]
+    page_rows = pages.shape[0]
+    here = pl.ds(pl.multiple_of(core * half, 128), half)
+    there = pl.ds(pl.multiple_of((1 - core) * half, 128), half)
+    partner = me + 1 - 2 * core
+    to_a, to_b, up, down = me + 2 * step_a, me + 2 * step_b, me + 8, me - 8
+    spot_a, spot_b, spot_ab = spot + step_a, spot + step_b, spot + step_a + step_b
+    low_z, high_z = layer > 0, layer < layers - 1
+    cuts = (pl.ds(0, early), pl.ds(early, chip_rows.shape[0] - early))
+
+    at = 0
+    for ref, unit in zip(weights, units):
+        swap_out[pl.ds(at, 24 * unit)] = ref[:, there]
+        at += 24 * unit
+    greet_everyone(me, n)
+    swaps = [
+        remote_copy(swap_out, swap_in, swap_send.at[0], swap_recv.at[0], partner),
+        remote_copy(
+            pages.at[:, there],
+            chip_rows.at[pl.ds(2 * at + core * page_rows, page_rows)],
+            swap_send.at[1],
+            swap_recv.at[1],
+            partner,
+        ),
+    ]
+    for copy in swaps:
+        copy.start()
+
+    def ask(step):
+        peer = lax.rem(me + step, n)
+        return remote_copy(lists.at[peer], asked.at[me], ask_send.at[step], ask_recv.at[step], peer)
+
+    def start_ask(step, carry):
+        ask(step).start()
+        return carry
+
+    def wait_ask(step, carry):
+        ask(step).wait()
+        return carry
+
+    lax.fori_loop(1, n, start_ask, 0)
+    asked[me] = lists[me]
+    chip_rows[pl.ds(2 * at + pl.multiple_of(core * page_rows, page_rows), page_rows)] = pages[:, here]
+    for copy in swaps:
+        copy.wait_recv()
+    at = 0
+    for ref, unit in zip(weights, units):
+        mine, other = ref[:, here], swap_in[pl.ds(at, 24 * unit)]
+        ordered = jnp.where(
+            core == 0, jnp.concatenate([mine, other], 0), jnp.concatenate([other, mine], 0)
+        )
+        chip_rows[pl.ds(2 * at, 48 * unit)] = ordered.astype(low)
+        at += 24 * unit
+
+    def block(g, level, index):
+        return full.at[level, index, cuts[g], here]
+
+    def z_hop(g, way, level, src=None):
+        return remote_copy(
+            block(g, level, spot) if src is None else src, block(g, level, spot),
+            z_send.at[g, way, level], hop_recv.at[g, level, spot], up if way == 0 else down,
+        )
+
+    def a_hop(g, level, src=None):
+        return remote_copy(
+            block(g, level, spot) if src is None else src, block(g, level, spot),
+            a_send.at[g, level], hop_recv.at[g, level, spot], to_a,
+        )
+
+    def b_hop(g, kind, level, src=None):
+        index = spot if kind == 0 else spot_a
+        return remote_copy(
+            block(g, level, index) if src is None else src, block(g, level, index),
+            b_send.at[g, kind, level], hop_recv.at[g, level, index], to_b,
+        )
+
+    def core_hop(g, level, index, src=None):
+        return remote_copy(
+            block(g, level, index) if src is None else src, block(g, level, index),
+            core_send.at[g, level, index], core_recv.at[g, level, index], partner,
+        )
+
+    def arrived(g, level, index):
+        view = block(g, level, index)
+        pltpu.make_async_copy(view, view, hop_recv.at[g, level, index]).wait()
+
+    def own_copy(g):
+        return pltpu.make_async_copy(chip_rows.at[cuts[g]], block(g, layer, spot), own_sem.at[g])
+
+    def send_own(g):
+        src = chip_rows.at[cuts[g]]
+
+        @pl.when(high_z)
+        def _():
+            z_hop(g, 0, layer, src).start()
+
+        @pl.when(low_z)
+        def _():
+            z_hop(g, 1, layer, src).start()
+
+        a_hop(g, layer, src).start()
+        b_hop(g, 0, layer, src).start()
+        core_hop(g, layer, spot, src).start()
+        own_copy(g).start()
+
+    def relay_column(g, gap):
+        for way, level, there_is, further in (
+            (0, layer - gap, layer - gap >= 0, high_z),
+            (1, layer + gap, layer + gap < layers, low_z),
+        ):
+
+            @pl.when(there_is)
+            def _():
+                arrived(g, level, spot)
+
+                @pl.when(further)
+                def _():
+                    z_hop(g, way, level).start()
+
+                a_hop(g, level).start()
+                b_hop(g, 0, level).start()
+                core_hop(g, level, spot).start()
+
+    def at_gap(gap, visit):
+        if gap == 0:
+            visit(layer)
+            return
+
+        @pl.when(layer - gap >= 0)
+        def _():
+            visit(layer - gap)
+
+        @pl.when(layer + gap < layers)
+        def _():
+            visit(layer + gap)
+
+    def relay_a(g, gap):
+        def visit(level):
+            arrived(g, level, spot_a)
+            b_hop(g, 1, level).start()
+            core_hop(g, level, spot_a).start()
+
+        at_gap(gap, visit)
+
+    def relay_b(g, gap):
+        for index in (spot_b, spot_ab):
+
+            def visit(level):
+                arrived(g, level, index)
+                core_hop(g, level, index).start()
+
+            at_gap(gap, visit)
+
+    def relays(g):
+        steps = [lambda: relay_a(g, 0)]
+        for gap in range(1, layers):
+            steps.append(lambda gap=gap: relay_column(g, gap))
+            steps.append(lambda gap=gap: relay_a(g, gap))
+            steps.append(lambda gap=gap: relay_b(g, gap - 1))
+        steps.append(lambda: relay_b(g, layers - 1))
+        return steps
+
+    def gathered(g):
+        def wait(level, carry):
+            for index in range(4):
+                view = full.at[level, index, cuts[g], there]
+                pltpu.make_async_copy(view, view, core_recv.at[g, level, index]).wait()
+            return carry
+
+        lax.fori_loop(0, layers, wait, 0)
+        own_copy(g).wait()
+
+    send_own(0)
+
+    lax.fori_loop(1, n, wait_ask, 0)
+    rows_own = vocabulary.shape[0]
+    table = vocabulary[...].astype(low)
+    group = 128 // capacity
+
+    def row_copy(peer):
+        return remote_copy(
+            answers.at[peer], rows.at[me], row_send.at[peer], row_recv.at[me], peer
+        )
+
+    def answer(turn, carry):
+        ids = jnp.zeros((8, 128), jnp.float32)
+        for j in range(group):
+            ids = ids + asked[turn * group + j]
+        ids = ids.T[:, 6:7]
+        wanted = lax.broadcasted_iota(jnp.int32, (128, rows_own), 1) + 1
+        picks = jnp.where(ids.astype(jnp.int32) == wanted, 1.0, 0.0).astype(low)
+        found = dot_nn(picks, table).astype(low)
+        for j in range(group):
+            peer = turn * group + j
+            answers[peer] = found[j * capacity : (j + 1) * capacity]
+
+            @pl.when(peer != me)
+            def _():
+                row_copy(peer).start()
+
+        return carry
+
+    lax.fori_loop(0, n // group, answer, 0)
+    first = relays(0)
+    rest = relays(1)
+    for step in first[:2]:
+        step()
+    send_own(1)
+    rows[me] = answers[me]
+    cols = gains.shape[1] // n
+    for source in range(n):
+        gains[:, source * cols : (source + 1) * cols] = (
+            asked[source, :, 0:cols].astype(low).astype(jnp.float32)
+        )
+    lane = lax.broadcasted_iota(jnp.int32, sines.shape, 1)
+    angles = jnp.where(lane < sines.shape[1] // 2, points[:, 0:1], points[:, 1:2]) * omegas[...]
+    sines[...] = jnp.sin(angles)
+    cosines[...] = jnp.cos(angles)
+    boxes = jnp.concatenate([sines[...], cosines[...]], 1).astype(low)
+    bases[...] = jnp.concatenate([cosines[...], sines[...]], 1).astype(low)
+    for step in (*first[2:6], *rest[:2], *first[6:9], *rest[2:3], *first[9:], rest[4]):
+        step()
+    gathered(0)
+    map_copy = pltpu.make_async_copy(full.at[:, :, pl.ds(0, 192)], held, load_sem.at[0])
+    map_copy.start()
+    deep = (early - 192) if early > 192 else 0
+    for chip in range(4 * layers):
+        pltpu.make_async_copy(
+            full.at[chip // 4, chip % 4, pl.ds(192, deep)], rel_map.at[pl.ds(chip * deep, deep)], load_sem.at[1]
+        ).start()
+
+    def wait_row(step, carry):
+        source = lax.rem(me - step + n, n)
+        pltpu.make_async_copy(rows.at[source], rows.at[source], row_recv.at[source]).wait()
+        return carry
+
+    lax.fori_loop(1, n, wait_row, 0)
+    slots = n * capacity
+    seats = lax.broadcasted_iota(jnp.int32, (place.shape[0], slots), 1) == place[...]
+    target = dot_nn(jnp.where(seats, 1.0, 0.0).astype(low), rows[...].reshape(slots, -1))
+    target_out[...] = target
+    mask_owner, mask_slot = mask_token // rows_own, capacity - 1
+    mask_row = rows[mask_owner, mask_slot : mask_slot + 1].astype(jnp.float32)
+    entry = jnp.where(mask_col[...] == 1.0, mask_row, target)
+    map_copy.wait()
+    model = target.shape[1]
+
+    def weight(at):
+        return held[:, :, at : at + 48].reshape(-1, model)
+
+    embedded = entry + dot_nt(boxes, weight(0))
+    normed, white, scale = layer_norm(embedded, gains[0:1], gains[1:2])
+    normed_out[...], white_out[...], scale_out[...] = normed, white, scale
+    normed = normed.astype(low)
+    low_out[...] = normed
+    for third, ref in enumerate((q, k, v)):
+        ref[...] = dot_nn(normed, weight(48 + 48 * third)).astype(low)
+    rest[5]()
+    pltpu.make_async_copy(rel_map, rel_map, load_sem.at[1]).wait()
+    pairs = model // (2 * HD)
+    turns = [[] for _ in range(pairs)]
+    for at, which in zip((0, 1, 2, 3, 5), (7, 3, 6, 8, 9)):
+        turns[min(at, pairs - 1)].append(rest[which])
+
+    def shares_copy(pair):
+        slot = lax.rem(pair, 2)
+        return pltpu.make_async_copy(shares.at[slot], probs.at[pl.ds(2 * pair, 2)], out_sem.at[slot])
+
+    def attend(pair, carry):
+        for turn in range(pairs):
+
+            @pl.when(pair == turn)
+            def _():
+                for step in turns[turn]:
+                    step()
+
+        @pl.when(pair >= 2)
+        def _():
+            shares_copy(pair - 2).wait()
+
+        lanes = pl.ds(pl.multiple_of(pair * 2 * HD, 2 * HD), 2 * HD)
+        band = pl.ds(pl.multiple_of(pair * 2 * HD, 2 * HD), 2 * HD)
+        other = pl.ds(pl.multiple_of(model + pair * 2 * HD, 2 * HD), 2 * HD)
+        slot = lax.rem(pair, 2)
+        result = attend_pair(
+            q[:, lanes], k[:, lanes], v[:, lanes], rel_map.at[band], rel_map.at[other],
+            sines, cosines, bases[...], shares.at[slot],
+        )
+        attended[:, lanes] = result
+        shares_copy(pair).start()
+        return carry
+
+    lax.fori_loop(0, pairs, attend, 0)
+    shares_copy(pairs - 2).wait()
+    shares_copy(pairs - 1).wait()
+    rest[10]()
+    gathered(1)
+
+    def finish(level, carry):
+        for g in range(2):
+            for index in (spot, spot_a, spot_b, spot_ab):
+                core_hop(g, level, index).wait_send()
+            a_hop(g, level).wait_send()
+            b_hop(g, 0, level).wait_send()
+            b_hop(g, 1, level).wait_send()
+
+            @pl.when((level <= layer) & high_z)
+            def _():
+                z_hop(g, 0, level).wait_send()
+
+            @pl.when((level >= layer) & low_z)
+            def _():
+                z_hop(g, 1, level).wait_send()
+
+        return carry
+
+    lax.fori_loop(0, layers, finish, 0)
+    for copy in swaps:
+        copy.wait_send()
+
+    def finish_rows(step, carry):
+        peer = lax.rem(me + step, n)
+        pltpu.make_async_copy(answers.at[peer], answers.at[peer], row_send.at[peer]).wait()
+        return carry
+
+    lax.fori_loop(1, n, finish_rows, 0)
+
+
+def ahead(lists, vocabulary, pages, positions, place, mask_col, weights, early, n, capacity, ident):
+    model = vocabulary.shape[1]
+    size = place.shape[0]
+    layers = n // 8
+    units = [weight.shape[0] // 24 for weight in weights]
+    points = positions.astype(jnp.float32).T
+    waves = model // 4
+    omegas = jnp.power(10000.0, -jnp.arange(waves).astype(jnp.float32) / waves)
+    omegas = jnp.concatenate([omegas, omegas])[None]
+    swap = 24 * sum(units)
+    chip = 2 * (swap + pages.shape[0])
+    low, wide = jnp.bfloat16, jnp.float32
+    dma = pltpu.SemaphoreType.DMA
+    vmem = pl.BlockSpec(memory_space=pltpu.VMEM)
+    anywhere = pl.BlockSpec(memory_space=pl.ANY)
+    shape = jax.ShapeDtypeStruct
+    rows = lambda kind: shape((size, model), kind)
+    heads = model // HD
+    return pl.pallas_call(
+        partial(ahead_kernel, n, units, early, capacity),
+        name="ahead",
+        out_shape=(
+            shape(lists.shape, lists.dtype),
+            shape((layers, 4, chip, model), low),
+            shape((heads, size, size), wide),
+            shape((size, 2 * waves), wide),
+            shape((size, 2 * waves), wide),
+            rows(low),
+            rows(wide),
+            rows(wide),
+            rows(wide),
+            shape((size, 1), wide),
+            rows(low),
+            rows(low),
+            rows(low),
+            rows(low),
+            rows(low),
+            shape((8, model), wide),
+        ),
+        in_specs=[vmem] * (7 + len(weights)),
+        out_specs=(vmem, anywhere, anywhere) + (vmem,) * 13,
+        scratch_shapes=[
+            pltpu.VMEM((swap, model // 2), wide),
+            pltpu.VMEM((swap, model // 2), wide),
+            pltpu.VMEM((chip, model // 2), low),
+            pltpu.VMEM((n, capacity, model), low),
+            pltpu.VMEM((n, capacity, model), low),
+            pltpu.VMEM((layers, 4, 192, model), low),
+            pltpu.VMEM((2 * model, model), low),
+            pltpu.VMEM((2, 2, size, size), wide),
+            dma((n,)),
+            dma((n,)),
+            dma((n,)),
+            dma((n,)),
+            dma((2,)),
+            dma((2,)),
+            dma((2,)),
+            dma((2, layers, 4)),
+            dma((2, layers, 4)),
+            dma((2, layers, 4)),
+            dma((2, 2, layers)),
+            dma((2, layers)),
+            dma((2, 2, layers)),
+            dma((2,)),
+            dma((2,)),
+        ],
+        compiler_params=pltpu.CompilerParams(
+            collective_id=ident, has_side_effects=True, vmem_limit_bytes=62 * 2**20
+        ),
+        cost_estimate=pl.CostEstimate(
+            flops=13 * 10**9, bytes_accessed=100 * 2**20, transcendentals=0
+        ),
+    )(lists, vocabulary, pages, points, omegas, place, mask_col, *weights)
 
 
 def forward(weights, rows, positions):
@@ -1429,117 +1443,79 @@
     average_narrowing,
     average_scaling,
 ):
-    me = lax.axis_index("dp")
     size = tokens.shape[0]
     rows_own, model = vocabulary.shape
     page_rows = pages.shape[1]
-    capacity = max(16, -(-2 * size // n) // 16 * 16)
-    slots = n * capacity
     mask_float = masking.astype(jnp.float32)
+    mask_col = mask_float[:, None]
     low = jnp.bfloat16
-    fits = n % 8 == 0 and merging.shape[0] == 24 and page_rows % 16 == 0
-
-    fold = 128 // capacity if fits else 1
+    blocks = widening.shape[1] // model
+    decay = min(average_cap, (1.0 + STEP) / (10.0 + STEP))
+    masters = (vocabulary, geometry, mixing, relative, merging, widening, narrowing, scaling)
+    moments = (
+        moment_vocabulary,
+        moment_geometry,
+        moment_mixing,
+        moment_relative,
+        moment_merging,
+        moment_widening,
+        moment_narrowing,
+        moment_scaling,
+    )
+    averages = (
+        average_vocabulary,
+        average_geometry,
+        average_mixing,
+        average_relative,
+        average_merging,
+        average_widening,
+        average_narrowing,
+        average_scaling,
+    )
     pieces = [
         swap_middle(geometry).T,
+        *[mixing[:, k * model : (k + 1) * model] for k in range(3)],
         swap_middle(relative).T,
-        *[mixing[:, k * model : (k + 1) * model] for k in range(3)],
         merging,
-        *[widening[:, k * model : (k + 1) * model] for k in range(widening.shape[1] // model)],
+        *[widening[:, k * model : (k + 1) * model] for k in range(blocks)],
         narrowing,
     ]
-    cols = scaling.shape[1]
-    info = jnp.pad(scaling, ((1, 1), (0, 128 - cols)))
-    lists, place = make_plan(tokens, masking, documents, info, n, rows_own, capacity, fold)
     bank_piece = pages.reshape(-1, model)
-    if fits:
-        asked, table_rows, full, sines, cosines = front(
-            lists, vocabulary, bank_piece, positions, pieces, n, capacity, 1
-        )
-        full = full.reshape(-1, *full.shape[2:])
-        wanted = jnp.sum(asked[:, 0].reshape(n // fold, fold, 128), 1)
-    else:
-        (asked,) = exchange([lists], 1, "ask")
-        wanted = asked[:, 0, :capacity]
-        pieces = [piece.astype(low) for piece in pieces] + [bank_piece]
-        joined = lax.all_gather(jnp.concatenate(pieces, 0), "dp", axis=0, tiled=False)
+
+    def step(master, moment, average, piece, rate, factor):
+        clipped = piece * factor
+        velocity = momentum_decay * moment + clipped
+        updated = master - rate * (clipped + momentum_decay * velocity)
+        return updated, velocity, decay * average + (1.0 - decay) * updated
+
+    def dense():
+        chosen = (documents[0] == jnp.arange(DOCS)).astype(jnp.float32)
+        counts = lax.psum(chosen * jnp.sum(mask_float), "dp")
+        share = jnp.sum(chosen / (DOCS * jnp.maximum(counts, 1.0)))
+        cast = [piece.astype(low) for piece in pieces] + [bank_piece]
+        joined = lax.all_gather(jnp.concatenate(cast, 0), "dp", axis=0, tiled=False)
         weights, at = [], 0
-        for piece in pieces:
+        for piece in cast:
             weights.append(joined[:, at : at + piece.shape[0]].reshape(-1, model))
             at += piece.shape[0]
-    wanted = wanted.reshape(slots, 1)
-    picks = (wanted == (jnp.arange(rows_own) + 1).astype(jnp.float32)[None, :]).astype(low)
-    if not fits:
-        answer = dot_nn(picks, vocabulary.astype(low)).astype(low)
-        (table_rows,) = exchange([answer.reshape(n, capacity, model)], 2, "rows")
-    table_rows = table_rows.reshape(slots, model)
-    norm_rows = asked[:, 1:7, :cols].transpose(1, 0, 2).reshape(6, n * cols).astype(low)
-    count_of, doc_of = asked[:, 7, 0], asked[:, 7, 1]
-    overflow = jnp.max(asked[:, 7, 2]) > 0.0
-    my_count = jnp.sum(jnp.where(doc_of == documents[0].astype(jnp.float32), count_of, 0.0))
-    share = 1.0 / (DOCS * jnp.maximum(my_count, 1.0))
-    fixed = (mask_token // rows_own) * capacity + capacity - 1
-    seats = (place == jnp.arange(slots)[None, :]).astype(low)
-    target_rows = dot_nn(seats, table_rows)
-    mask_rows = table_rows[fixed : fixed + 1].astype(jnp.float32)
-
-    def dense_rows():
-        table = lax.all_gather(vocabulary.astype(low), "dp", axis=0, tiled=True)
-        return (
-            table[tokens].astype(jnp.float32),
-            table[mask_token : mask_token + 1].astype(jnp.float32),
-        )
-
-    target_rows, mask_rows = lax.cond(overflow, dense_rows, lambda: (target_rows, mask_rows))
-    mask_col = mask_float[:, None]
-    if fits:
-        gains = norm_rows.astype(jnp.float32)
-        rel_map = full[:, 48:144].reshape(-1, model)
-        bases = jnp.concatenate([cosines, sines], -1).astype(low)
-        normed, white, scale, normed_low, *joined = enter(
-            full, target_rows, mask_rows, mask_col, sines, cosines, gains
-        )
-        attended, probs = attend(joined, rel_map, sines, cosines, bases)
-        blocks = widening.shape[1] // model
-        upper_grads, d_attended, d_lower, positive_rows, upper_norms, loss_part = upper(
-            full,
-            attended,
-            normed,
-            target_rows,
-            mask_col,
-            negative_page,
-            negative_row,
-            share.reshape(1, 1),
-            gains,
-            blocks,
-            page_rows,
-        )
-        *d_joined, grad_rel = attend_back(
-            d_attended, joined, rel_map, probs, sines, cosines, bases
-        )
-        lower_grads, d_embedded, sent, lower_norms = lower(
-            full,
-            d_joined,
-            d_lower,
-            white,
-            scale,
-            gains,
-            normed_low,
-            sines,
-            cosines,
-            mask_col,
-            positive_rows,
-            place,
-            slots,
-            fixed,
-        )
-        grad_norms = jnp.concatenate([lower_norms, upper_norms], 0)
-        positive_rows = positive_rows.astype(jnp.float32)
-    else:
-        box_map, rel_map, mix_map = weights[0], weights[1], weights[2:5]
-        out_map, up_map, down_full, bank = weights[5], weights[6:-2], weights[-2], weights[-1]
-        entry_rows = jnp.where(masking[:, None] == 1, mask_rows, target_rows)
-
+        norm_rows = lax.all_gather(scaling.astype(low), "dp", axis=1, tiled=True)
+        entry = jnp.where(masking == 1, mask_token, tokens)
+        lanes = 4
+
+        def split(rows):
+            return rows.reshape(rows.shape[0], lanes, -1).transpose(1, 0, 2)
+
+        def join(rows):
+            return rows.transpose(1, 0, 2).reshape(rows.shape[1], -1)
+
+        def named_rows(part):
+            table = lax.all_gather(part, "dp", axis=0, tiled=True)
+            return table[tokens], table[entry]
+
+        found = lax.map(named_rows, split(vocabulary.astype(low)))
+        target_rows, entry_rows = [join(rows).astype(jnp.float32) for rows in found]
+        box_map, mix_map, rel_map, out_map = weights[0], weights[1:4], weights[4], weights[5]
+        up_map, down_full, bank = weights[6:-2], weights[-2], weights[-1]
         ff = len(up_map)
         down_map = [down_full[k * model : (k + 1) * model] for k in range(ff)]
         weights = (box_map, mix_map, rel_map, out_map, up_map, down_map, norm_rows)
@@ -1559,7 +1535,6 @@
         lead = jnp.exp(positive - highest)
         total = jnp.sum(powers, -1, keepdims=True) + lead
         per_token = highest + jnp.log(total) - positive
-        mask_col = mask_float[:, None]
         loss_part = share * jnp.sum(mask_col * per_token)
         weight_map = (powers * (share * mask_col / total) * inv_root).astype(low)
         positive_grad = share * mask_col * (lead / total - 1.0) * inv_root
@@ -1572,110 +1547,130 @@
             weights, cache, d_lower, d_attended
         )
         grad_norms = jnp.concatenate(lower_norms + upper_norms, 0)
-
         positive_rows = positive_grad * states_low.astype(jnp.float32)
-        token_grads = jnp.where(mask_col == 1.0, positive_rows, d_embedded).astype(low)
-        mask_grad = jnp.sum(mask_col * d_embedded, 0, keepdims=True)
-        sent = dot_tn(seats, token_grads)
-        sent = jnp.where(jnp.arange(slots)[:, None] == fixed, mask_grad, sent).astype(low)
-
-    norm_blocks = grad_norms.reshape(6, n, cols).transpose(1, 0, 2)
-    norm_blocks = jnp.pad(norm_blocks, ((0, 0), (0, 2), (0, 128 - cols)))
-    sent = sent.reshape(n, capacity, model)
-    if fits:
-        grads = [lower_grads, grad_rel.reshape(n // 2, -1, model), upper_grads]
-        parts = (1, 1, 1, 1, 2, 1) + (1,) * blocks + (narrowing.shape[0] // 24,)
-        came, norm_came, sums = to_owners(sent, norm_blocks, grads, parts, n, 2)
-    else:
-        came, norm_came = exchange([sent, norm_blocks], 3, "grads")
-        grads = [grad_box, grad_rel.reshape(-1, model), *grad_mix, grad_out, *grad_up]
+
+        def summed_rows(parts):
+            whole = jnp.zeros((rows_own * n, model // lanes), jnp.float32)
+            whole = whole.at[entry].add(parts[0]).at[tokens].add(parts[1])
+            return lax.psum_scatter(whole, "dp", scatter_dimension=0, tiled=True)
+
+        table_piece = join(lax.map(summed_rows, (split(d_embedded), split(positive_rows))))
+        norm_piece = lax.psum_scatter(grad_norms, "dp", scatter_dimension=1, tiled=True)
+        grads = [grad_box, *grad_mix, grad_rel.reshape(-1, model), grad_out, *grad_up]
         grads = [grad.astype(low) for grad in [*grads, jnp.concatenate(grad_down, 0)]]
         sums = scatter(grads, n)
-
-    def sparse_table():
-        return dot_tn(picks, came.reshape(slots, model))
-
-    def dense_table():
-        entry = jnp.where(masking == 1, mask_token, tokens)
-        table_grad = jnp.zeros((rows_own * n, model), jnp.float32).at[entry].add(d_embedded)
-        table_grad = table_grad.at[tokens].add(positive_rows)
-        return lax.psum_scatter(table_grad, "dp", scatter_dimension=0, tiled=True)
-
-    table_piece = lax.cond(overflow, dense_table, sparse_table)
-
-    masters = (vocabulary, geometry, mixing, relative, merging, widening, narrowing, scaling)
-    moments = (
-        moment_vocabulary,
-        moment_geometry,
-        moment_mixing,
-        moment_relative,
-        moment_merging,
-        moment_widening,
-        moment_narrowing,
-        moment_scaling,
-    )
-    averages = (
-        average_vocabulary,
-        average_geometry,
-        average_mixing,
-        average_relative,
-        average_merging,
-        average_widening,
-        average_narrowing,
-        average_scaling,
-    )
-    decay = min(average_cap, (1.0 + STEP) / (10.0 + STEP))
-    if fits:
-        totals, norm_piece = sum_totals(table_piece, sums, norm_came, loss_part, n, 4)
-        norm_piece = norm_piece[:6, :cols]
-    else:
-        norm_piece = jnp.sum(norm_came, 0)[:6, :cols]
         reduced = (
             table_piece,
             swap_middle(sums[0].T),
-            jnp.concatenate(sums[2:5], 1),
-            swap_middle(sums[1].T),
+            jnp.concatenate(sums[1:4], 1),
+            swap_middle(sums[4].T),
             sums[5],
             jnp.concatenate(sums[6:-1], 1),
             sums[-1],
             norm_piece,
         )
-        square = sum((jnp.sum(piece * piece) for piece in reduced))
-        lane = jnp.arange(128)
-        message = jnp.where(lane == 0, square, jnp.where(lane == 1, loss_part, 0.0))
-        (totals,) = exchange([jnp.broadcast_to(message, (n, 8, 128))], 4, "totals")
-        totals = jnp.sum(totals, 0)
-    loss = totals[0, 1]
-    grad_norm = jnp.sqrt(totals[0, 0])
-    factor = clip_limit / jnp.maximum(grad_norm, clip_limit)
-
-    def update(master, moment, average, piece, rate):
-        clipped = piece * factor
-        velocity = momentum_decay * moment + clipped
-        updated = master - rate * (clipped + momentum_decay * velocity)
-        return updated, velocity, decay * average + (1.0 - decay) * updated
-
-    last = update(scaling, moment_scaling, average_scaling, norm_piece, learn_rate)
-    if fits:
-        row = sums.shape[0] - narrowing.shape[0]
+        square = lax.psum(sum(jnp.sum(piece * piece) for piece in reduced), "dp")
+        grad_norm = jnp.sqrt(square)
+        factor = clip_limit / jnp.maximum(grad_norm, clip_limit)
+        rates = (table_rate,) + (learn_rate,) * 7
+        done = [step(*group, factor) for group in zip(masters, moments, averages, reduced, rates)]
+        return (lax.psum(loss_part, "dp"), grad_norm) + sum(zip(*done), ())
+
+    if n // 8 != 4 or n % 8 != 0 or merging.shape[0] != 24 or page_rows % 16 != 0 or size % 128 != 0:
+        return dense()
+
+    capacity = max(16, -(-2 * size // n) // 16 * 16)
+    slots = n * capacity
+    fold = 128 // capacity
+    cols = scaling.shape[1]
+    info = jnp.pad(scaling, ((0, 2), (0, 128 - cols)))
+    lists, place = make_plan(tokens, masking, documents, info, n, rows_own, capacity, fold)
+    early = 48 * (1 + 3 + relative.shape[1] // 24)
+    (
+        asked,
+        full,
+        probs,
+        sines,
+        cosines,
+        bases,
+        target,
+        normed,
+        white,
+        scale,
+        normed_low,
+        *joined,
+        attended,
+        gains,
+    ) = ahead(
+        lists, vocabulary, bank_piece, positions, place, mask_col, pieces, early, n, capacity, 1
+    )
+    full = full.reshape(-1, *full.shape[2:])
+    upper_grads, d_attended, d_lower, positive_rows, upper_norms, loss_part = upper(
+        full,
+        attended,
+        normed,
+        target,
+        mask_col,
+        negative_page,
+        negative_row,
+        asked,
+        documents,
+        gains,
+        blocks,
+        page_rows,
+    )
+    rel_map = full[:, 192:early].reshape(-1, model)
+    *d_joined, grad_rel = attend_back(d_attended, joined, rel_map, probs, sines, cosines, bases)
+    fixed = (mask_token // rows_own) * capacity + capacity - 1
+    lower_grads, sent, norm_blocks = lower(
+        full,
+        d_joined,
+        d_lower,
+        white,
+        scale,
+        gains,
+        normed_low,
+        sines,
+        cosines,
+        mask_col,
+        positive_rows,
+        place,
+        upper_norms,
+        n,
+        slots,
+        fixed,
+    )
+    grads = [lower_grads, grad_rel.reshape(n // 2, -1, model), upper_grads]
+    parts = (1, 1, 1, 1, 2, 1) + (1,) * blocks + (narrowing.shape[0] // 24,)
+    sent = sent.reshape(n, capacity, model)
+    sums, table_piece, norm_piece, totals = to_owners(
+        sent, norm_blocks, asked, loss_part, grads, parts, rows_own, fold, n, 2
+    )
+
+    def finish():
+        grad_norm = jnp.sqrt(totals[0, 0])
+        factor = clip_limit / jnp.maximum(grad_norm, clip_limit)
+        last = step(
+            scaling, moment_scaling, average_scaling, norm_piece[:6, :cols], learn_rate, factor
+        )
         layout = (
             (1, 0, 1, 24, True),
             (2, 24, 3, 24, False),
             (3, 96, 1, 48, True),
             (4, 144, 1, 24, False),
             (5, 168, blocks, 24, False),
-            (6, row, 1, narrowing.shape[0], False),
-        )
-        groups = [group[:7] for group in (masters, moments, averages)]
+            (6, 168 + 24 * blocks, 1, narrowing.shape[0], False),
+        )
+        lay = lambda group: [group[0], group[1].T, group[2], group[3].T, *group[4:7]]
+        groups = [lay(group) for group in (masters, moments, averages)]
         done = update_all(factor.reshape(1, 1), table_piece, sums, *groups, decay, layout)
-        fresh, speeds, smooths = done[:7], done[7:14], done[14:]
-    else:
-        rates = (table_rate,) + (learn_rate,) * 6
-        done = [
-            update(*group) for group in zip(masters[:7], moments[:7], averages[:7], reduced[:7], rates)
-        ]
-        fresh, speeds, smooths = zip(*done)
-    return (loss, grad_norm, *fresh, last[0], *speeds, last[1], *smooths, last[2])
+        results = [totals[0, 1], grad_norm]
+        for at, tail in zip((0, 7, 14), last):
+            results += [*lay(done[at : at + 7]), tail]
+        return tuple(results)
+
+    overflow = jnp.max(asked[:, 7, 2]) > 0.0
+    return lax.cond(overflow, dense, finish)
 
 
 ROWS = P("dp", None)

time: 445 us -> 389 us (0.87)
  Pallas kernels: 379 us -> 349 us
  local copies, waits for them, and re-layouts: 28.2 us -> 12.5 us
  matrix products: 6.06 us -> 0 us
    pallas_call x5 -> x2, Pallas kernels: 286 us -> 258 us  [the longest x1 131 us: ahead(): pl.pallas_call(partial(ahead_kernel, n, units, early, capacity), name='ah...]
    unnamed x70 -> x92, local copies, waits for them, and re-layouts: 18.4 us -> 3.04 us
    dot_general x2 -> x0, matrix products: 6.06 us -> none  [the longest x1 3.57 us: dot_tn(): lax.dot_general(left, right, (((0,), (0,)), ((), ())), preferred_element_...]
where the time goes in v4:
time: 389 us; the launch traced here: 383 us
  Pallas kernels  349 us (90%)
  between operations  17.6 us (5%)
  local copies, waits for them, and re-layouts  12.5 us (3%)
    pallas_call x1, Pallas kernels, ahead(): pl.pallas_call(partial(ahead_kernel, n, units, early, capacity), name='ah...  131 us
    pallas_call x1, Pallas kernels, to_owners(): pl.pallas_call(partial(back_kernel, n, units, pieces, chunks, fold), name...  127 us
    pallas_call x1, Pallas kernels, upper(): pl.pallas_call(partial(upper_kernel, page_rows), name='upper', out_shape=...  33.2 us
    pallas_call x1, Pallas kernels, attend_back(): pl.pallas_call(attend_back_kernel, name='attend_back', grid=(pairs,), out...  32.3 us
    pallas_call x1, Pallas kernels, lower(): pl.pallas_call(partial(lower_kernel, fixed), name='lower', out_shape=(sha...  13 us
    pallas_call x1, Pallas kernels, update_all(): pl.pallas_call(partial(update_kernel, decay, layout), name='update', grid...  10.4 us

profile of v4, /device:TPU:0, one launch (start us, length us, event | category | flops | bytes accessed | tf_op | source)
XLA Modules:
  0.0 383.2 jit_solution(1136434657639780545)
XLA Ops:
  7.3 1.1 fusion.70
  8.4 0.1 maximum_bitcast_fusion.refs_11_
  8.5 0.9 fusion.71
  9.4 0.1 maximum_bitcast_fusion.1.refs_7_
  9.5 1.2 fusion.68
  10.8 0.9 copy.161.refs_6_.mask_col
  12.3 0.1 pad_add_fusion.own
  12.4 0.1 copy.159.tok_col
  12.6 1.8 plan.1
  14.4 0.7 copy-done
  15.1 0.7 copy-done.1
  15.8 0.9 copy.160
  16.7 0.1 pad_maximum_fusion.11
  16.7 0.6 broadcast_in_dim.79.refs_4_
  17.3 131.2 %ahead.1 = (f32[32,8,128]{2,1,0:T(8,128)}, bf16[4,4,848,768]{3,2,1,0:T(8,128)(2,1)}, f32[12,512,512]{2,1,0:T(8,128)}, f32[512,384]{1,0:T(8,128)}, f32[512,384]{1...) custom-call(f32[32,8,128]{2,1,0:T(8,128)} %copy-done.1, ...), custom_call_target="tpu_custom_call" | custom-call | flops 12999999488 | bytes 104857600 | tf_op jit(solution)/shard_map/ahead/pallas_call | solution.py:1273
  148.6 33.2 %upper.1 = (bf16[16,432,768]{2,1,0:T(8,128)(2,1)}, bf16[512,768]{1,0:T(8,128)(2,1)}, f32[512,768]{1,0:T(8,128)}, bf16[512,768]{1,0:T(8,128)(2,1)}, f32[4,768]{1,0:T(4,128)}, /*index=5*/f32[1,1]{1,0:T(1,128)}) custom-call(bf16[16,848,768]{2,1,0:T(8,128)(2,1)} %bitcast.237, bf16[512,768]{1,0:T(8,128)(2,1)} %get-tuple-element.367.attended, ...), custom_call_target="tpu_custom_call" | custom-call | flops 20000000000 | bytes 33554432 | tf_op jit(solution)/shard_map/upper/pallas_call | solution.py:605
  181.9 3.2 slice.267
  185.1 32.3 %attend_back.3 = (bf16[512,768]{1,0:T(8,128)(2,1)}, bf16[512,768]{1,0:T(8,128)(2,1)}, bf16[512,768]{1,0:T(8,128)(2,1)}, bf16[2,768,768]{2,1,0:T(8,128)(2,1)}) custom-call(bf16[512,768]{1,0:T(8,128)(2,1)} %get-tuple-element.371.d_out, bf16[512,768]{1,0:T(8,128)(2,1)} %get-tuple-element.372.q, bf16[512,768]{1,0:T(8,128)(2,1)} %get-tuple-element.373.k, ...), custom_call_target="tpu_custom_call" | custom-call | flops 13740539904 | bytes 26214400 | tf_op jit(solution)/shard_map/attend_back/pallas_call | solution.py:894
  217.5 13.0 %lower.1 = (bf16[16,192,768]{2,1,0:T(8,128)(2,1)}, bf16[1024,768]{1,0:T(8,128)(2,1)}, f32[32,8,128]{2,1,0:T(8,128)}) custom-call(bf16[16,848,768]{2,1,0:T(8,128)(2,1)} %bitcast.239, bf16[512,768]{1,0:T(8,128)(2,1)} %get-tuple-element.379.dq, bf16[512,768]{1,0:T(8,128)(2,1)} %get-tuple-element.380.dk, bf16[512,768]{1,0:T(8,128)(2,1)} %get-tuple-element.381.dv, ...), custom_call_target="tpu_custom_call" | custom-call | flops 6000000000 | bytes 25165824 | tf_op jit(solution)/shard_map/lower/pallas_call | solution.py:689
  230.5 127.2 %back.1 = (f32[360,768]{1,0:T(8,128)}, f32[960,768]{1,0:T(8,128)}, f32[8,128]{1,0:T(8,128)S(1)}, f32[8,128]{1,0:T(8,128)S(1)}) custom-call(bf16[32,32,768]{2,1,0:T(8,128)(2,1)} %bitcast.271, f32[32,8,128]{2,1,0:T(8,128)} %get-tuple-element.389.refs_1_, f32[32,8,128]{2,1,0:T(8,128)} %get-tuple-element.365.asked.refs_2_, f32[1,1]{1,0:T(1,128)} %get-tuple-element.390.refs_3_, ...), custom_call_target="tpu_custom_call" | custom-call | bytes 104857600 | tf_op jit(solution)/shard_map/back/pallas_call | solution.py:420
  357.7 1.6 slice_reduce_fusion.6
  360.0 13.0 %conditional.1 = (f32[24,2304]{1,0:T(8,128)S(1)}, f32[24,768]{1,0:T(8,128)S(1)}, f32[24,3072]{1,0:T(8,128)S(1)}, f32[96,768]{1,0:T(8,128)S(1)}, f32[24,2304]{1,0...) conditional(s32[]{:T(128)} %convert_element_type.211, ...), branch_computations={%region_1.2_spmd, %region_2.47_spmd} | conditional | flops 52047237120 | bytes 1127846400 | solution.py:1673
  360.0 0.6 fusion.58
  361.3 10.4 %update.1 = (f32[960,768]{1,0:T(8,128)}, f32[24,768]{1,0:T(8,128)S(1)}, f32[24,2304]{1,0:T(8,128)S(1)}, f32[48,768]{1,0:T(8,128)S(1)}, f32[24,768]{1,0:T(8,128)S...) custom-call(f32[1,1]{1,0:T(1,128)} %bitcast.1.factor, ...), custom_call_target="tpu_custom_call" | custom-call | bytes 29360128 | tf_op jit(solution)/shard_map/cond/branch_0_fun/update/pallas_call | solution.py:745
  373.3 0.3 copy-done.141
  373.7 0.1 copy-done.146
  373.8 0.1 copy-done.147
  373.9 0.1 copy-done.148
  374.0 0.1 copy-done.149
  374.1 0.1 copy-done.150
  374.2 0.1 copy-done.151
  374.3 0.1 copy-done.153
  (87 shorter events, 0.7 us)
Async XLA Ops:
  7.2 3.6 copy-start.124
  7.2 5.2 %copy-start.88 = (s32[512]{0:T(512)S(1)}, s32[512]{0:T(512)}, u32[]{:S(2)}) copy-start(s32[512]{0:T(512)} %param.37) | copy-start | bytes 6148
  7.2 5.3 %copy-start.115 = (f32[6,24]{1,0:T(8,128)S(1)}, f32[6,24]{1,0:T(8,128)}, u32[]{:S(2)}) copy-start(f32[6,24]{1,0:T(8,128)} %param.51) | copy-start | bytes 1732
  7.2 10.1 %copy-start.113 = (bf16[1,64,768]{2,1,0:T(8,128)(2,1)S(1)}, bf16[1,64,768]{2,1,0:T(8,128)(2,1)}, u32[]{:S(2)}) copy-start(bf16[1,64,768]{2,1,0:T(8,128)(2,1)} %param.43) | copy-start | bytes 294916
  7.2 8.5 %copy-start.133 = (s32[2,512]{1,0:T(2,128)S(1)}, s32[2,512]{1,0:T(2,128)}, u32[]{:S(2)}) copy-start(s32[2,512]{1,0:T(2,128)} %param.38) | copy-start | bytes 12292
  7.3 10.1 %copy-start.70 = (f32[24,768]{1,0:T(8,128)S(1)}, f32[24,768]{1,0:T(8,128)}, u32[]{:S(2)}) copy-start(f32[24,768]{1,0:T(8,128)} %refs_12_.1) | copy-start | bytes 221188
  7.3 10.0 %copy-start.13 = (f32[96,768]{1,0:T(8,128)S(1)}, f32[96,768]{1,0:T(8,128)}, u32[]{:S(2)}) copy-start(f32[96,768]{1,0:T(8,128)} %refs_17_.1) | copy-start | bytes 884740
  8.5 140.0 %copy-start.84 = (f32[48,768]{1,0:T(8,128)}, f32[48,768]{1,0:T(8,128)S(1)}, u32[]{:S(2)}) copy-start(f32[48,768]{1,0:T(8,128)S(1)} %maximum_bitcast_fusion.refs_11_) | copy-start | bytes 442372
  9.5 139.0 %copy-start.102 = (f32[24,768]{1,0:T(8,128)}, f32[24,768]{1,0:T(8,128)S(1)}, u32[]{:S(2)}) copy-start(f32[24,768]{1,0:T(8,128)S(1)} %maximum_bitcast_fusion.1.refs_7_) | copy-start | bytes 221188
  10.7 137.8 %copy-start.95 = (f32[24,768]{1,0:T(8,128)}, f32[24,768]{1,0:T(8,128)S(1)}, u32[]{:S(2)}) copy-start(f32[24,768]{1,0:T(8,128)S(1)} %get-tuple-element.927.refs_16_) | copy-start | bytes 221188
  10.7 137.8 %copy-start.96 = (f32[24,768]{1,0:T(8,128)}, f32[24,768]{1,0:T(8,128)S(1)}, u32[]{:S(2)}) copy-start(f32[24,768]{1,0:T(8,128)S(1)} %get-tuple-element.928.refs_15_) | copy-start | bytes 221188
  10.7 137.8 %copy-start.97 = (f32[24,768]{1,0:T(8,128)}, f32[24,768]{1,0:T(8,128)S(1)}, u32[]{:S(2)}) copy-start(f32[24,768]{1,0:T(8,128)S(1)} %get-tuple-element.929.refs_14_) | copy-start | bytes 221188
  10.8 137.8 %copy-start.98 = (f32[24,768]{1,0:T(8,128)}, f32[24,768]{1,0:T(8,128)S(1)}, u32[]{:S(2)}) copy-start(f32[24,768]{1,0:T(8,128)S(1)} %get-tuple-element.930.refs_13_) | copy-start | bytes 221188
  10.8 137.8 %copy-start.99 = (f32[24,768]{1,0:T(8,128)}, f32[24,768]{1,0:T(8,128)S(1)}, u32[]{:S(2)}) copy-start(f32[24,768]{1,0:T(8,128)S(1)} %get-tuple-element.942.refs_8_) | copy-start | bytes 221188
  10.8 137.8 %copy-start.100 = (f32[24,768]{1,0:T(8,128)}, f32[24,768]{1,0:T(8,128)S(1)}, u32[]{:S(2)}) copy-start(f32[24,768]{1,0:T(8,128)S(1)} %get-tuple-element.943.refs_9_) | copy-start | bytes 221188
  10.8 137.8 %copy-start.101 = (f32[24,768]{1,0:T(8,128)}, f32[24,768]{1,0:T(8,128)S(1)}, u32[]{:S(2)}) copy-start(f32[24,768]{1,0:T(8,128)S(1)} %get-tuple-element.944.refs_10_) | copy-start | bytes 221188
  17.3 131.3 %copy-start.130 = (s32[8,512]{1,0:T(8,128)S(1)}, s32[8,512]{1,0:T(8,128)}, u32[]{:S(2)}) copy-start(s32[8,512]{1,0:T(8,128)} %page.1) | copy-start | bytes 49156
  17.3 131.3 %copy-start.131 = (s32[8,512]{1,0:T(8,128)S(1)}, s32[8,512]{1,0:T(8,128)}, u32[]{:S(2)}) copy-start(s32[8,512]{1,0:T(8,128)} %row.1) | copy-start | bytes 49156
  230.5 129.5 %copy-start.5 = (f32[960,768]{1,0:T(8,128)S(1)}, f32[960,768]{1,0:T(8,128)}, u32[]{:S(2)}) copy-start(f32[960,768]{1,0:T(8,128)} %refs_1_.1) | copy-start | bytes 8847364
  230.5 129.5 %copy-start.20 = (f32[768,48]{0,1:T(8,128)S(1)}, f32[768,48]{0,1:T(8,128)}, u32[]{:S(2)}) copy-start(f32[768,48]{0,1:T(8,128)} %param.47) | copy-start | bytes 442372
  230.5 129.5 %copy-start.58 = (f32[768,24]{0,1:T(8,128)S(1)}, f32[768,24]{0,1:T(8,128)}, u32[]{:S(2)}) copy-start(f32[768,24]{0,1:T(8,128)} %param.45) | copy-start | bytes 221188
  230.5 129.5 %copy-start.134 = (f32[6,24]{1,0:T(8,128)S(1)}, f32[6,24]{1,0:T(8,128)}, u32[]{:S(2)}) copy-start(f32[6,24]{1,0:T(8,128)} %param.59) | copy-start | bytes 1732
  230.5 129.5 %copy-start.137 = (f32[6,24]{1,0:T(8,128)S(1)}, f32[6,24]{1,0:T(8,128)}, u32[]{:S(2)}) copy-start(f32[6,24]{1,0:T(8,128)} %param.67) | copy-start | bytes 1732
  373.2 1.4 copy-start.155
  373.2 1.4 copy-start.156
  373.2 1.4 copy-start.157
  373.2 1.4 copy-start.158
  373.2 1.4 copy-start.159
  373.2 1.5 copy-start.160
  373.3 1.5 copy-start.161
  373.3 1.5 copy-start.162
  373.3 1.5 copy-start.163
  (14 other events, 12.5 us)

commit v5 on v4

--- a/solution.py
+++ b/solution.py
@@ -170,304 +170,6 @@
     pl.semaphore_wait(barrier, n - 1)
 
 
-def back_kernel(n, units, pieces, chunks, fold, *refs):
-    count = len(units)
-    sent, small, asked, loss_part, grads = *refs[:4], refs[4 : 4 + count]
-    out, table, norm_piece, totals = refs[4 + count : 8 + count]
-    own, par, from_b, from_a, from_z, mine, gone, back = refs[8 + count : 16 + count]
-    came, small_came, picks, message, told = refs[16 + count : 21 + count]
-    row_send, row_recv, own_sem, load_sem, pair_send, pair_recv = refs[21 + count : 27 + count]
-    b_send, b_recv, a_send, a_recv, z_send, z_recv, f_send, f_recv, t_send, t_recv = refs[27 + count :]
-    layers = n // 8
-    me = lax.axis_index("dp")
-    core, spot, layer, step_a, step_b = place_of(me)
-    half = own.shape[3]
-    here = pl.ds(pl.multiple_of(core * half, 128), half)
-    there = pl.ds(pl.multiple_of((1 - core) * half, 128), half)
-    partner = me + 1 - 2 * core
-    to_a, to_b = me + 2 * step_a, me + 2 * step_b
-    offsets = [48 * sum(units[:k]) for k in range(count)]
-    spot_a, spot_b, spot_ab = spot + step_a, spot + step_b, spot + step_a + step_b
-    size = own.shape[2] // chunks
-
-    greet_everyone(me, n)
-    for index in (spot_ab, spot_a, spot_b, spot):
-        for ref, at, unit in zip(grads, offsets, units):
-            remote_copy(
-                ref.at[:, index, :, there],
-                par.at[:, index, pl.ds(at, 48 * unit)],
-                pair_send.at[index],
-                pair_recv.at[index],
-                partner,
-            ).start()
-    for index in (spot_ab, spot_b, spot_a, spot):
-        for ref, at, unit in zip(grads, offsets, units):
-            pltpu.make_async_copy(
-                ref.at[:, index, :, here], own.at[:, index, pl.ds(at, 48 * unit)], load_sem.at[index]
-            ).start()
-
-    def row_copies(step):
-        peer = lax.rem(me + step, n)
-        return [
-            remote_copy(src.at[peer], dst.at[me], row_send.at[k, step], row_recv.at[k, step], peer)
-            for k, (src, dst) in enumerate(((sent, came), (small, small_came)))
-        ]
-
-    def start_rows(step, carry):
-        for copy in row_copies(step):
-            copy.start()
-        return carry
-
-    def finish_rows(step, carry):
-        for copy in row_copies(step):
-            copy.wait()
-        return carry
-
-    lax.fori_loop(1, n, start_rows, 0)
-    own_copies = [
-        pltpu.make_async_copy(src.at[me], dst.at[me], own_sem.at[k])
-        for k, (src, dst) in enumerate(((sent, came), (small, small_came)))
-    ]
-    for copy in own_copies:
-        copy.start()
-
-    def arrived(index):
-        pltpu.make_async_copy(own.at[:, index], own.at[:, index], load_sem.at[index]).wait()
-        pltpu.make_async_copy(par.at[:, index], par.at[:, index], pair_recv.at[index]).wait()
-
-    def total(*parts):
-        return sum(part[...].astype(jnp.float32) for part in parts)
-
-    def b_copy(kind, level, part):
-        cut = pl.ds(part * size, size)
-        return remote_copy(
-            own.at[level, spot_ab if kind == 0 else spot_b, cut], from_b.at[kind, level, cut],
-            b_send.at[kind, level, part], b_recv.at[kind, level, part], to_b,
-        )
-
-    def a_copy(level, part):
-        cut = pl.ds(part * size, size)
-        return remote_copy(
-            own.at[level, spot_a, cut], from_a.at[level, cut],
-            a_send.at[level, part], a_recv.at[level, part], to_a,
-        )
-
-    def z_copy(level, part):
-        cut = pl.ds(part * size, size)
-        return remote_copy(
-            own.at[level, spot, cut], from_z.at[layer, cut],
-            z_send.at[level, part], z_recv.at[layer, part], me + 8 * (level - layer),
-        )
-
-    def cross_b(kind, index, part):
-        cut = pl.ds(part * size, size)
-
-        def step(level, carry):
-            own[level, index, cut] = total(
-                own.at[level, index, cut], par.at[level, index, cut]
-            ).astype(own.dtype)
-            b_copy(kind, level, part).start()
-            return carry
-
-        lax.fori_loop(0, layers, step, 0)
-
-    def cross_a(part):
-        cut = pl.ds(part * size, size)
-
-        def step(level, carry):
-            b_copy(0, level, part).wait_recv()
-            own[level, spot_a, cut] = total(
-                own.at[level, spot_a, cut], par.at[level, spot_a, cut], from_b.at[0, level, cut]
-            ).astype(own.dtype)
-            a_copy(level, part).start()
-            return carry
-
-        lax.fori_loop(0, layers, step, 0)
-
-    def column(level, part):
-        cut = pl.ds(part * size, size)
-        b_copy(1, level, part).wait_recv()
-        a_copy(level, part).wait_recv()
-        return total(
-            own.at[level, spot, cut], par.at[level, spot, cut],
-            from_b.at[1, level, cut], from_a.at[level, cut],
-        )
-
-    def cross_z(part):
-        cut = pl.ds(part * size, size)
-
-        def step(gap, carry):
-            level = lax.rem(layer + gap, layers)
-            own[level, spot, cut] = column(level, part).astype(own.dtype)
-            z_copy(level, part).start()
-            return carry
-
-        lax.fori_loop(1, layers, step, 0)
-        mine[cut] = column(layer, part)
-
-    arrived(spot_ab)
-    cross_b(0, spot_ab, 0)
-    arrived(spot_b)
-    for part in range(chunks):
-        if part > 0:
-            cross_b(0, spot_ab, part)
-        cross_b(1, spot_b, part)
-    wanted = lax.broadcasted_iota(jnp.int32, (table.shape[0], 128), 0) + 1
-    for turn in range(n // fold):
-        ids = asked[turn * fold]
-        for k in range(1, fold):
-            ids = ids + asked[turn * fold + k]
-        found = ids[6:7].astype(jnp.int32) == wanted
-        picks[:, turn * 128 : (turn + 1) * 128] = jnp.where(found, 1.0, 0.0).astype(picks.dtype)
-    arrived(spot_a)
-    arrived(spot)
-    for part in range(chunks):
-        cross_a(part)
-        if part > 0:
-            cross_z(part - 1)
-    cross_z(chunks - 1)
-    lax.fori_loop(1, n, finish_rows, 0)
-    for copy in own_copies:
-        copy.wait()
-    table[...] = dot_nn(picks[...], came[...].reshape(picks.shape[1], -1))
-    squares = jnp.zeros((1, 1), jnp.float32)
-    for part in range(4):
-        rows = table.shape[0] // 4
-        piece = table[part * rows : (part + 1) * rows]
-        squares = squares + jnp.sum(piece * piece, keepdims=True)
-    norm = small_came[0]
-    for k in range(1, n):
-        norm = norm + small_came[k]
-    norm_piece[...] = norm
-    squares = squares + jnp.sum(norm * norm, keepdims=True)
-    for part in range(chunks):
-        cut = pl.ds(part * size, size)
-
-        def step(gap, carry):
-            level = lax.rem(layer + gap, layers)
-            remote_copy(
-                own.at[level, spot, cut], from_z.at[level, cut],
-                z_send.at[level, part], z_recv.at[level, part], me,
-            ).wait_recv()
-            mine[cut] += total(from_z.at[level, cut])
-            return carry
-
-        lax.fori_loop(1, layers, step, 0)
-
-    at = 0
-    for piece in pieces:
-        offset, rows = 2 * at, 24 * piece
-        gone[pl.ds(at, rows)] = mine[pl.ds(pl.multiple_of(offset + (1 - core) * rows, 8), rows)]
-        out[pl.ds(at, rows), here] = mine[pl.ds(pl.multiple_of(offset + core * rows, 8), rows)]
-        at += rows
-    last = remote_copy(gone, back, f_send, f_recv, partner)
-    last.start()
-    squares = squares + jnp.sum(out[:, here] * out[:, here], keepdims=True)
-    last.wait()
-    out[:, there] = back[...]
-    squares = squares + jnp.sum(back[...] * back[...], keepdims=True)
-    lane = lax.broadcasted_iota(jnp.int32, message.shape, 1)
-    message[...] = jnp.where(lane == 0, squares, jnp.where(lane == 1, loss_part[...], 0.0))
-
-    def tell(step):
-        peer = lax.rem(me + step, n)
-        return remote_copy(message, told.at[me], t_send.at[step], t_recv.at[step], peer)
-
-    def start_told(step, carry):
-        tell(step).start()
-        return carry
-
-    def wait_told(step, carry):
-        tell(step).wait()
-        return carry
-
-    lax.fori_loop(1, n, start_told, 0)
-    told[me] = message[...]
-    for index in range(4):
-        pltpu.make_async_copy(par.at[:, index], par.at[:, index], pair_send.at[index]).wait()
-
-    def settle(level, carry):
-        for part in range(chunks):
-            b_copy(0, level, part).wait_send()
-            b_copy(1, level, part).wait_send()
-            a_copy(level, part).wait_send()
-
-            @pl.when(level != layer)
-            def _():
-                z_copy(level, part).wait_send()
-
-        return carry
-
-    lax.fori_loop(0, layers, settle, 0)
-    lax.fori_loop(1, n, wait_told, 0)
-    total_line = told[0]
-    for k in range(1, n):
-        total_line = total_line + told[k]
-    totals[...] = total_line
-
-
-def to_owners(sent, small, asked, loss_part, grads, pieces, rows_own, fold, n, ident):
-    model = grads[0].shape[2]
-    layers = n // 8
-    units = [grad.shape[1] // 48 for grad in grads]
-    chunks = max(k for k in range(1, 6) if sum(units) % k == 0)
-    rows = 48 * sum(units)
-    half = model // 2
-    low = jnp.bfloat16
-    dma = pltpu.SemaphoreType.DMA
-    anywhere = pl.BlockSpec(memory_space=pl.ANY)
-    vmem = pl.BlockSpec(memory_space=pltpu.VMEM)
-    return pl.pallas_call(
-        partial(back_kernel, n, units, pieces, chunks, fold),
-        name="back",
-        out_shape=(
-            jax.ShapeDtypeStruct((rows // 2, model), jnp.float32),
-            jax.ShapeDtypeStruct((rows_own, model), jnp.float32),
-            jax.ShapeDtypeStruct((8, 128), jnp.float32),
-            jax.ShapeDtypeStruct((8, 128), jnp.float32),
-        ),
-        in_specs=[anywhere, anywhere, vmem, vmem] + [anywhere] * len(grads),
-        out_specs=(vmem,) * 4,
-        scratch_shapes=[
-            pltpu.VMEM((layers, 4, rows, half), low),
-            pltpu.VMEM((layers, 4, rows, half), low),
-            pltpu.VMEM((2, layers, rows, half), low),
-            pltpu.VMEM((layers, rows, half), low),
-            pltpu.VMEM((layers, rows, half), low),
-            pltpu.VMEM((rows, half), jnp.float32),
-            pltpu.VMEM((rows // 2, half), jnp.float32),
-            pltpu.VMEM((rows // 2, half), jnp.float32),
-            pltpu.VMEM(sent.shape, low),
-            pltpu.VMEM(small.shape, jnp.float32),
-            pltpu.VMEM((rows_own, sent.shape[0] * sent.shape[1]), low),
-            pltpu.VMEM((8, 128), jnp.float32),
-            pltpu.VMEM((n, 8, 128), jnp.float32),
-            dma((2, n)),
-            dma((2, n)),
-            dma((2,)),
-            dma((4,)),
-            dma((4,)),
-            dma((4,)),
-            dma((2, layers, chunks)),
-            dma((2, layers, chunks)),
-            dma((layers, chunks)),
-            dma((layers, chunks)),
-            dma((layers, chunks)),
-            dma((layers, chunks)),
-            dma,
-            dma,
-            dma((n,)),
-            dma((n,)),
-        ],
-        compiler_params=pltpu.CompilerParams(
-            collective_id=ident, has_side_effects=True, vmem_limit_bytes=60 * 2**20
-        ),
-        cost_estimate=pl.CostEstimate(
-            flops=0, bytes_accessed=100 * 2**20, transcendentals=0
-        ),
-    )(sent, small, asked, loss_part, *[grad.reshape(layers, 4, -1, model) for grad in grads])
-
-
 def flat(rows):
     return rows.reshape(-1, rows.shape[-1])
 
@@ -633,80 +335,6 @@
     )(full, attended, normed, target, mask_col, page, row, asked, doc, gains)
 
 
-def lower_kernel(
-    fixed, full, dq, dk, dv, d_lower, white, scale, gains, normed, sines, cosines, mask_col, pos_rows, place, upper_norms,
-    grads, sent, norms, held, sem,
-):
-    low = jnp.bfloat16
-    chips, _, model = held.shape
-    load = pltpu.make_async_copy(full.at[:, pl.ds(48, 144)], held.at[:, pl.ds(48, 144)], sem.at[0])
-    load.start()
-    mask = mask_col[...]
-    d_first = d_lower[...]
-    load.wait()
-    stores = []
-    for third, ref in enumerate((dq, dk, dv)):
-        at = 48 + 48 * third
-        upstream = ref[...]
-        d_first = d_first + dot_nt(upstream, flat(held[:, at : at + 48]))
-        held[:, at : at + 48] = dot_tn(normed[...], upstream).astype(low).reshape(chips, 48, model)
-        stores.append(
-            pltpu.make_async_copy(held.at[:, pl.ds(at, 48)], grads.at[:, pl.ds(at, 48)], sem.at[1 + third])
-        )
-        stores[-1].start()
-    d_rows, gain, bias = norm_back(d_first, white[...], scale[...], gains[0:1])
-    boxes = jnp.concatenate([sines[...], cosines[...]], 1).astype(low)
-    held[:, 0:48] = dot_tn(d_rows.astype(low), boxes).astype(low).reshape(chips, 48, model)
-    stores.append(pltpu.make_async_copy(held.at[:, pl.ds(0, 48)], grads.at[:, pl.ds(0, 48)], sem.at[4]))
-    stores[-1].start()
-    count = norms.shape[0]
-    lines = jnp.concatenate([gain, bias, upper_norms[...]], 0)
-    cols = model // count
-    norms[...] = jnp.zeros_like(norms)
-    for owner in range(count):
-        norms[owner, 0:6, 0:cols] = lines[:, owner * cols : (owner + 1) * cols]
-    token_grads = jnp.where(mask == 1.0, pos_rows[...].astype(jnp.float32), d_rows).astype(low)
-    mask_grad = jnp.sum(mask * d_rows, 0, keepdims=True)
-    slots = sent.shape[0]
-    seats = lax.broadcasted_iota(jnp.int32, (place.shape[0], slots), 1) == place[...]
-    found = dot_tn(jnp.where(seats, 1.0, 0.0).astype(low), token_grads)
-    line = lax.broadcasted_iota(jnp.int32, (slots, 1), 0)
-    sent[...] = jnp.where(line == fixed, mask_grad, found).astype(low)
-    for copy in stores:
-        copy.wait()
-
-
-def lower(
-    full, d_joined, d_lower, white, scale, gains, normed, sines, cosines, mask_col, pos_rows, place,
-    upper_norms, n, slots, fixed,
-):
-    size, model = d_lower.shape
-    chips = full.shape[0]
-    low, wide = jnp.bfloat16, jnp.float32
-    vmem = pl.BlockSpec(memory_space=pltpu.VMEM)
-    anywhere = pl.BlockSpec(memory_space=pl.ANY)
-    shape = jax.ShapeDtypeStruct
-    return pl.pallas_call(
-        partial(lower_kernel, fixed),
-        name="lower",
-        out_shape=(
-            shape((chips, 192, model), low),
-            shape((slots, model), low),
-            shape((n, 8, 128), wide),
-        ),
-        in_specs=[anywhere] + [vmem] * 14,
-        out_specs=(anywhere,) + (vmem,) * 2,
-        scratch_shapes=[
-            pltpu.VMEM((chips, 192, model), low),
-            pltpu.SemaphoreType.DMA((5,)),
-        ],
-        compiler_params=pltpu.CompilerParams(vmem_limit_bytes=60 * 2**20),
-        cost_estimate=pl.CostEstimate(
-            flops=6 * 10**9, bytes_accessed=24 * 2**20, transcendentals=0
-        ),
-    )(full, *d_joined, d_lower, white, scale, gains, normed, sines, cosines, mask_col, pos_rows, place, upper_norms)
-
-
 def update_kernel(decay, layout, factor, table, sums, *refs):
     masters, moments, averages = refs[0:7], refs[7:14], refs[14:21]
     fresh, speeds, smooths = refs[21:28], refs[28:35], refs[35:42]
@@ -813,7 +441,7 @@
         scores = scores * HD ** (-0.5)
         powers = jnp.exp(scores - jnp.max(scores, -1, keepdims=True))
         shares = powers * (1.0 / jnp.sum(powers, -1, keepdims=True))
-        probs[half] = shares
+        probs[half] = shares.astype(probs.dtype)
         results.append(dot_nn(shares.astype(jnp.bfloat16), values))
     return pick_halves(*results).astype(jnp.bfloat16)
 
@@ -854,16 +482,12 @@
     )(*joined, rel_map, rel_map, sines, cosines, bases)
 
 
-def attend_back_kernel(
-    d_out, q, k, v, rel_text, rel_box, probs, sines, cosines, bases, dq, dk, dv, g_rel
-):
-    queries, keys, values, upstream = q[...], k[...], v[...], d_out[...]
-    spread = bases[...]
+def attend_back_pair(upstream, queries, keys, values, rel_text, rel_box, probs, sines, cosines, spread):
     scale = HD ** (-0.5)
     low = jnp.bfloat16
     got = [[], [], []]
     for half in range(2):
-        shares = probs[half]
+        shares = probs[half].astype(jnp.float32)
         d_probs = dot_nt(masked(upstream, half), values)
         got[2].append(dot_tn(shares.astype(low), upstream))
         inner = jnp.sum(d_probs * shares, -1, keepdims=True)
@@ -877,10 +501,17 @@
         got[1].append(dot_nn(turned, queries) * scale + dot_nt(d_box, rel_box[...]))
         part = dot_tn(masked(keys, half), d_box)
         box_sum = part if half == 0 else box_sum + part
-    for ref, halves in zip((dq, dk, dv), got):
-        ref[...] = pick_halves(*halves).astype(low)
-    g_rel[0] = text_sum.astype(low)
-    g_rel[1] = box_sum.astype(low)
+    return (*[pick_halves(*halves).astype(low) for halves in got], text_sum, box_sum)
+
+
+def attend_back_kernel(
+    d_out, q, k, v, rel_text, rel_box, probs, sines, cosines, bases, dq, dk, dv, g_rel
+):
+    dq[...], dk[...], dv[...], text_sum, box_sum = attend_back_pair(
+        d_out[...], q[...], k[...], v[...], rel_text, rel_box, probs, sines, cosines, bases[...]
+    )
+    g_rel[0] = text_sum.astype(jnp.bfloat16)
+    g_rel[1] = box_sum.astype(jnp.bfloat16)
 
 
 def attend_back(d_attended, joined, rel_map, probs, sines, cosines, bases):
@@ -1276,7 +907,7 @@
         out_shape=(
             shape(lists.shape, lists.dtype),
             shape((layers, 4, chip, model), low),
-            shape((heads, size, size), wide),
+            shape((heads, size, size), low),
             shape((size, 2 * waves), wide),
             shape((size, 2 * waves), wide),
             rows(low),
@@ -1301,7 +932,7 @@
             pltpu.VMEM((n, capacity, model), low),
             pltpu.VMEM((layers, 4, 192, model), low),
             pltpu.VMEM((2 * model, model), low),
-            pltpu.VMEM((2, 2, size, size), wide),
+            pltpu.VMEM((2, 2, size, size), low),
             dma((n,)),
             dma((n,)),
             dma((n,)),
@@ -1325,6 +956,437 @@
             flops=13 * 10**9, bytes_accessed=100 * 2**20, transcendentals=0
         ),
     )(lists, vocabulary, pages, points, omegas, place, mask_col, *weights)
+
+
+def behind_kernel(n, early, pieces, fold, fixed, *refs):
+    full, upper, probs, d_lower, white, q_in, k_in, v_in, d_attended, sines, cosines, bases = refs[:12]
+    scale, gains, normed, mask_col, pos_rows, place, upper_norms, asked, loss_part = refs[12:21]
+    out, table, norm_piece, totals = refs[21:25]
+    rel_map, low_grads, shares, q, k, v, sent, small = refs[25:33]
+    own, par, par_low, from_b, from_a, from_z, mine, gone, back = refs[33:42]
+    came, small_came, message, told = refs[42:46]
+    row_send, row_recv, own_sem, load_sem, pair_send, pair_recv, local_sem, share_sem = refs[46:54]
+    b_send, b_recv, a_send, a_recv, z_send, z_recv, f_send, f_recv, t_send, t_recv = refs[54:]
+    low, wide = jnp.bfloat16, jnp.float32
+    layers = n // 8
+    me = lax.axis_index("dp")
+    core, spot, layer, step_a, step_b = place_of(me)
+    half = own.shape[3]
+    model = 2 * half
+    size = normed.shape[0]
+    here = pl.ds(pl.multiple_of(core * half, 128), half)
+    there = pl.ds(pl.multiple_of((1 - core) * half, 128), half)
+    partner = me + 1 - 2 * core
+    to_a, to_b = me + 2 * step_a, me + 2 * step_b
+    spot_a, spot_b, spot_ab = spot + step_a, spot + step_b, spot + step_a + step_b
+    bulk = own.shape[2]
+    chunk = 144
+    parts = (bulk // chunk, early // chunk)
+    pairs = model // (2 * HD)
+    deep = early - 192
+
+    for chip in range(4 * layers):
+        pltpu.make_async_copy(
+            full.at[chip // 4, chip % 4, pl.ds(192, deep)], rel_map.at[pl.ds(chip * deep, deep)], local_sem.at[0]
+        ).start()
+    joined = [
+        pltpu.make_async_copy(src, dst, local_sem.at[1 + j])
+        for j, (src, dst) in enumerate(((q_in, q), (k_in, k), (v_in, v)))
+    ]
+    mixing = pltpu.make_async_copy(
+        full.at[:, :, pl.ds(48, 144)], low_grads.at[:, :, pl.ds(48, 144)], local_sem.at[4]
+    )
+    rest = size - (table.shape[0] - size)
+    kept = [
+        pltpu.make_async_copy(d_lower, table.at[pl.ds(0, size)], local_sem.at[5]),
+        pltpu.make_async_copy(
+            white.at[pl.ds(0, size - rest)], table.at[pl.ds(size, size - rest)], local_sem.at[6]
+        ),
+        pltpu.make_async_copy(white.at[pl.ds(size - rest, rest)], out.at[pl.ds(0, rest)], local_sem.at[7]),
+    ]
+
+    def shares_copy(pair):
+        slot = lax.rem(pair, 2)
+        return pltpu.make_async_copy(probs.at[pl.ds(2 * pair, 2)], shares.at[slot], share_sem.at[slot])
+
+    for copy in (*joined, shares_copy(0), shares_copy(1), mixing, *kept):
+        copy.start()
+
+    greet_everyone(me, n)
+
+    def pair_copy(g, index):
+        if g == 0:
+            src, dst = upper.at[:, index, :, there], par.at[:, index]
+        else:
+            src, dst = low_grads.at[:, index, :, there], par_low.at[:, index]
+        return remote_copy(src, dst, pair_send.at[g, index], pair_recv.at[g, index], partner)
+
+    def load_copy(index):
+        return pltpu.make_async_copy(upper.at[:, index, :, here], own.at[:, index], load_sem.at[index])
+
+    for index in (spot_ab, spot_a, spot_b, spot):
+        pair_copy(0, index).start()
+    for index in (spot_ab, spot_b, spot_a, spot):
+        load_copy(index).start()
+
+    def arrived(g, index):
+        if g == 0:
+            load_copy(index).wait()
+        pair_copy(g, index).wait_recv()
+
+    def total(*views):
+        return sum(view[...].astype(wide) for view in views)
+
+    def mine_at(g, level, index, part):
+        cut = pl.ds(part * chunk, chunk)
+        return own.at[level, index, cut] if g == 0 else low_grads.at[level, index, cut, here]
+
+    def par_at(g, level, index, part):
+        cut = pl.ds(part * chunk, chunk)
+        return (par if g == 0 else par_low).at[level, index, cut]
+
+    def cut_of(g, part):
+        return pl.ds(g * bulk + part * chunk, chunk)
+
+    def b_copy(g, kind, level, part):
+        return remote_copy(
+            mine_at(g, level, spot_ab if kind == 0 else spot_b, part),
+            from_b.at[kind, level, cut_of(g, part)],
+            b_send.at[g, kind, level, part], b_recv.at[g, kind, level, part], to_b,
+        )
+
+    def a_copy(g, level, part):
+        return remote_copy(
+            mine_at(g, level, spot_a, part), from_a.at[level, cut_of(g, part)],
+            a_send.at[g, level, part], a_recv.at[g, level, part], to_a,
+        )
+
+    def z_copy(g, level, part):
+        return remote_copy(
+            mine_at(g, level, spot, part), from_z.at[layer, cut_of(g, part)],
+            z_send.at[g, level, part], z_recv.at[g, layer, part], me + 8 * (level - layer),
+        )
+
+    def cross_b(g, kind):
+        index = spot_ab if kind == 0 else spot_b
+
+        def step(turn, carry):
+            part, level = lax.div(turn, layers), lax.rem(turn, layers)
+            view = mine_at(g, level, index, part)
+            view[...] = total(view, par_at(g, level, index, part)).astype(low)
+            b_copy(g, kind, level, part).start()
+            return carry
+
+        lax.fori_loop(0, layers * parts[g], step, 0)
+
+    def cross_a(g, part):
+        def step(level, carry):
+            b_copy(g, 0, level, part).wait_recv()
+            view = mine_at(g, level, spot_a, part)
+            view[...] = total(
+                view, par_at(g, level, spot_a, part), from_b.at[0, level, cut_of(g, part)]
+            ).astype(low)
+            a_copy(g, level, part).start()
+            return carry
+
+        lax.fori_loop(0, layers, step, 0)
+
+    def column(g, level, part):
+        b_copy(g, 1, level, part).wait_recv()
+        a_copy(g, level, part).wait_recv()
+        cut = cut_of(g, part)
+        return total(
+            mine_at(g, level, spot, part), par_at(g, level, spot, part),
+            from_b.at[1, level, cut], from_a.at[level, cut],
+        )
+
+    def cross_z(g, part):
+        def step(gap, carry):
+            level = lax.rem(layer + gap, layers)
+            view = mine_at(g, level, spot, part)
+            view[...] = column(g, level, part).astype(low)
+            z_copy(g, level, part).start()
+            return carry
+
+        lax.fori_loop(1, layers, step, 0)
+        mine[cut_of(g, part)] = column(g, layer, part)
+
+    def last_z(g, part):
+        cut = cut_of(g, part)
+
+        def step(gap, carry):
+            level = lax.rem(layer + gap, layers)
+            view = from_z.at[level, cut]
+            pltpu.make_async_copy(view, view, z_recv.at[g, level, part]).wait()
+            mine[cut] += total(view)
+            return carry
+
+        lax.fori_loop(1, layers, step, 0)
+
+    for copy in joined:
+        copy.wait()
+    pltpu.make_async_copy(rel_map, rel_map, local_sem.at[0]).wait()
+
+    def first_cross():
+        arrived(0, spot_ab)
+        cross_b(0, 0)
+
+    def second_cross():
+        arrived(0, spot_b)
+        cross_b(0, 1)
+        arrived(0, spot_a)
+        arrived(0, spot)
+
+    turns = [[] for _ in range(pairs)]
+    turns[1], turns[2] = [first_cross], [second_cross]
+    for part in range(parts[0]):
+        turns[min(3 + part, pairs - 1)].append(lambda part=part: cross_a(0, part))
+
+    def attend_turn(pair, carry):
+        for at in range(pairs):
+
+            @pl.when(pair == at)
+            def _():
+                for step in turns[at]:
+                    step()
+
+        shares_copy(pair).wait()
+        start = pl.multiple_of(pair * 2 * HD, 2 * HD)
+        lanes = pl.ds(start, 2 * HD)
+        other = pl.ds(pl.multiple_of(model + start, 2 * HD), 2 * HD)
+        dq, dk, dv, text_sum, box_sum = attend_back_pair(
+            d_attended[:, lanes], q[:, lanes], k[:, lanes], v[:, lanes],
+            rel_map.at[pl.ds(start, 2 * HD)], rel_map.at[other], shares.at[lax.rem(pair, 2)],
+            sines, cosines, bases[...],
+        )
+        q[:, lanes], k[:, lanes], v[:, lanes] = dq, dk, dv
+        for first, rows in ((0, text_sum), (model, box_sum)):
+            for j in range(0, 2 * HD, 32):
+                row = first + pair * 2 * HD + j
+                chip = lax.div(row, deep)
+                at = pl.multiple_of(192 + lax.rem(row, deep), 32)
+                low_grads[lax.div(chip, 4), lax.rem(chip, 4), pl.ds(at, 32)] = rows[j : j + 32].astype(low)
+
+        @pl.when(pair + 2 < pairs)
+        def _():
+            shares_copy(pair + 2).start()
+
+        return carry
+
+    lax.fori_loop(0, pairs, attend_turn, 0)
+
+    mixing.wait()
+    for copy in kept:
+        copy.wait()
+    d_first = table[0:size]
+    for third, ref in enumerate((q, k, v)):
+        at = 48 + 48 * third
+        upstream = ref[...]
+        d_first = d_first + dot_nt(upstream, low_grads[:, :, at : at + 48].reshape(-1, model))
+        grad = dot_tn(normed[...], upstream).astype(low)
+        low_grads[:, :, at : at + 48] = grad.reshape(layers, 4, 48, model)
+    whitened = jnp.concatenate([table[size : 2 * size - rest], out[0:rest]], 0)
+    d_rows, gain, bias = norm_back(d_first, whitened, scale[...], gains[0:1])
+    boxes = jnp.concatenate([sines[...], cosines[...]], 1).astype(low)
+    grad = dot_tn(d_rows.astype(low), boxes).astype(low)
+    low_grads[:, :, 0:48] = grad.reshape(layers, 4, 48, model)
+    for index in (spot_ab, spot_a, spot_b, spot):
+        pair_copy(1, index).start()
+    mask = mask_col[...]
+    token_grads = jnp.where(mask == 1.0, pos_rows[...].astype(wide), d_rows).astype(low)
+    mask_grad = jnp.sum(mask * d_rows, 0, keepdims=True)
+    slots = sent.shape[0] * sent.shape[1]
+    seats = lax.broadcasted_iota(jnp.int32, (size, slots), 1) == place[...]
+    found = dot_tn(jnp.where(seats, 1.0, 0.0).astype(low), token_grads)
+    line = lax.broadcasted_iota(jnp.int32, (slots, 1), 0)
+    sent[...] = jnp.where(line == fixed, mask_grad, found).astype(low).reshape(sent.shape)
+    lines = jnp.concatenate([gain, bias, upper_norms[...]], 0)
+    cols = model // n
+    small[...] = jnp.zeros_like(small)
+    for owner in range(n):
+        small[owner, 0:6, 0:cols] = lines[:, owner * cols : (owner + 1) * cols]
+
+    def row_copies(step):
+        peer = lax.rem(me + step, n)
+        return [
+            remote_copy(src.at[peer], dst.at[me], row_send.at[j, step], row_recv.at[j, step], peer)
+            for j, (src, dst) in enumerate(((sent, came), (small, small_came)))
+        ]
+
+    def start_rows(step, carry):
+        for copy in row_copies(step):
+            copy.start()
+        return carry
+
+    def finish_rows(step, carry):
+        for copy in row_copies(step):
+            copy.wait()
+        return carry
+
+    lax.fori_loop(1, n, start_rows, 0)
+    came[me] = sent[me]
+    small_came[me] = small[me]
+
+    cross_z(0, 0)
+    arrived(1, spot_ab)
+    cross_b(1, 0)
+    arrived(1, spot_b)
+    cross_b(1, 1)
+    for part in range(1, parts[0]):
+        cross_z(0, part)
+    arrived(1, spot_a)
+    arrived(1, spot)
+    for part in range(parts[1]):
+        cross_a(1, part)
+    for part in range(parts[1]):
+        cross_z(1, part)
+    lax.fori_loop(1, n, finish_rows, 0)
+    wanted = lax.broadcasted_iota(jnp.int32, (table.shape[0], 128), 0) + 1
+    group = 128 // sent.shape[1]
+    for turn in range(n // fold):
+        ids = asked[turn * fold]
+        for j in range(1, fold):
+            ids = ids + asked[turn * fold + j]
+        picks = jnp.where(ids[6:7].astype(jnp.int32) == wanted, 1.0, 0.0).astype(low)
+        found = dot_nn(picks, came[turn * group : (turn + 1) * group].reshape(128, model))
+        if turn == 0:
+            table[...] = found
+        else:
+            table[...] += found
+    squares = jnp.zeros((1, 1), wide)
+    for part in range(4):
+        rows = table.shape[0] // 4
+        piece = table[part * rows : (part + 1) * rows]
+        squares = squares + jnp.sum(piece * piece, keepdims=True)
+    norm = small_came[0]
+    for j in range(1, n):
+        norm = norm + small_came[j]
+    norm_piece[...] = norm
+    squares = squares + jnp.sum(norm * norm, keepdims=True)
+    for g in range(2):
+        for part in range(parts[g]):
+            last_z(g, part)
+
+    at = 0
+    for piece in pieces:
+        offset, rows = 2 * at, 24 * piece
+        gone[pl.ds(at, rows)] = mine[pl.ds(pl.multiple_of(offset + (1 - core) * rows, 8), rows)]
+        out[pl.ds(at, rows), here] = mine[pl.ds(pl.multiple_of(offset + core * rows, 8), rows)]
+        at += rows
+    last = remote_copy(gone, back, f_send, f_recv, partner)
+    last.start()
+    squares = squares + jnp.sum(out[:, here] * out[:, here], keepdims=True)
+    last.wait()
+    out[:, there] = back[...]
+    squares = squares + jnp.sum(back[...] * back[...], keepdims=True)
+    lane = lax.broadcasted_iota(jnp.int32, message.shape, 1)
+    message[...] = jnp.where(lane == 0, squares, jnp.where(lane == 1, loss_part[...], 0.0))
+
+    def tell(step):
+        peer = lax.rem(me + step, n)
+        return remote_copy(message, told.at[me], t_send.at[step], t_recv.at[step], peer)
+
+    def start_told(step, carry):
+        tell(step).start()
+        return carry
+
+    def wait_told(step, carry):
+        tell(step).wait()
+        return carry
+
+    lax.fori_loop(1, n, start_told, 0)
+    told[me] = message[...]
+    for g in range(2):
+        for index in range(4):
+            pair_copy(g, index).wait_send()
+
+        def settle(turn, carry, g=g):
+            part, level = lax.div(turn, layers), lax.rem(turn, layers)
+            b_copy(g, 0, level, part).wait_send()
+            b_copy(g, 1, level, part).wait_send()
+            a_copy(g, level, part).wait_send()
+
+            @pl.when(level != layer)
+            def _():
+                z_copy(g, level, part).wait_send()
+
+            return carry
+
+        lax.fori_loop(0, layers * parts[g], settle, 0)
+    lax.fori_loop(1, n, wait_told, 0)
+    total_line = told[0]
+    for j in range(1, n):
+        total_line = total_line + told[j]
+    totals[...] = total_line
+
+
+def behind(in_hbm, in_vmem, rows_own, early, pieces, capacity, fold, fixed, n, ident):
+    size, model = in_vmem[0].shape
+    layers = n // 8
+    bulk = in_hbm[1].shape[2]
+    rows = bulk + early
+    half = model // 2
+    most = max(bulk, early) // 144
+    low, wide = jnp.bfloat16, jnp.float32
+    dma = pltpu.SemaphoreType.DMA
+    vmem = pl.BlockSpec(memory_space=pltpu.VMEM)
+    anywhere = pl.BlockSpec(memory_space=pl.ANY)
+    shape = jax.ShapeDtypeStruct
+    tile = shape((8, 128), wide)
+    return pl.pallas_call(
+        partial(behind_kernel, n, early, pieces, fold, fixed),
+        name="behind",
+        out_shape=(shape((rows // 2, model), wide), shape((rows_own, model), wide), tile, tile),
+        in_specs=[anywhere] * len(in_hbm) + [vmem] * len(in_vmem),
+        out_specs=(vmem,) * 4,
+        scratch_shapes=[
+            pltpu.VMEM((2 * model, model), low),
+            pltpu.VMEM((layers, 4, early, model), low),
+            pltpu.VMEM((2, 2, size, size), low),
+            pltpu.VMEM((size, model), low),
+            pltpu.VMEM((size, model), low),
+            pltpu.VMEM((size, model), low),
+            pltpu.VMEM((n, capacity, model), low),
+            pltpu.VMEM((n, 8, 128), wide),
+            pltpu.VMEM((layers, 4, bulk, half), low),
+            pltpu.VMEM((layers, 4, bulk, half), low),
+            pltpu.VMEM((layers, 4, early, half), low),
+            pltpu.VMEM((2, layers, rows, half), low),
+            pltpu.VMEM((layers, rows, half), low),
+            pltpu.VMEM((layers, rows, half), low),
+            pltpu.VMEM((rows, half), wide),
+            pltpu.VMEM((rows // 2, half), wide),
+            pltpu.VMEM((rows // 2, half), wide),
+            pltpu.VMEM((n, capacity, model), low),
+            pltpu.VMEM((n, 8, 128), wide),
+            pltpu.VMEM((8, 128), wide),
+            pltpu.VMEM((n, 8, 128), wide),
+            dma((2, n)),
+            dma((2, n)),
+            dma((2,)),
+            dma((4,)),
+            dma((2, 4)),
+            dma((2, 4)),
+            dma((8,)),
+            dma((2,)),
+            dma((2, 2, layers, most)),
+            dma((2, 2, layers, most)),
+            dma((2, layers, most)),
+            dma((2, layers, most)),
+            dma((2, layers, most)),
+            dma((2, layers, most)),
+            dma,
+            dma,
+            dma((n,)),
+            dma((n,)),
+        ],
+        compiler_params=pltpu.CompilerParams(
+            collective_id=ident, has_side_effects=True, vmem_limit_bytes=64 * 2**20 - 2**17
+        ),
+        cost_estimate=pl.CostEstimate(
+            flops=20 * 10**9, bytes_accessed=100 * 2**20, transcendentals=0
+        ),
+    )(*in_hbm, *in_vmem)
 
 
 def forward(weights, rows, positions):
@@ -1604,9 +1666,8 @@
     ) = ahead(
         lists, vocabulary, bank_piece, positions, place, mask_col, pieces, early, n, capacity, 1
     )
-    full = full.reshape(-1, *full.shape[2:])
     upper_grads, d_attended, d_lower, positive_rows, upper_norms, loss_part = upper(
-        full,
+        full.reshape(-1, *full.shape[2:]),
         attended,
         normed,
         target,
@@ -1619,32 +1680,39 @@
         blocks,
         page_rows,
     )
-    rel_map = full[:, 192:early].reshape(-1, model)
-    *d_joined, grad_rel = attend_back(d_attended, joined, rel_map, probs, sines, cosines, bases)
     fixed = (mask_token // rows_own) * capacity + capacity - 1
-    lower_grads, sent, norm_blocks = lower(
-        full,
-        d_joined,
-        d_lower,
-        white,
-        scale,
-        gains,
-        normed_low,
-        sines,
-        cosines,
-        mask_col,
-        positive_rows,
-        place,
-        upper_norms,
+    sums, table_piece, norm_piece, totals = behind(
+        (
+            full,
+            upper_grads.reshape(*full.shape[:2], -1, model),
+            probs,
+            d_lower,
+            white,
+            *joined,
+        ),
+        (
+            d_attended,
+            sines,
+            cosines,
+            bases,
+            scale,
+            gains,
+            normed_low,
+            mask_col,
+            positive_rows,
+            place,
+            upper_norms,
+            asked,
+            loss_part,
+        ),
+        rows_own,
+        early,
+        (1,) + (1,) * blocks + (narrowing.shape[0] // 24, 1, 1, 1, 1, 2),
+        capacity,
+        fold,
+        fixed,
         n,
-        slots,
-        fixed,
-    )
-    grads = [lower_grads, grad_rel.reshape(n // 2, -1, model), upper_grads]
-    parts = (1, 1, 1, 1, 2, 1) + (1,) * blocks + (narrowing.shape[0] // 24,)
-    sent = sent.reshape(n, capacity, model)
-    sums, table_piece, norm_piece, totals = to_owners(
-        sent, norm_blocks, asked, loss_part, grads, parts, rows_own, fold, n, 2
+        2,
     )
 
     def finish():
@@ -1653,13 +1721,14 @@
         last = step(
             scaling, moment_scaling, average_scaling, norm_piece[:6, :cols], learn_rate, factor
         )
+        row = 24 * (1 + blocks) + narrowing.shape[0]
         layout = (
-            (1, 0, 1, 24, True),
-            (2, 24, 3, 24, False),
-            (3, 96, 1, 48, True),
-            (4, 144, 1, 24, False),
-            (5, 168, blocks, 24, False),
-            (6, 168 + 24 * blocks, 1, narrowing.shape[0], False),
+            (1, row, 1, 24, True),
+            (2, row + 24, 3, 24, False),
+            (3, row + 96, 1, 48, True),
+            (4, 0, 1, 24, False),
+            (5, 24, blocks, 24, False),
+            (6, 24 * (1 + blocks), 1, narrowing.shape[0], False),
         )
         lay = lambda group: [group[0], group[1].T, group[2], group[3].T, *group[4:7]]
         groups = [lay(group) for group in (masters, moments, averages)]

time: 389 us -> 361 us (0.928)
  Pallas kernels: 349 us -> 325 us
    pallas_call x3 -> x1, Pallas kernels: 173 us -> 148 us  [behind(): pl.pallas_call(partial(behind_kernel, n, early, pieces, fold, fixed), nam...]
where the time goes in v5:
time: 361 us; the launch traced here: 356 us
  Pallas kernels  325 us (90%)
  between operations  17.2 us (5%)
  local copies, waits for them, and re-layouts  9.26 us (3%)
    pallas_call x1, Pallas kernels, behind(): pl.pallas_call(partial(behind_kernel, n, early, pieces, fold, fixed), nam...  148 us
    pallas_call x1, Pallas kernels, ahead(): pl.pallas_call(partial(ahead_kernel, n, units, early, capacity), name='ah...  131 us
    pallas_call x1, Pallas kernels, upper(): pl.pallas_call(partial(upper_kernel, page_rows), name='upper', out_shape=...  33.1 us
    pallas_call x1, Pallas kernels, update_all(): pl.pallas_call(partial(update_kernel, decay, layout), name='update', grid...  11.1 us

profile of v5, /device:TPU:0, one launch (start us, length us, event | category | flops | bytes accessed | tf_op | source)
XLA Modules:
  0.0 355.6 jit_solution(16387197150478378105)
XLA Ops:
  7.3 1.1 fusion.70
  8.4 0.1 maximum_bitcast_fusion.refs_11_
  8.5 0.9 fusion.71
  9.4 0.1 maximum_bitcast_fusion.1.refs_7_
  9.5 1.2 fusion.68
  10.8 0.9 copy.161.refs_6_.mask_col.refs_15_
  12.3 0.1 pad_add_fusion.own
  12.4 0.1 copy.159.tok_col
  12.6 1.8 plan.1
  14.4 0.7 copy-done
  15.1 0.7 copy-done.1
  15.8 0.9 copy.160
  16.7 0.1 pad_maximum_fusion.11
  16.7 0.6 broadcast_in_dim.79.refs_4_
  17.3 130.8 %ahead.1 = (f32[32,8,128]{2,1,0:T(8,128)}, bf16[4,4,848,768]{3,2,1,0:T(8,128)(2,1)}, bf16[12,512,512]{2,1,0:T(8,128)(2,1)}, f32[512,384]{1,0:T(8,128)}, f32[512,...) custom-call(f32[32,8,128]{2,1,0:T(8,128)} %copy-done.1, ...), custom_call_target="tpu_custom_call" | custom-call | flops 12999999488 | bytes 104857600 | tf_op jit(solution)/shard_map/ahead/pallas_call | solution.py:904
  148.3 33.1 %upper.1 = (bf16[16,432,768]{2,1,0:T(8,128)(2,1)}, bf16[512,768]{1,0:T(8,128)(2,1)}, f32[512,768]{1,0:T(8,128)}, bf16[512,768]{1,0:T(8,128)(2,1)}, f32[4,768]{1,0:T(4,128)}, /*index=5*/f32[1,1]{1,0:T(1,128)}) custom-call(bf16[16,848,768]{2,1,0:T(8,128)(2,1)} %bitcast.323, bf16[512,768]{1,0:T(8,128)(2,1)} %get-tuple-element.360.attended, ...), custom_call_target="tpu_custom_call" | custom-call | flops 20000000000 | bytes 33554432 | tf_op jit(solution)/shard_map/upper/pallas_call | solution.py:307
  181.4 147.8 %behind.1 = (f32[360,768]{1,0:T(8,128)}, f32[960,768]{1,0:T(8,128)}, f32[8,128]{1,0:T(8,128)S(1)}, f32[8,128]{1,0:T(8,128)S(1)}) custom-call(bf16[4,4,848,768]{3,2,1,0:T(8,128)(2,1)} %get-tuple-element.359.refs_0_, bf16[4,4,432,768]{3,2,1,0:T(8,128)(2,1)} %bitcast.324, bf16[12,512,512]{2,1,0:T(8,128)(2,1)} %get-tuple-element.365.refs_2_, ...), custom_call_target="tpu_custom_call" | custom-call | flops 20000000000 | bytes 104857600 | tf_op jit(solution)/shard_map/behind/pallas_call | solution.py:1336
  329.2 1.6 slice_reduce_fusion.6
  331.5 14.2 %conditional.1 = (f32[24,2304]{1,0:T(8,128)S(1)}, f32[24,768]{1,0:T(8,128)S(1)}, f32[24,3072]{1,0:T(8,128)S(1)}, f32[96,768]{1,0:T(8,128)S(1)}, f32[24,2304]{1,0...) conditional(s32[]{:T(128)} %convert_element_type.211, ...), branch_computations={%region_1.2_spmd, %region_2.47_spmd} | conditional | flops 52047237120 | bytes 1115460224 | solution.py:1742
  331.5 0.6 fusion.58
  332.8 11.1 %update.1 = (f32[960,768]{1,0:T(8,128)}, f32[24,768]{1,0:T(8,128)S(1)}, f32[24,2304]{1,0:T(8,128)S(1)}, f32[48,768]{1,0:T(8,128)S(1)}, f32[24,768]{1,0:T(8,128)S...) custom-call(f32[1,1]{1,0:T(1,128)} %bitcast.1.factor, ...), custom_call_target="tpu_custom_call" | custom-call | bytes 29360128 | tf_op jit(solution)/shard_map/cond/branch_0_fun/update/pallas_call | solution.py:373
  343.9 0.6 multiply_add_fusion
  345.9 0.5 copy-done.138
  346.4 0.1 copy-done.139
  346.5 0.1 copy-done.140
  346.6 0.1 copy-done.141
  346.7 0.1 copy-done.142
  346.8 0.1 copy-done.143
  346.9 0.1 copy-done.144
  347.0 0.1 copy-done.145
  347.0 0.1 copy-done.146
  347.1 0.0 copy-done.147
  (72 shorter events, 0.5 us)
Async XLA Ops:
  7.2 3.6 %copy-start.119 = (s32[512]{0:T(512)S(1)}, s32[512]{0:T(512)}, u32[]{:S(2)}) copy-start(s32[512]{0:T(512)} %param.40) | copy-start | bytes 6148
  7.2 5.2 %copy-start.83 = (s32[512]{0:T(512)S(1)}, s32[512]{0:T(512)}, u32[]{:S(2)}) copy-start(s32[512]{0:T(512)} %param.37) | copy-start | bytes 6148
  7.2 5.4 %copy-start.110 = (f32[6,24]{1,0:T(8,128)S(1)}, f32[6,24]{1,0:T(8,128)}, u32[]{:S(2)}) copy-start(f32[6,24]{1,0:T(8,128)} %param.51) | copy-start | bytes 1732
  7.2 10.1 %copy-start.108 = (bf16[1,64,768]{2,1,0:T(8,128)(2,1)S(1)}, bf16[1,64,768]{2,1,0:T(8,128)(2,1)}, u32[]{:S(2)}) copy-start(bf16[1,64,768]{2,1,0:T(8,128)(2,1)} %param.43) | copy-start | bytes 294916
  7.2 8.5 %copy-start.128 = (s32[2,512]{1,0:T(2,128)S(1)}, s32[2,512]{1,0:T(2,128)}, u32[]{:S(2)}) copy-start(s32[2,512]{1,0:T(2,128)} %param.38) | copy-start | bytes 12292
  7.3 10.1 %copy-start.64 = (f32[24,768]{1,0:T(8,128)S(1)}, f32[24,768]{1,0:T(8,128)}, u32[]{:S(2)}) copy-start(f32[24,768]{1,0:T(8,128)} %refs_12_.1) | copy-start | bytes 221188
  7.3 10.0 %copy-start.11 = (f32[96,768]{1,0:T(8,128)S(1)}, f32[96,768]{1,0:T(8,128)}, u32[]{:S(2)}) copy-start(f32[96,768]{1,0:T(8,128)} %refs_17_.1) | copy-start | bytes 884740
  8.5 139.7 %copy-start.79 = (f32[48,768]{1,0:T(8,128)}, f32[48,768]{1,0:T(8,128)S(1)}, u32[]{:S(2)}) copy-start(f32[48,768]{1,0:T(8,128)S(1)} %maximum_bitcast_fusion.refs_11_) | copy-start | bytes 442372
  9.5 138.7 %copy-start.97 = (f32[24,768]{1,0:T(8,128)}, f32[24,768]{1,0:T(8,128)S(1)}, u32[]{:S(2)}) copy-start(f32[24,768]{1,0:T(8,128)S(1)} %maximum_bitcast_fusion.1.refs_7_) | copy-start | bytes 221188
  10.7 137.5 %copy-start.90 = (f32[24,768]{1,0:T(8,128)}, f32[24,768]{1,0:T(8,128)S(1)}, u32[]{:S(2)}) copy-start(f32[24,768]{1,0:T(8,128)S(1)} %get-tuple-element.913.refs_16_) | copy-start | bytes 221188
  10.7 137.5 %copy-start.91 = (f32[24,768]{1,0:T(8,128)}, f32[24,768]{1,0:T(8,128)S(1)}, u32[]{:S(2)}) copy-start(f32[24,768]{1,0:T(8,128)S(1)} %get-tuple-element.914.refs_15_) | copy-start | bytes 221188
  10.7 137.5 %copy-start.92 = (f32[24,768]{1,0:T(8,128)}, f32[24,768]{1,0:T(8,128)S(1)}, u32[]{:S(2)}) copy-start(f32[24,768]{1,0:T(8,128)S(1)} %get-tuple-element.915.refs_14_) | copy-start | bytes 221188
  10.8 137.5 %copy-start.93 = (f32[24,768]{1,0:T(8,128)}, f32[24,768]{1,0:T(8,128)S(1)}, u32[]{:S(2)}) copy-start(f32[24,768]{1,0:T(8,128)S(1)} %get-tuple-element.916.refs_13_) | copy-start | bytes 221188
  10.8 137.5 %copy-start.94 = (f32[24,768]{1,0:T(8,128)}, f32[24,768]{1,0:T(8,128)S(1)}, u32[]{:S(2)}) copy-start(f32[24,768]{1,0:T(8,128)S(1)} %get-tuple-element.928.refs_8_) | copy-start | bytes 221188
  10.8 137.5 %copy-start.95 = (f32[24,768]{1,0:T(8,128)}, f32[24,768]{1,0:T(8,128)S(1)}, u32[]{:S(2)}) copy-start(f32[24,768]{1,0:T(8,128)S(1)} %get-tuple-element.929.refs_9_) | copy-start | bytes 221188
  10.8 137.5 %copy-start.96 = (f32[24,768]{1,0:T(8,128)}, f32[24,768]{1,0:T(8,128)S(1)}, u32[]{:S(2)}) copy-start(f32[24,768]{1,0:T(8,128)S(1)} %get-tuple-element.930.refs_10_) | copy-start | bytes 221188
  17.3 131.0 %copy-start.125 = (s32[8,512]{1,0:T(8,128)S(1)}, s32[8,512]{1,0:T(8,128)}, u32[]{:S(2)}) copy-start(s32[8,512]{1,0:T(8,128)} %page.1) | copy-start | bytes 49156
  17.3 131.0 %copy-start.126 = (s32[8,512]{1,0:T(8,128)S(1)}, s32[8,512]{1,0:T(8,128)}, u32[]{:S(2)}) copy-start(s32[8,512]{1,0:T(8,128)} %row.1) | copy-start | bytes 49156
  181.4 150.1 %copy-start.129 = (f32[6,24]{1,0:T(8,128)S(1)}, f32[6,24]{1,0:T(8,128)}, u32[]{:S(2)}) copy-start(f32[6,24]{1,0:T(8,128)} %param.59) | copy-start | bytes 1732
  181.4 150.1 %copy-start.132 = (f32[6,24]{1,0:T(8,128)S(1)}, f32[6,24]{1,0:T(8,128)}, u32[]{:S(2)}) copy-start(f32[6,24]{1,0:T(8,128)} %param.67) | copy-start | bytes 1732
  345.8 1.2 copy-start.144
  345.8 1.3 copy-start.145
  345.8 1.3 copy-start.146
  345.8 1.4 copy-start.147
  345.8 1.4 copy-start.148
  345.8 1.4 copy-start.149
  345.8 1.4 copy-start.150
  345.8 1.4 copy-start.151
  345.9 1.5 copy-start.152
  345.9 1.5 copy-start.153
  345.9 1.5 copy-start.154
  345.9 1.5 copy-start.155
  (8 other events, 6.9 us)

commit v6 on v5

--- a/solution.py
+++ b/solution.py
@@ -75,11 +75,14 @@
 
 
 def plan_kernel(
-    n, rows_own, capacity, fold, tok_col, tok_row, mask_row, own, info, lists, place
+    n, rows_own, capacity, fold, tok_row, mask_row, own, info, lists, place, mask_col
 ):
-    size = tok_col.shape[0]
-    ids_col = tok_col[...]
+    size = tok_row.shape[1]
     ids_row = tok_row[...]
+    line = lax.broadcasted_iota(jnp.int32, (8, size), 0)
+    columns = jnp.where(line == 0, ids_row, mask_row[...]).astype(jnp.float32).T
+    ids_col = columns[:, 0:1].astype(jnp.int32)
+    mask_col[...] = columns[:, 1:2]
     owner_col = lax.div(ids_col, rows_own)
     owner_row = lax.div(ids_row, rows_own)
     at_col = lax.broadcasted_iota(jnp.int32, (size, size), 0)
@@ -126,12 +129,12 @@
         out_shape=(
             jax.ShapeDtypeStruct((n, 8, 128), jnp.float32),
             jax.ShapeDtypeStruct((size, 1), jnp.int32),
+            jax.ShapeDtypeStruct((size, 1), jnp.float32),
         ),
-        in_specs=[vmem, vmem, vmem, pl.BlockSpec(memory_space=pltpu.SMEM), vmem],
-        out_specs=(vmem, vmem),
+        in_specs=[vmem, vmem, pl.BlockSpec(memory_space=pltpu.SMEM), vmem],
+        out_specs=(vmem,) * 3,
         compiler_params=pltpu.CompilerParams(vmem_limit_bytes=32 * 2**20),
     )(
-        tokens[:, None],
         tokens[None, :],
         masking[None, :],
         jnp.stack([documents[0], lax.axis_index("dp")]),
@@ -541,16 +544,16 @@
     )(d_attended, *joined, rel_map, rel_map, probs, sines, cosines, bases)
 
 
-def ahead_kernel(n, units, early, capacity, *refs):
-    count = len(units)
-    lists, vocabulary, pages, points, omegas, place, mask_col = refs[:7]
+def ahead_kernel(n, layout, early, capacity, *refs):
+    count = 1 + max(source for source, _, _ in layout)
+    lists, vocabulary, pages, positions, omegas, place, mask_col = refs[:7]
     weights = refs[7 : 7 + count]
     outs = refs[7 + count : 23 + count]
     asked, full, probs, sines, cosines, bases, target_out, normed_out, white_out, scale_out, low_out = outs[:11]
     q, k, v, attended, gains = outs[11:]
-    swap_out, swap_in, chip_rows, answers, rows, held, rel_map, shares = refs[23 + count : 31 + count]
-    ask_send, ask_recv, row_send, row_recv, own_sem, swap_send, swap_recv = refs[31 + count : 38 + count]
-    hop_recv, core_recv, core_send, z_send, a_send, b_send, load_sem, out_sem = refs[38 + count :]
+    swap_out, swap_in, chip_rows, answers, rows, held, rel_map, shares, turned = refs[23 + count : 32 + count]
+    ask_send, ask_recv, row_send, row_recv, own_sem, swap_send, swap_recv = refs[32 + count : 39 + count]
+    hop_recv, core_recv, core_send, z_send, a_send, b_send, load_sem, out_sem = refs[39 + count :]
     low = jnp.bfloat16
     me = lax.axis_index("dp")
     core, spot, layer, step_a, step_b = place_of(me)
@@ -565,9 +568,19 @@
     low_z, high_z = layer > 0, layer < layers - 1
     cuts = (pl.ds(0, early), pl.ds(early, chip_rows.shape[0] - early))
 
+    high = weights[0].shape[0]
+    turned[0:high] = swap_middle(weights[0][...], 1)
+    turned[high:] = swap_middle(weights[1][...], 1)
+
+    def piece(source, column, side):
+        lanes = pl.ds(pl.multiple_of(column + side * half, 128), half)
+        if source == 0:
+            return turned[0:high, lanes]
+        return turned[high:, lanes] if source == 1 else weights[source][:, lanes]
+
     at = 0
-    for ref, unit in zip(weights, units):
-        swap_out[pl.ds(at, 24 * unit)] = ref[:, there]
+    for source, column, unit in layout:
+        swap_out[pl.ds(at, 24 * unit)] = piece(source, column, 1 - core)
         at += 24 * unit
     greet_everyone(me, n)
     swaps = [
@@ -601,8 +614,8 @@
     for copy in swaps:
         copy.wait_recv()
     at = 0
-    for ref, unit in zip(weights, units):
-        mine, other = ref[:, here], swap_in[pl.ds(at, 24 * unit)]
+    for source, column, unit in layout:
+        mine, other = piece(source, column, core), swap_in[pl.ds(at, 24 * unit)]
         ordered = jnp.where(
             core == 0, jnp.concatenate([mine, other], 0), jnp.concatenate([other, mine], 0)
         )
@@ -770,6 +783,8 @@
             asked[source, :, 0:cols].astype(low).astype(jnp.float32)
         )
     lane = lax.broadcasted_iota(jnp.int32, sines.shape, 1)
+    line = lax.broadcasted_iota(jnp.int32, (8, sines.shape[0]), 0)
+    points = jnp.where(line == 0, positions[0:1], positions[1:2]).astype(jnp.float32).T
     angles = jnp.where(lane < sines.shape[1] // 2, points[:, 0:1], points[:, 1:2]) * omegas[...]
     sines[...] = jnp.sin(angles)
     cosines[...] = jnp.cos(angles)
@@ -883,16 +898,14 @@
     lax.fori_loop(1, n, finish_rows, 0)
 
 
-def ahead(lists, vocabulary, pages, positions, place, mask_col, weights, early, n, capacity, ident):
+def ahead(lists, vocabulary, pages, positions, place, mask_col, weights, layout, early, n, capacity, ident):
     model = vocabulary.shape[1]
     size = place.shape[0]
     layers = n // 8
-    units = [weight.shape[0] // 24 for weight in weights]
-    points = positions.astype(jnp.float32).T
     waves = model // 4
     omegas = jnp.power(10000.0, -jnp.arange(waves).astype(jnp.float32) / waves)
     omegas = jnp.concatenate([omegas, omegas])[None]
-    swap = 24 * sum(units)
+    swap = 24 * sum(unit for _, _, unit in layout)
     chip = 2 * (swap + pages.shape[0])
     low, wide = jnp.bfloat16, jnp.float32
     dma = pltpu.SemaphoreType.DMA
@@ -902,7 +915,7 @@
     rows = lambda kind: shape((size, model), kind)
     heads = model // HD
     return pl.pallas_call(
-        partial(ahead_kernel, n, units, early, capacity),
+        partial(ahead_kernel, n, layout, early, capacity),
         name="ahead",
         out_shape=(
             shape(lists.shape, lists.dtype),
@@ -933,6 +946,7 @@
             pltpu.VMEM((layers, 4, 192, model), low),
             pltpu.VMEM((2 * model, model), low),
             pltpu.VMEM((2, 2, size, size), low),
+            pltpu.VMEM((weights[0].shape[0] + weights[1].shape[0], model), wide),
             dma((n,)),
             dma((n,)),
             dma((n,)),
@@ -955,7 +969,7 @@
         cost_estimate=pl.CostEstimate(
             flops=13 * 10**9, bytes_accessed=100 * 2**20, transcendentals=0
         ),
-    )(lists, vocabulary, pages, points, omegas, place, mask_col, *weights)
+    )(lists, vocabulary, pages, positions, omegas, place, mask_col, *weights)
 
 
 def behind_kernel(n, early, pieces, fold, fixed, *refs):
@@ -963,10 +977,10 @@
     scale, gains, normed, mask_col, pos_rows, place, upper_norms, asked, loss_part = refs[12:21]
     out, table, norm_piece, totals = refs[21:25]
     rel_map, low_grads, shares, q, k, v, sent, small = refs[25:33]
-    own, par, par_low, from_b, from_a, from_z, mine, gone, back = refs[33:42]
-    came, small_came, message, told = refs[42:46]
-    row_send, row_recv, own_sem, load_sem, pair_send, pair_recv, local_sem, share_sem = refs[46:54]
-    b_send, b_recv, a_send, a_recv, z_send, z_recv, f_send, f_recv, t_send, t_recv = refs[54:]
+    own, par, par_low, from_b, from_a, from_z, chained, mine, gone, back = refs[33:43]
+    came, small_came, message, told = refs[43:47]
+    row_send, row_recv, load_sem, pair_send, pair_recv, local_sem, share_sem = refs[47:54]
+    b_send, b_recv, a_send, a_recv, z_send, z_recv, c_send, c_recv, f_send, f_recv, t_send, t_recv = refs[54:]
     low, wide = jnp.bfloat16, jnp.float32
     layers = n // 8
     me = lax.axis_index("dp")
@@ -979,6 +993,7 @@
     partner = me + 1 - 2 * core
     to_a, to_b = me + 2 * step_a, me + 2 * step_b
     spot_a, spot_b, spot_ab = spot + step_a, spot + step_b, spot + step_a + step_b
+    low_z, high_z = layer > 0, layer < layers - 1
     bulk = own.shape[2]
     chunk = 144
     parts = (bulk // chunk, early // chunk)
@@ -1061,11 +1076,23 @@
             a_send.at[g, level, part], a_recv.at[g, level, part], to_a,
         )
 
-    def z_copy(g, level, part):
+    def z_copy(level, part):
         return remote_copy(
-            mine_at(g, level, spot, part), from_z.at[layer, cut_of(g, part)],
-            z_send.at[g, level, part], z_recv.at[g, layer, part], me + 8 * (level - layer),
-        )
+            mine_at(1, level, spot, part), from_z.at[layer, pl.ds(part * chunk, chunk)],
+            z_send.at[level, part], z_recv.at[layer, part], me + 8 * (level - layer),
+        )
+
+    def chain_copy(way, gap, level, part):
+        place = layers if way == 1 and gap == 1 else level
+        return remote_copy(
+            mine_at(0, level, spot, part), chained.at[place, pl.ds(part * chunk, chunk)],
+            c_send.at[level, part], c_recv.at[place, part], me + (8 if way == 0 else -8),
+        )
+
+    def chain_part(place, part):
+        view = chained.at[place, pl.ds(part * chunk, chunk)]
+        pltpu.make_async_copy(view, view, c_recv.at[place, part]).wait()
+        return total(view)
 
     def cross_b(g, kind):
         index = spot_ab if kind == 0 else spot_b
@@ -1100,25 +1127,65 @@
             from_b.at[1, level, cut], from_a.at[level, cut],
         )
 
-    def cross_z(g, part):
+    def chain(gap):
+        for way, guard, further, level in (
+            (0, layer + gap < layers, low_z, layer + gap),
+            (1, layer - gap >= 0, high_z, layer - gap),
+        ):
+
+            def step(part, carry, way=way, level=level, further=further):
+                view = mine_at(0, level, spot, part)
+                value = column(0, level, part)
+
+                @pl.when(further)
+                def _():
+                    view[...] = (value + chain_part(level, part)).astype(low)
+
+                @pl.when(jnp.logical_not(further))
+                def _():
+                    view[...] = value.astype(low)
+
+                chain_copy(way, gap, level, part).start()
+                return carry
+
+            @pl.when(guard)
+            def _():
+                lax.fori_loop(0, parts[0], step, 0)
+
+    def chain_end():
+        def step(part, carry):
+            cut = pl.ds(part * chunk, chunk)
+            mine[cut] = column(0, layer, part)
+
+            @pl.when(low_z)
+            def _():
+                mine[cut] += chain_part(layer, part)
+
+            @pl.when(high_z)
+            def _():
+                mine[cut] += chain_part(layers, part)
+
+            return carry
+
+        lax.fori_loop(0, parts[0], step, 0)
+
+    def cross_z(part):
         def step(gap, carry):
             level = lax.rem(layer + gap, layers)
-            view = mine_at(g, level, spot, part)
-            view[...] = column(g, level, part).astype(low)
-            z_copy(g, level, part).start()
+            view = mine_at(1, level, spot, part)
+            view[...] = column(1, level, part).astype(low)
+            z_copy(level, part).start()
             return carry
 
         lax.fori_loop(1, layers, step, 0)
-        mine[cut_of(g, part)] = column(g, layer, part)
-
-    def last_z(g, part):
-        cut = cut_of(g, part)
-
+        mine[cut_of(1, part)] = column(1, layer, part)
+
+    def last_z(part):
         def step(gap, carry):
             level = lax.rem(layer + gap, layers)
-            view = from_z.at[level, cut]
-            pltpu.make_async_copy(view, view, z_recv.at[g, level, part]).wait()
-            mine[cut] += total(view)
+            view = from_z.at[level, pl.ds(part * chunk, chunk)]
+            pltpu.make_async_copy(view, view, z_recv.at[level, part]).wait()
+            mine[cut_of(1, part)] += total(view)
             return carry
 
         lax.fori_loop(1, layers, step, 0)
@@ -1187,11 +1254,6 @@
         low_grads[:, :, at : at + 48] = grad.reshape(layers, 4, 48, model)
     whitened = jnp.concatenate([table[size : 2 * size - rest], out[0:rest]], 0)
     d_rows, gain, bias = norm_back(d_first, whitened, scale[...], gains[0:1])
-    boxes = jnp.concatenate([sines[...], cosines[...]], 1).astype(low)
-    grad = dot_tn(d_rows.astype(low), boxes).astype(low)
-    low_grads[:, :, 0:48] = grad.reshape(layers, 4, 48, model)
-    for index in (spot_ab, spot_a, spot_b, spot):
-        pair_copy(1, index).start()
     mask = mask_col[...]
     token_grads = jnp.where(mask == 1.0, pos_rows[...].astype(wide), d_rows).astype(low)
     mask_grad = jnp.sum(mask * d_rows, 0, keepdims=True)
@@ -1223,23 +1285,30 @@
             copy.wait()
         return carry
 
-    lax.fori_loop(1, n, start_rows, 0)
     came[me] = sent[me]
     small_came[me] = small[me]
 
-    cross_z(0, 0)
+    lax.fori_loop(1, n, start_rows, 0)
+    boxes = jnp.concatenate([sines[...], cosines[...]], 1).astype(low)
+    grad = dot_tn(d_rows.astype(low), boxes).astype(low)
+    low_grads[:, :, 0:48] = grad.reshape(layers, 4, 48, model)
+    for index in (spot_ab, spot_a, spot_b, spot):
+        pair_copy(1, index).start()
+
     arrived(1, spot_ab)
     cross_b(1, 0)
     arrived(1, spot_b)
     cross_b(1, 1)
-    for part in range(1, parts[0]):
-        cross_z(0, part)
+    chain(layers - 1)
+    for gap in range(layers - 2, 0, -1):
+        chain(gap)
     arrived(1, spot_a)
     arrived(1, spot)
     for part in range(parts[1]):
         cross_a(1, part)
+    chain_end()
     for part in range(parts[1]):
-        cross_z(1, part)
+        cross_z(part)
     lax.fori_loop(1, n, finish_rows, 0)
     wanted = lax.broadcasted_iota(jnp.int32, (table.shape[0], 128), 0) + 1
     group = 128 // sent.shape[1]
@@ -1263,9 +1332,8 @@
         norm = norm + small_came[j]
     norm_piece[...] = norm
     squares = squares + jnp.sum(norm * norm, keepdims=True)
-    for g in range(2):
-        for part in range(parts[g]):
-            last_z(g, part)
+    for part in range(parts[1]):
+        last_z(part)
 
     at = 0
     for piece in pieces:
@@ -1308,7 +1376,10 @@
 
             @pl.when(level != layer)
             def _():
-                z_copy(g, level, part).wait_send()
+                if g == 0:
+                    chain_copy(0, 2, level, part).wait_send()
+                else:
+                    z_copy(level, part).wait_send()
 
             return carry
 
@@ -1353,7 +1424,8 @@
             pltpu.VMEM((layers, 4, early, half), low),
             pltpu.VMEM((2, layers, rows, half), low),
             pltpu.VMEM((layers, rows, half), low),
-            pltpu.VMEM((layers, rows, half), low),
+            pltpu.VMEM((layers, early, half), low),
+            pltpu.VMEM((layers + 1, bulk, half), low),
             pltpu.VMEM((rows, half), wide),
             pltpu.VMEM((rows // 2, half), wide),
             pltpu.VMEM((rows // 2, half), wide),
@@ -1363,7 +1435,6 @@
             pltpu.VMEM((n, 8, 128), wide),
             dma((2, n)),
             dma((2, n)),
-            dma((2,)),
             dma((4,)),
             dma((2, 4)),
             dma((2, 4)),
@@ -1373,8 +1444,10 @@
             dma((2, 2, layers, most)),
             dma((2, layers, most)),
             dma((2, layers, most)),
-            dma((2, layers, most)),
-            dma((2, layers, most)),
+            dma((layers, most)),
+            dma((layers, most)),
+            dma((layers, most)),
+            dma((layers + 1, most)),
             dma,
             dma,
             dma((n,)),
@@ -1646,7 +1719,7 @@
     fold = 128 // capacity
     cols = scaling.shape[1]
     info = jnp.pad(scaling, ((0, 2), (0, 128 - cols)))
-    lists, place = make_plan(tokens, masking, documents, info, n, rows_own, capacity, fold)
+    lists, place, mask_col = make_plan(tokens, masking, documents, info, n, rows_own, capacity, fold)
     early = 48 * (1 + 3 + relative.shape[1] // 24)
     (
         asked,
@@ -1664,7 +1737,25 @@
         attended,
         gains,
     ) = ahead(
-        lists, vocabulary, bank_piece, positions, place, mask_col, pieces, early, n, capacity, 1
+        lists,
+        vocabulary,
+        bank_piece,
+        positions,
+        place,
+        mask_col,
+        (geometry.T, relative.T, mixing, merging, widening, narrowing),
+        (
+            (0, 0, 1),
+            *[(2, k * model, 1) for k in range(3)],
+            (1, 0, relative.shape[1] // 24),
+            (3, 0, 1),
+            *[(4, k * model, 1) for k in range(blocks)],
+            (5, 0, narrowing.shape[0] // 24),
+        ),
+        early,
+        n,
+        capacity,
+        1,
     )
     upper_grads, d_attended, d_lower, positive_rows, upper_norms, loss_part = upper(
         full.reshape(-1, *full.shape[2:]),

time: 361 us -> 350 us (0.970)
  Pallas kernels: 325 us -> 316 us
    pallas_call x1, Pallas kernels: 148 us -> 139 us  [behind(): pl.pallas_call(partial(behind_kernel, n, early, pieces, fold, fixed), nam...]
where the time goes in v6:
time: 350 us; the launch traced here: 345 us
  Pallas kernels  316 us (90%)
  between operations  17.1 us (5%)
  local copies, waits for them, and re-layouts  6.66 us (2%)
    pallas_call x1, Pallas kernels, behind(): pl.pallas_call(partial(behind_kernel, n, early, pieces, fold, fixed), nam...  139 us
    pallas_call x1, Pallas kernels, ahead(): pl.pallas_call(partial(ahead_kernel, n, layout, early, capacity), name='a...  131 us
    pallas_call x1, Pallas kernels, upper(): pl.pallas_call(partial(upper_kernel, page_rows), name='upper', out_shape=...  33.2 us
    pallas_call x1, Pallas kernels, update_all(): pl.pallas_call(partial(update_kernel, decay, layout), name='update', grid...  11.1 us

profile of v6, /device:TPU:0, one launch (start us, length us, event | category | flops | bytes accessed | tf_op | source)
XLA Modules:
  0.0 345.0 jit_solution(13990657608080796841)
XLA Ops:
  7.9 0.1 pad_add_fusion.own
  7.9 0.7 pad.4.info
  8.6 2.2 plan.1
  10.8 0.7 copy-done
  11.5 0.7 copy-done.1
  12.2 0.1 pad_maximum_fusion.11
  12.2 0.6 broadcast_in_dim.40.refs_4_
  12.8 131.0 %ahead.1 = (f32[32,8,128]{2,1,0:T(8,128)}, bf16[4,4,848,768]{3,2,1,0:T(8,128)(2,1)}, bf16[12,512,512]{2,1,0:T(8,128)(2,1)}, f32[512,384]{1,0:T(8,128)}, f32[512,...) custom-call(f32[32,8,128]{2,1,0:T(8,128)} %copy-done.1, ...), custom_call_target="tpu_custom_call" | custom-call | flops 12999999488 | bytes 104857600 | tf_op jit(solution)/shard_map/ahead/pallas_call | solution.py:917
  143.9 33.2 %upper.1 = (bf16[16,432,768]{2,1,0:T(8,128)(2,1)}, bf16[512,768]{1,0:T(8,128)(2,1)}, f32[512,768]{1,0:T(8,128)}, bf16[512,768]{1,0:T(8,128)(2,1)}, f32[4,768]{1,0:T(4,128)}, /*index=5*/f32[1,1]{1,0:T(1,128)}) custom-call(bf16[16,848,768]{2,1,0:T(8,128)(2,1)} %bitcast.319, bf16[512,768]{1,0:T(8,128)(2,1)} %get-tuple-element.362.attended, ...), custom_call_target="tpu_custom_call" | custom-call | flops 20000000000 | bytes 33554432 | tf_op jit(solution)/shard_map/upper/pallas_call | solution.py:310
  177.2 138.6 %behind.1 = (f32[360,768]{1,0:T(8,128)}, f32[960,768]{1,0:T(8,128)}, f32[8,128]{1,0:T(8,128)S(1)}, f32[8,128]{1,0:T(8,128)S(1)}) custom-call(bf16[4,4,848,768]{3,2,1,0:T(8,128)(2,1)} %get-tuple-element.361.refs_0_, bf16[4,4,432,768]{3,2,1,0:T(8,128)(2,1)} %bitcast.320, bf16[12,512,512]{2,1,0:T(8,128)(2,1)} %get-tuple-element.367.refs_2_, ...), custom_call_target="tpu_custom_call" | custom-call | flops 20000000000 | bytes 104857600 | tf_op jit(solution)/shard_map/behind/pallas_call | solution.py:1407
  315.8 1.6 slice_reduce_fusion.6
  318.0 1.0 fusion.68
  319.0 0.7 maximum_bitcast_fusion
  319.7 0.9 fusion.69
  320.6 0.1 maximum_bitcast_fusion.1
  320.8 14.3 %conditional.1 = (f32[24,2304]{1,0:T(8,128)S(1)}, f32[24,768]{1,0:T(8,128)S(1)}, f32[24,3072]{1,0:T(8,128)S(1)}, f32[96,768]{1,0:T(8,128)S(1)}, f32[24,2304]{1,0...) conditional(s32[]{:T(128)} %convert_element_type.206, ...), branch_computations={%region_1.2_spmd, %region_2.47_spmd} | conditional | flops 52047056896 | bytes 1111573120 | solution.py:1833
  320.8 0.6 fusion.58
  322.1 11.1 %update.1 = (f32[960,768]{1,0:T(8,128)}, f32[24,768]{1,0:T(8,128)S(1)}, f32[24,2304]{1,0:T(8,128)S(1)}, f32[48,768]{1,0:T(8,128)S(1)}, f32[24,768]{1,0:T(8,128)S...) custom-call(f32[1,1]{1,0:T(1,128)} %bitcast.1.factor, ...), custom_call_target="tpu_custom_call" | custom-call | bytes 29360128 | tf_op jit(solution)/shard_map/cond/branch_0_fun/update/pallas_call | solution.py:376
  333.2 0.6 multiply_add_fusion
  335.3 0.5 copy-done.125
  335.8 0.1 copy-done.126
  335.9 0.1 copy-done.127
  336.0 0.1 copy-done.128
  336.1 0.1 copy-done.129
  336.2 0.1 copy-done.130
  336.3 0.1 copy-done.131
  336.3 0.1 copy-done.132
  336.4 0.1 copy-done.133
  336.5 0.0 copy-done.134
  336.5 0.0 copy-done.135
  336.6 0.0 copy-done.136
  336.6 0.0 copy-done.138
  (43 shorter events, 0.2 us)
Async XLA Ops:
  10.8 0.7 copy-start
  11.5 0.7 copy-start.1
  12.2 131.7 %copy-start.86 = (f32[512,1]{1,0:T(8,128)}, f32[512,1]{1,0:T(8,128)S(1)}, u32[]{:S(2)}) copy-start(f32[512,1]{1,0:T(8,128)S(1)} %get-tuple-element.359.refs_6_.mask_col.refs_15_) | copy-start | bytes 6148
  12.8 131.0 %copy-start.111 = (s32[8,512]{1,0:T(8,128)S(1)}, s32[8,512]{1,0:T(8,128)}, u32[]{:S(2)}) copy-start(s32[8,512]{1,0:T(8,128)} %page.1) | copy-start | bytes 49156
  12.8 131.0 %copy-start.112 = (s32[8,512]{1,0:T(8,128)S(1)}, s32[8,512]{1,0:T(8,128)}, u32[]{:S(2)}) copy-start(s32[8,512]{1,0:T(8,128)} %row.1) | copy-start | bytes 49156
  177.1 143.6 %copy-start.105 = (s32[512]{0:T(512)S(1)}, s32[512]{0:T(512)}, u32[]{:S(2)}) copy-start(s32[512]{0:T(512)} %param.40) | copy-start | bytes 6148
  177.1 143.6 %copy-start.83 = (s32[512]{0:T(512)S(1)}, s32[512]{0:T(512)}, u32[]{:S(2)}) copy-start(s32[512]{0:T(512)} %param.37) | copy-start | bytes 6148
  177.1 143.6 %copy-start.98 = (f32[6,24]{1,0:T(8,128)S(1)}, f32[6,24]{1,0:T(8,128)}, u32[]{:S(2)}) copy-start(f32[6,24]{1,0:T(8,128)} %param.51) | copy-start | bytes 1732
  177.1 143.6 %copy-start.114 = (f32[6,24]{1,0:T(8,128)S(1)}, f32[6,24]{1,0:T(8,128)}, u32[]{:S(2)}) copy-start(f32[6,24]{1,0:T(8,128)} %param.59) | copy-start | bytes 1732
  177.2 143.6 %copy-start.117 = (f32[6,24]{1,0:T(8,128)S(1)}, f32[6,24]{1,0:T(8,128)}, u32[]{:S(2)}) copy-start(f32[6,24]{1,0:T(8,128)} %param.67) | copy-start | bytes 1732
  335.1 0.7 copy-start.125
  335.1 0.8 copy-start.126
  335.1 0.9 copy-start.127
  335.1 1.0 copy-start.128
  335.1 1.1 copy-start.129
  335.1 1.1 copy-start.130
  335.1 1.2 copy-start.131
  335.1 1.3 copy-start.132
  335.1 1.3 copy-start.133
  335.2 1.4 copy-start.134
  335.2 1.4 copy-start.135
  335.2 1.4 copy-start.136
  335.2 1.4 copy-start.137
  335.2 1.4 copy-start.138
  335.2 1.5 copy-start.139
  335.2 1.5 copy-start.140
  335.2 1.5 copy-start.141
  335.3 1.5 copy-start.142

commit v7 on v6

--- a/solution.py
+++ b/solution.py
@@ -211,13 +211,14 @@
     )
     middle = second.astype(low)
     loads[1].wait()
-    loads[2].wait()
     for k in range(blocks):
         pre = dot_nn(middle, up_map(k))
         normal = 0.5 + 0.5 * lax.erf(pre * (0.5**0.5))
         active = (pre * normal).astype(low)
         slopes[k] = normal + pre * (jnp.exp(-0.5 * pre * pre) * 0.3989422804014327)
         hidden[k] = active
+        if k == 0:
+            loads[2].wait()
         part = dot_nn(active, down_map(k))
         lowered = part if k == 0 else lowered + part
     states, white_last, scale_last = layer_norm(second + lowered, gains[4:5], gains[5:6])
@@ -367,7 +368,7 @@
 
 
 def update_all(factor, table, sums, masters, moments, averages, decay, layout):
-    steps = 6
+    steps = 4
     rows, model = table.shape
     banded = pl.BlockSpec((rows // steps, model), lambda i: (i, 0))
     whole = lambda array: pl.BlockSpec(array.shape, lambda i: (0, 0))
@@ -1388,7 +1389,8 @@
     total_line = told[0]
     for j in range(1, n):
         total_line = total_line + told[j]
-    totals[...] = total_line
+    over = jnp.max(jnp.max(asked[:, 7, :], 0, keepdims=True)[:, 2:3], keepdims=True)
+    totals[...] = jnp.where(lane == 2, over, total_line)
 
 
 def behind(in_hbm, in_vmem, rows_own, early, pieces, capacity, fold, fixed, n, ident):
@@ -1829,7 +1831,7 @@
             results += [*lay(done[at : at + 7]), tail]
         return tuple(results)
 
-    overflow = jnp.max(asked[:, 7, 2]) > 0.0
+    overflow = totals[0, 2] > 0.0
     return lax.cond(overflow, dense, finish)
 
 

time: 350 us -> 347 us (level)
  no operation moved by 1% of the time
where the time goes in v7:
time: 347 us; the launch traced here: 343 us
  Pallas kernels  315 us (91%)
  between operations  17 us (5%)
  local copies, waits for them, and re-layouts  7.24 us (2%)
    pallas_call x1, Pallas kernels, behind(): pl.pallas_call(partial(behind_kernel, n, early, pieces, fold, fixed), nam...  139 us
    pallas_call x1, Pallas kernels, ahead(): pl.pallas_call(partial(ahead_kernel, n, layout, early, capacity), name='a...  131 us
    pallas_call x1, Pallas kernels, upper(): pl.pallas_call(partial(upper_kernel, page_rows), name='upper', out_shape=...  32.3 us
    pallas_call x1, Pallas kernels, update_all(): pl.pallas_call(partial(update_kernel, decay, layout), name='update', grid...  10.3 us

profile of v7, /device:TPU:0, one launch (start us, length us, event | category | flops | bytes accessed | tf_op | source)
XLA Modules:
  0.0 342.6 jit_solution(9153273328250707608)
XLA Ops:
  7.9 0.1 pad_add_fusion.own
  7.9 0.7 pad.4.info
  8.6 2.2 plan.1
  10.8 0.7 copy-done
  11.5 0.7 copy-done.1
  12.2 0.1 pad_maximum_fusion.11
  12.2 0.6 broadcast_in_dim.40.refs_4_
  12.8 131.3 %ahead.1 = (f32[32,8,128]{2,1,0:T(8,128)}, bf16[4,4,848,768]{3,2,1,0:T(8,128)(2,1)}, bf16[12,512,512]{2,1,0:T(8,128)(2,1)}, f32[512,384]{1,0:T(8,128)}, f32[512,...) custom-call(f32[32,8,128]{2,1,0:T(8,128)} %copy-done.1, ...), custom_call_target="tpu_custom_call" | custom-call | flops 12999999488 | bytes 104857600 | tf_op jit(solution)/shard_map/ahead/pallas_call | solution.py:918
  144.2 32.3 %upper.1 = (bf16[16,432,768]{2,1,0:T(8,128)(2,1)}, bf16[512,768]{1,0:T(8,128)(2,1)}, f32[512,768]{1,0:T(8,128)}, bf16[512,768]{1,0:T(8,128)(2,1)}, f32[4,768]{1,0:T(4,128)}, /*index=5*/f32[1,1]{1,0:T(1,128)}) custom-call(bf16[16,848,768]{2,1,0:T(8,128)(2,1)} %bitcast.320, bf16[512,768]{1,0:T(8,128)(2,1)} %get-tuple-element.361.attended, ...), custom_call_target="tpu_custom_call" | custom-call | flops 20000000000 | bytes 33554432 | tf_op jit(solution)/shard_map/upper/pallas_call | solution.py:311
  176.6 138.8 %behind.1 = (f32[360,768]{1,0:T(8,128)}, f32[960,768]{1,0:T(8,128)}, f32[8,128]{1,0:T(8,128)S(1)}, f32[8,128]{1,0:T(8,128)S(1)}) custom-call(bf16[4,4,848,768]{3,2,1,0:T(8,128)(2,1)} %get-tuple-element.360.refs_0_, bf16[4,4,432,768]{3,2,1,0:T(8,128)(2,1)} %bitcast.321, bf16[12,512,512]{2,1,0:T(8,128)(2,1)} %get-tuple-element.367.refs_2_, ...), custom_call_target="tpu_custom_call" | custom-call | flops 20000000000 | bytes 104857600 | tf_op jit(solution)/shard_map/behind/pallas_call | solution.py:1409
  315.3 0.6 slice.203
  316.6 1.0 fusion.68
  317.5 0.7 maximum_bitcast_fusion
  318.3 0.9 fusion.69
  319.2 0.1 maximum_bitcast_fusion.1
  319.3 13.4 %conditional.1 = (f32[24,2304]{1,0:T(8,128)S(1)}, f32[24,768]{1,0:T(8,128)S(1)}, f32[24,3072]{1,0:T(8,128)S(1)}, f32[96,768]{1,0:T(8,128)S(1)}, f32[24,2304]{1,0...) conditional(s32[]{:T(128)} %bitcast.93, ...), branch_computations={%region_0.1_spmd, %region_1.46_spmd} | conditional | flops 52047056896 | bytes 1111573120 | solution.py:1835
  319.3 0.6 fusion.58
  320.6 10.3 %update.1 = (f32[960,768]{1,0:T(8,128)}, f32[24,768]{1,0:T(8,128)S(1)}, f32[24,2304]{1,0:T(8,128)S(1)}, f32[48,768]{1,0:T(8,128)S(1)}, f32[24,768]{1,0:T(8,128)S...) custom-call(f32[1,1]{1,0:T(1,128)} %bitcast.1.factor, ...), custom_call_target="tpu_custom_call" | custom-call | bytes 29360128 | tf_op jit(solution)/shard_map/cond/branch_0_fun/update/pallas_call | solution.py:377
  330.9 0.6 multiply_add_fusion
  332.9 0.5 copy-done.125
  333.4 0.1 copy-done.126
  333.5 0.1 copy-done.127
  333.6 0.1 copy-done.128
  333.7 0.1 copy-done.129
  333.8 0.1 copy-done.130
  333.9 0.1 copy-done.131
  334.0 0.1 copy-done.132
  334.0 0.1 copy-done.133
  334.1 0.0 copy-done.134
  334.1 0.0 copy-done.135
  334.2 0.0 copy-done.136
  334.3 0.0 copy-done.138
  (43 shorter events, 0.2 us)
Async XLA Ops:
  10.8 0.7 copy-start
  11.5 0.7 copy-start.1
  12.2 132.0 %copy-start.86 = (f32[512,1]{1,0:T(8,128)}, f32[512,1]{1,0:T(8,128)S(1)}, u32[]{:S(2)}) copy-start(f32[512,1]{1,0:T(8,128)S(1)} %get-tuple-element.359.refs_6_.mask_col.refs_15_) | copy-start | bytes 6148
  12.8 131.4 %copy-start.111 = (s32[8,512]{1,0:T(8,128)S(1)}, s32[8,512]{1,0:T(8,128)}, u32[]{:S(2)}) copy-start(s32[8,512]{1,0:T(8,128)} %page.1) | copy-start | bytes 49156
  12.8 131.4 %copy-start.112 = (s32[8,512]{1,0:T(8,128)S(1)}, s32[8,512]{1,0:T(8,128)}, u32[]{:S(2)}) copy-start(s32[8,512]{1,0:T(8,128)} %row.1) | copy-start | bytes 49156
  176.5 142.7 %copy-start.105 = (s32[512]{0:T(512)S(1)}, s32[512]{0:T(512)}, u32[]{:S(2)}) copy-start(s32[512]{0:T(512)} %param.40) | copy-start | bytes 6148
  176.5 142.7 %copy-start.83 = (s32[512]{0:T(512)S(1)}, s32[512]{0:T(512)}, u32[]{:S(2)}) copy-start(s32[512]{0:T(512)} %param.37) | copy-start | bytes 6148
  176.5 142.7 %copy-start.98 = (f32[6,24]{1,0:T(8,128)S(1)}, f32[6,24]{1,0:T(8,128)}, u32[]{:S(2)}) copy-start(f32[6,24]{1,0:T(8,128)} %param.51) | copy-start | bytes 1732
  176.5 142.7 %copy-start.114 = (f32[6,24]{1,0:T(8,128)S(1)}, f32[6,24]{1,0:T(8,128)}, u32[]{:S(2)}) copy-start(f32[6,24]{1,0:T(8,128)} %param.59) | copy-start | bytes 1732
  176.6 142.7 %copy-start.117 = (f32[6,24]{1,0:T(8,128)S(1)}, f32[6,24]{1,0:T(8,128)}, u32[]{:S(2)}) copy-start(f32[6,24]{1,0:T(8,128)} %param.67) | copy-start | bytes 1732
  332.7 0.7 copy-start.125
  332.7 0.8 copy-start.126
  332.7 0.9 copy-start.127
  332.7 1.0 copy-start.128
  332.7 1.1 copy-start.129
  332.7 1.1 copy-start.130
  332.8 1.2 copy-start.131
  332.8 1.3 copy-start.132
  332.8 1.3 copy-start.133
  332.8 1.4 copy-start.134
  332.8 1.4 copy-start.135
  332.8 1.4 copy-start.136
  332.8 1.4 copy-start.137
  332.8 1.4 copy-start.138
  332.9 1.5 copy-start.139
  332.9 1.5 copy-start.140
  332.9 1.5 copy-start.141
  332.9 1.5 copy-start.142
